TPU v7x, 512 devices: a whole 4x4x16 slice. The times are simulated.
512 devices in a mesh: wide: 128 (over z, x, core), narrow: 4 (over y).
Axes of the slice: x: 4, y: 4, z: 16, core: 2. Of those that a mesh axis runs over, the one named last changes fastest.
Arguments:
- piece_ids: int32 [131072], P('wide'), may hold values from 0 to 131071, as said below
- point_counts: int32 [131072, 128], P('wide'), may hold values from 0 to 15, as said below
- wavenumber: float32 [4], P('narrow'), may hold values from 0.05 to 0.6
- strength: float32 [4], P('narrow'), may hold values from 0.5 to 2
- displacement: float32 [2, 4], P(None, 'narrow'), may hold values from -0.5 to 0.5
- node_position: float32 [2, 15], replicated, may hold values from -0.5 to 0.5
- node_weights: float32 [15], replicated, may hold values from 0.25 to 1
Outputs:
- spectrum_real: float32 [4, 4096, 4096], P(None, ('wide', 'narrow'))
- spectrum_imag: float32 [4, 4096, 4096], P(None, ('wide', 'narrow'))
Inputs may be any that keep to these rules, and one draw needn't show every extreme that they name: `piece_ids`: each of the 131072 piece numbers appears exactly once. The 1024 entries of one index of wide hold, from each block of 1024 consecutive piece numbers, between 4 and 12 numbers, and exactly 12 from some block. `point_counts`: zero exactly at offsets whose row or column offset exceeds 1536 - 1 in size; 15 at offset (0, 0); 7 to 15 where both offsets are within 8 of zero; 1 to 3 elsewhere.
All inputs are finite; a program needn't handle non-finite values.
Results may differ from a plain program's by a relative error of at most 0.0003.
Values sent between devices are 32-bit elements; how exact they have to be, the bound alone decides.
No kernel may reach another device: no remote copies, remote signals or barrier semaphores. Data moves between devices by JAX's collectives and lax.ppermute only.
A program may use at most 64 MiB of HBM per device.

v0:
```python
import functools
import math

import jax
import jax.numpy as jnp
import numpy as np
from jax import lax
from jax.experimental import pallas as pl
from jax.experimental.pallas import tpu as pltpu
from jax.sharding import Mesh, PartitionSpec as P

LENGTH = 4096
NODES = 15
FAR = 3
HEIGHT_SQ = 0.0625
RANKS = 12
SHARED = 3
LIVE_BLOCKS = 24
HALF = 1536
ROWS = 6
PLANES = 4

PI_HI = 6.28125
PI_LO = 2.0 * math.pi - 6.28125
ROUNDER = 12582912.0


def fit_even(function, degree):
    top = math.pi**2
    grid = (np.cos(np.pi * (np.arange(400) + 0.5) / 400) + 1.0) * 0.5 * top
    series = np.polynomial.chebyshev.Chebyshev.fit(grid, function(np.sqrt(grid)), degree, [0, top])
    return [float(x) for x in series.convert(kind=np.polynomial.Polynomial).coef]


COS_COEF = fit_even(np.cos, 6)
SIN_COEF = fit_even(lambda x: np.sin(x) / x, 6)


def split_np(values):
    high = values.astype(np.float32).astype(jnp.bfloat16)
    low = (values - high.astype(np.float64)).astype(jnp.bfloat16)
    return high, low


def tables():
    v1 = np.arange(32)
    cb = np.arange(LIVE_BLOCKS)
    angle = 2.0 * np.pi * (((cb[None, :] - 12) * v1[:, None]) % 32) / 32
    cos, sin = np.cos(angle), np.sin(angle)
    first = np.concatenate(
        [np.concatenate([cos, sin], 1), np.concatenate([-sin, cos], 1)], 0
    )
    high, low = split_np(first)
    first = np.concatenate([high, high, low], 1)
    t = np.arange(128)
    angle = 2.0 * np.pi * (v1[:, None] * t[None, :]) / LENGTH
    turn_one = np.concatenate([np.cos(angle), -np.sin(angle)], 0).astype(np.float32)
    angle = 2.0 * np.pi * ((t[:, None] * t[None, :]) % 128) / 128
    second = split_np(np.concatenate([np.cos(angle), np.sin(angle)], 1) / 64.0)
    z = np.arange(16)
    third = np.zeros((2, 2, 128, 2, 2, 128))
    for b_low in range(2):
        for q2 in range(2):
            for k in range(3):
                c = z + 16 * (2 * k + b_low)
                angle = 2.0 * np.pi * (((c[:, None] - 48) * t[None, :]) % 128) / 128
                lanes = slice((q2 * 3 + k) * 16, (q2 * 3 + k) * 16 + 16)
                third[b_low, 0, lanes, q2, 0] = np.cos(angle)
                third[b_low, 0, lanes, q2, 1] = -np.sin(angle)
                third[b_low, 1, lanes, q2, 0] = np.sin(angle)
                third[b_low, 1, lanes, q2, 1] = np.cos(angle)
    third = split_np(third.reshape(512, 512) / 64.0)
    angle = 2.0 * np.pi * (v1[:, None] * t[None, :]) / LENGTH
    turn_two = np.concatenate([np.cos(angle), -np.sin(angle)], 0).astype(np.float32)
    return first, turn_one, second, third, turn_two


def iota(shape, axis):
    return lax.broadcasted_iota(jnp.int32, shape, axis)


def dot(left, right):
    return jnp.dot(left, right, preferred_element_type=jnp.float32)


def as_mask(chosen):
    return jnp.where(chosen, 1.0, 0.0).astype(jnp.bfloat16)


def split(values):
    high = values.astype(jnp.bfloat16)
    low = (values - high.astype(jnp.float32)).astype(jnp.bfloat16)
    return high, low


def sort_kernel(copy_ref, ids_ref, counts_ref, out_ref):
    base = copy_ref[0] * SHARED
    ids = ids_ref[...]
    block = ((ids >> 10) + 48) & 127
    target = ((block & 15) << 3) | (block >> 4)
    local = (ids & 1023) + 1
    owner = iota((128, 128), 0)
    lane = iota((128, 128), 1)
    prefix = jnp.concatenate([as_mask(owner < lane), jnp.ones((128, 128), jnp.bfloat16)], 1)
    running = jnp.zeros((128, 128), jnp.float32)
    picked = [jnp.zeros((128, 128), jnp.float32) for _ in range(SHARED)]
    names = [jnp.zeros((128, 128), jnp.int32) for _ in range(SHARED)]
    for k in range(8):
        here = owner == target[k : k + 1, :]
        sums = dot(as_mask(here), prefix)
        rank = running + sums[:, :128]
        running = running + sums[:, 128:]
        counts = counts_ref[k * 128 : (k + 1) * 128, :].astype(jnp.float32).astype(jnp.bfloat16)
        for s in range(SHARED):
            chosen = here & (rank == (base + s).astype(jnp.float32))
            picked[s] = picked[s] + dot(as_mask(chosen), counts)
            names[s] = names[s] + jnp.where(chosen, local[k : k + 1, :], 0)
    named = jnp.zeros((128, 128), jnp.int32)
    for s in range(SHARED):
        out_ref[pl.ds(s, 128, stride=4), :] = picked[s].astype(jnp.int32)
        total = jnp.sum(names[s].astype(jnp.float32), axis=1, keepdims=True).astype(jnp.int32)
        named = jnp.where(lane == s, total, named)
    out_ref[pl.ds(3, 128, stride=4), :] = named


def place_kernel(slot_ref, plane_ref, got_ref, out_ref):
    names = got_ref[pl.ds(3, 128, stride=4), :].astype(jnp.float32).T
    row = iota((768, 128), 0)
    grid = jnp.zeros((768, 128), jnp.float32)
    for s in range(SHARED):
        name = names[s : s + 1, :].astype(jnp.int32)
        local = name - 1
        column = ((local & 31) + 12) & 31
        valid = (name > 0) & (column < LIVE_BLOCKS)
        key = jnp.where(valid, (local >> 5) * LIVE_BLOCKS + column, -1)
        counts = got_ref[pl.ds(s, 128, stride=4), :].astype(jnp.float32).astype(jnp.bfloat16)
        grid = grid + dot(as_mask(row == key), counts)
    lane = iota((768, 128), 1)
    traits = jnp.zeros((768, 128), jnp.float32)
    for i in range(4):
        traits = jnp.where(lane == i, plane_ref[i], traits)
    out_ref[...] = jnp.where(slot_ref[0] >= ROWS, traits, grid)


def evaluate(square, wave, strength, weight):
    inverse = lax.rsqrt(square)
    radius = square * inverse
    phase = wave * radius
    turns = (phase * (0.5 / math.pi) + ROUNDER) - ROUNDER
    angle = (phase - turns * PI_HI) - turns * PI_LO
    arg = angle * angle
    cosine = jnp.full_like(arg, COS_COEF[-1])
    for value in COS_COEF[-2::-1]:
        cosine = cosine * arg + value
    sine = jnp.full_like(arg, SIN_COEF[-1])
    for value in SIN_COEF[-2::-1]:
        sine = sine * arg + value
    amplitude = weight * (1.0 + strength * inverse)
    return amplitude * cosine, amplitude * (angle * sine)


def fill_kernel(
    place_ref,
    position_ref,
    weight_ref,
    got_ref,
    first_ref,
    turn_ref,
    high_ref,
    low_ref,
    out_ref,
    fill_ref,
    turned_ref,
):
    device = place_ref[0]
    column = (
        iota((LIVE_BLOCKS, 128), 0) * 128 + iota((LIVE_BLOCKS, 128), 1) - HALF
    ).astype(jnp.float32)
    counts = []
    for b in range(ROWS):
        parts = [got_ref[(b * 4 + j) * 24 : (b * 4 + j) * 24 + 24, :] for j in range(4)]
        counts.append((parts[0] + parts[1]) + (parts[2] + parts[3]))
    lower = device < 256
    near_counts = jnp.where(lower, counts[3][8:16], counts[2][8:16])
    near_row = jnp.where(lower, device, device - 512).astype(jnp.float32)
    weights = [
        [jnp.where(counts[b] > float(q), weight_ref[q], 0.0) for q in range(FAR)]
        for b in range(ROWS)
    ]
    for p in range(PLANES):
        traits = got_ref[(24 + p) * 24 : (24 + p) * 24 + 1, :]
        wave, strength = traits[:, 0:1], traits[:, 1:2]
        shift_row, shift_col = traits[:, 2:3], traits[:, 3:4]
        col_base = column + shift_col
        col_sq = []
        for q in range(FAR):
            col_pos = col_base + position_ref[1, q]
            col_sq.append(col_pos * col_pos)
        extra_real = jnp.zeros((8, 128), jnp.float32)
        extra_imag = jnp.zeros((8, 128), jnp.float32)
        for q in range(FAR, NODES):
            row_pos = (near_row + shift_row) + position_ref[0, q]
            col_pos = col_base[8:16] + position_ref[1, q]
            square = row_pos * row_pos + col_pos * col_pos + HEIGHT_SQ
            weight = jnp.where(near_counts > float(q), weight_ref[q], 0.0)
            real, imag = evaluate(square, wave, strength, weight)
            extra_real = extra_real + real
            extra_imag = extra_imag + imag
        for b in range(ROWS):
            row_offset = (device + (512 * b - HALF)).astype(jnp.float32)
            total_real = jnp.zeros((LIVE_BLOCKS, 128), jnp.float32)
            total_imag = jnp.zeros((LIVE_BLOCKS, 128), jnp.float32)
            for q in range(FAR):
                row_pos = (row_offset + shift_row) + position_ref[0, q]
                square = row_pos * row_pos + col_sq[q] + HEIGHT_SQ
                real, imag = evaluate(square, wave, strength, weights[b][q])
                total_real = total_real + real
                total_imag = total_imag + imag
            lanes = slice((p * ROWS + b) * 128, (p * ROWS + b) * 128 + 128)
            fill_ref[0:24, lanes] = total_real
            fill_ref[24:48, lanes] = -total_imag
            if b in (2, 3):
                use = lower if b == 3 else jnp.logical_not(lower)
                fill_ref[8:16, lanes] = total_real[8:16] + jnp.where(use, extra_real, 0.0)
                fill_ref[32:40, lanes] = -(total_imag[8:16] + jnp.where(use, extra_imag, 0.0))
    turn_real = turn_ref[0:32, :]
    turn_imag = turn_ref[32:64, :]
    for p in range(PLANES):
        lanes = slice(p * ROWS * 128, (p + 1) * ROWS * 128)
        high, low = split(fill_ref[:, lanes])
        stage = dot(first_ref[...], jnp.concatenate([high, low, high], 0))
        for b in range(ROWS):
            real = stage[0:32, b * 128 : (b + 1) * 128]
            imag = stage[32:64, b * 128 : (b + 1) * 128]
            next_real = real * turn_real - imag * turn_imag
            next_imag = real * turn_imag + imag * turn_real
            for j in range(4):
                rows = slice(j * 8, j * 8 + 8)
                at = (j * 12 + b * 2) * 32 + p * 8
                turned_ref[at : at + 8, 0:128] = next_real[rows]
                turned_ref[at : at + 8, 128:256] = next_imag[rows]
                turned_ref[at + 32 : at + 40, 0:128] = next_imag[rows]
                turned_ref[at + 32 : at + 40, 128:256] = -next_real[rows]
    contract = (((1,), (1,)), ((), ()))
    for j in range(4):
        high, low = split(turned_ref[j * 384 : (j + 1) * 384, :])
        product = lax.dot_general(
            high_ref[...], high, contract, preferred_element_type=jnp.float32
        )
        product = product + lax.dot_general(
            high_ref[...], low, contract, preferred_element_type=jnp.float32
        )
        product = product + lax.dot_general(
            low_ref[...], high, contract, preferred_element_type=jnp.float32
        )
        for k in range(3):
            out_ref[pl.ds(j * 3 + k, 128, stride=12), :] = product[:, k * 128 : (k + 1) * 128]


def fft_list(values):
    size = len(values)
    if size == 1:
        return values
    even = fft_list(values[0::2])
    odd = fft_list(values[1::2])
    top, bottom = [], []
    for k in range(size // 2):
        real, imag = odd[k]
        if k == 0:
            pass
        elif 4 * k == size:
            real, imag = imag, -real
        elif 8 * k == size:
            half = math.sqrt(0.5)
            real, imag = (real + imag) * half, (imag - real) * half
        elif 8 * k == 3 * size:
            half = math.sqrt(0.5)
            real, imag = (imag - real) * half, -(real + imag) * half
        else:
            cos = math.cos(2.0 * math.pi * k / size)
            sin = math.sin(2.0 * math.pi * k / size)
            real, imag = real * cos + imag * sin, imag * cos - real * sin
        top.append((even[k][0] + real, even[k][1] + imag))
        bottom.append((even[k][0] - real, even[k][1] - imag))
    return top + bottom


def column_kernel(got_ref, high_ref, low_ref, turn_ref, real_ref, imag_ref, gathered_ref, stage_ref):
    blank = jnp.zeros((32, 128), jnp.float32)
    for pair in range(16):
        parts = []
        for q2 in range(2):
            for k in range(3):
                parts.append(got_ref[pl.ds((pair * 2 + q2) * 3 + k, 16, stride=96), :])
        flipped = jnp.concatenate(parts + [blank], 0).T
        for block in range(4):
            gathered_ref[pair * 32 : pair * 32 + 32, block * 128 : (block + 1) * 128] = flipped[
                block * 32 : block * 32 + 32
            ]
    for part in range(4):
        rows = slice(part * 128, (part + 1) * 128)
        high, low = split(gathered_ref[rows, :])
        stage_ref[rows, :] = (
            dot(high, high_ref[...]) + dot(low, high_ref[...]) + dot(high, low_ref[...])
        )
    for p in range(PLANES):
        values = []
        for q in range(32):
            at = (q // 2) * 32 + p * 8
            lane = (q % 2) * 256
            real = stage_ref[at : at + 8, lane : lane + 128]
            imag = stage_ref[at : at + 8, lane + 128 : lane + 256]
            if q:
                turn_real = turn_ref[q : q + 1, :]
                turn_imag = turn_ref[32 + q : 33 + q, :]
                real, imag = (
                    real * turn_real - imag * turn_imag,
                    real * turn_imag + imag * turn_real,
                )
            values.append((real, imag))
        for u, (real, imag) in enumerate(fft_list(values)):
            real_ref[p, :, u * 128 : (u + 1) * 128] = real
            imag_ref[p, :, u * 128 : (u + 1) * 128] = imag


VMEM = pl.BlockSpec(memory_space=pltpu.VMEM)
SMEM = pl.BlockSpec(memory_space=pltpu.SMEM)
PARAMS = pltpu.CompilerParams(vmem_limit_bytes=40 * 1024 * 1024)


def exchange(values, axes):
    return lax.all_to_all(values, axes, split_axis=0, concat_axis=0, tiled=True)


def shards(
    piece_ids, point_counts, wavenumber, strength, displacement, node_position, node_weights
):
    first, turn_one, second, third, turn_two = tables()
    copy = lax.axis_index("y").astype(jnp.int32).reshape(1)
    slot = (lax.axis_index("x") * 2 + lax.axis_index("core")).astype(jnp.int32).reshape(1)
    device = lax.axis_index(("z", "x", "core", "y")).astype(jnp.int32).reshape(1)
    traits = jnp.concatenate([wavenumber, strength, displacement[0], displacement[1]])
    sent = pl.pallas_call(
        sort_kernel,
        out_shape=jax.ShapeDtypeStruct((512, 128), jnp.int32),
        in_specs=[SMEM, VMEM, VMEM],
        out_specs=VMEM,
        compiler_params=PARAMS,
    )(copy, piece_ids.reshape(8, 128), point_counts)
    got = exchange(sent.reshape(128, 4, 128), ("z", "x", "core")).reshape(512, 128)
    grid = pl.pallas_call(
        place_kernel,
        out_shape=jax.ShapeDtypeStruct((768, 128), jnp.float32),
        in_specs=[SMEM, SMEM, VMEM],
        out_specs=VMEM,
        compiler_params=PARAMS,
    )(slot, traits, got)
    grid = exchange(grid, ("x", "core", "y"))
    sent = pl.pallas_call(
        fill_kernel,
        out_shape=jax.ShapeDtypeStruct((1536, 128), jnp.float32),
        in_specs=[SMEM, SMEM, SMEM] + [VMEM] * 5,
        out_specs=VMEM,
        scratch_shapes=[
            pltpu.VMEM((48, PLANES * ROWS * 128), jnp.float32),
            pltpu.VMEM((1536, 256), jnp.float32),
        ],
        compiler_params=PARAMS,
    )(device, node_position, node_weights, grid, first, turn_one, second[0], second[1])
    got = exchange(sent.reshape(1536, 1, 128), ("z", "x", "core", "y")).reshape(1536, 128)
    shape = jax.ShapeDtypeStruct((PLANES, 8, LENGTH), jnp.float32)
    return pl.pallas_call(
        column_kernel,
        out_shape=(shape, shape),
        in_specs=[VMEM] * 4,
        out_specs=(VMEM, VMEM),
        scratch_shapes=[
            pltpu.VMEM((512, 512), jnp.float32),
            pltpu.VMEM((512, 512), jnp.float32),
        ],
        compiler_params=PARAMS,
    )(got, third[0], third[1], turn_two)


def solution(mesh):
    fine = Mesh(mesh.devices.reshape(16, 4, 2, 4), ("z", "x", "core", "y"))
    wide = ("z", "x", "core")
    every = ("z", "x", "core", "y")
    placed = (P(wide), P(wide, None), P("y"), P("y"), P(None, "y"), P(), P())
    return jax.shard_map(
        shards,
        mesh=fine,
        in_specs=placed,
        out_specs=(P(None, every, None), P(None, every, None)),
        check_vma=False,
    )
```

profile of v0, /device:TPU:1, one launch (start us, length us, event | category | flops | bytes accessed | tf_op | source)
XLA Modules:
  0.0 129.5 jit_solution(2411134430547522363)
XLA Ops:
  0.6 0.0 copy-start.7
  0.6 0.7 copy-done.7
  1.3 1.0 copy-done.2
  2.4 2.0 %shard_map.149 = s32[512,128]{1,0:T(8,128)} custom-call(s32[1]{0:T(128)} %bitcast.4.copy_ref, s32[8,128]{1,0:T(8,128)S(1)} %bitcast.18, s32[1024,128]{1,0:T(8,128)S(1)} %copy-done.2), custom_call_target="tpu_custom_call" | custom-call | tf_op jit(solution)/shard_map/pallas_call | solution.py:343
  4.4 20.4 %all-to-all-start = ((s32[128,4,128]{2,1,0:T(4,128)}), s32[128,4,128]{2,1,0:T(4,128)S(1)}, u32[]{:S(2)}, u32[]{:S(2)}) async-start(s32[128,4,128]{2,1,0:T(4,128)} %bitcast.6), calls=%async_computation | async-start | bytes 524288 | tf_op jit(solution)/shard_map/all_to_all | solution.py:332
  26.1 0.0 copy-start.10
  26.1 0.6 copy-done.10
  26.8 0.6 fusion
  27.3 1.3 pad_maximum_fusion.plane_ref
  28.6 16.7 %all-to-all-done = s32[128,4,128]{2,1,0:T(4,128)S(1)} async-done(((s32[128,4,128]{2,1,0:T(4,128)}), s32[128,4,128]{2,1,0:T(4,128)S(1)}, u32[]{:S(2)}, u32[]{:S(2)}) %all-to-all-start) | async-done | bytes 262176 | tf_op jit(solution)/shard_map/all_to_all | solution.py:332
  45.3 1.7 %shard_map.150 = f32[768,128]{1,0:T(8,128)} custom-call(s32[1]{0:T(128)} %bitcast.1.slot_ref, f32[4]{0:T(128)S(1)} %pad_maximum_fusion.plane_ref, s32[512,128]{1,0:T(8,128)S(1)} %bitcast.17), custom_call_target="tpu_custom_call" | custom-call | tf_op jit(solution)/shard_map/pallas_call | solution.py:351
  47.0 8.9 %all-to-all-start.1 = ((f32[32,24,128]{2,1,0:T(8,128)}), f32[32,24,128]{2,1,0:T(8,128)S(1)}, u32[]{:S(2)}, u32[]{:S(2)}) async-start(f32[32,24,128]{2,1,0:T(8,128)} %bitcast.8), calls=%async_computation.1 | async-start | bytes 786432 | tf_op jit(solution)/shard_map/all_to_all | solution.py:332
  55.9 10.0 %all-to-all-done.1 = f32[32,24,128]{2,1,0:T(8,128)S(1)} async-done(((f32[32,24,128]{2,1,0:T(8,128)}), f32[32,24,128]{2,1,0:T(8,128)S(1)}, u32[]{:S(2)}, u32[]{:S(2)}) %all-to-all-start.1) | async-done | bytes 393248 | tf_op jit(solution)/shard_map/all_to_all | solution.py:332
  65.9 0.0 copy-done.3
  65.9 0.0 copy-done.4
  65.9 0.0 copy-done.5
  65.9 0.6 copy-done.8
  66.6 0.0 copy-done.9
  66.6 3.4 %shard_map.151 = f32[1536,128]{1,0:T(8,128)S(1)} custom-call(s32[1]{0:T(128)} %bitcast.place_ref, f32[2,15]{1,0:T(2,128)S(1)} %copy-done.8, f32[15]{0:T(128)S(1)} %copy-done.9, f32[768,128]{1,0:T(8,128)S(1)} %bitcast.16, bf16[64,144]{1,0:T(8,128)(2,1)S(1)} %copy-done.6, f32[64,128]{1,0:T(8,128)S(1)} %copy-done.3, bf16[128,256]{1,0:T(8,128)(2,1)S(1)} %copy-done.5, ...), custom_call_target="tpu_custom_call" | custom-call | tf_op jit(solution)/shard_map/pallas_call | solution.py:359
  70.0 0.0 copy-start
  70.0 0.0 copy-start.1
  70.0 57.0 %all_to_all.21 = f32[1536,1,128]{2,1,0:T(1,128)S(1)} all-to-all(f32[1536,1,128]{2,1,0:T(1,128)S(1)} %bitcast.15), channel_id=1, replica_groups=mesh['z'=16,'x'=4,'core'=2,'y'=4] {'z','x','core','y'}, dimensions={0} | all-to-all | bytes 1572864 | tf_op jit(solution)/shard_map/all_to_all | solution.py:332
  127.0 0.0 copy-done
  127.0 2.5 %shard_map.152 = (f32[4,8,4096]{2,1,0:T(8,128)}, f32[4,8,4096]{2,1,0:T(8,128)}) custom-call(f32[1536,128]{1,0:T(8,128)S(1)} %bitcast.14, bf16[512,512]{1,0:T(8,128)(2,1)S(1)} %copy-done.1, bf16[512,512]{1,0:T(8,128)(2,1)S(1)} %copy-done, f32[64,128]{1,0:T(8,128)S(1)} %copy-done.3), custom_call_target="tpu_custom_call" | custom-call | tf_op jit(solution)/shard_map/pallas_call | solution.py:372
  (9 shorter events, 0.0 us)
Async XLA Ops:
  0.6 0.7 copy-start.7
  1.3 1.0 copy-start.2
  4.4 40.9 %all-to-all-start = ((s32[128,4,128]{2,1,0:T(4,128)}), s32[128,4,128]{2,1,0:T(4,128)S(1)}, u32[]{:S(2)}, u32[]{:S(2)}) async-start(s32[128,4,128]{2,1,0:T(4,128)} %bitcast.6), calls=%async_computation | async-start | bytes 524288 | tf_op jit(solution)/shard_map/all_to_all | solution.py:332
  26.1 0.7 copy-start.10
  47.0 18.9 %copy-start.3 = (f32[64,128]{1,0:T(8,128)S(1)}, f32[64,128]{1,0:T(8,128)}, u32[]{:S(2)}) copy-start(f32[64,128]{1,0:T(8,128)} %constant.39.clone.turn_ref) | copy-start | bytes 98308
  47.0 18.9 %copy-start.4 = (bf16[128,256]{1,0:T(8,128)(2,1)S(1)}, bf16[128,256]{1,0:T(8,128)(2,1)}, u32[]{:S(2)}) copy-start(bf16[128,256]{1,0:T(8,128)(2,1)} %constant.41.clone.low_ref) | copy-start | bytes 196612
  47.0 19.0 %copy-start.5 = (bf16[128,256]{1,0:T(8,128)(2,1)S(1)}, bf16[128,256]{1,0:T(8,128)(2,1)}, u32[]{:S(2)}) copy-start(bf16[128,256]{1,0:T(8,128)(2,1)} %constant.40.clone.high_ref) | copy-start | bytes 196612
  47.0 19.0 %copy-start.6 = (bf16[64,144]{1,0:T(8,128)(2,1)S(1)}, bf16[64,144]{1,0:T(8,128)(2,1)}, u32[]{:S(2)}) copy-start(bf16[64,144]{1,0:T(8,128)(2,1)} %constant.38.clone.first_ref) | copy-start | bytes 55300
  47.0 18.9 %all-to-all-start.1 = ((f32[32,24,128]{2,1,0:T(8,128)}), f32[32,24,128]{2,1,0:T(8,128)S(1)}, u32[]{:S(2)}, u32[]{:S(2)}) async-start(f32[32,24,128]{2,1,0:T(8,128)} %bitcast.8), calls=%async_computation.1 | async-start | bytes 786432 | tf_op jit(solution)/shard_map/all_to_all | solution.py:332
  65.9 0.7 copy-start.8
  65.9 0.7 copy-start.9
  70.0 57.0 %copy-start = (bf16[512,512]{1,0:T(8,128)(2,1)S(1)}, bf16[512,512]{1,0:T(8,128)(2,1)}, u32[]{:S(2)}) copy-start(bf16[512,512]{1,0:T(8,128)(2,1)} %constant.43.clone.low_ref) | copy-start | bytes 1572868
  70.0 57.0 %copy-start.1 = (bf16[512,512]{1,0:T(8,128)(2,1)S(1)}, bf16[512,512]{1,0:T(8,128)(2,1)}, u32[]{:S(2)}) copy-start(bf16[512,512]{1,0:T(8,128)(2,1)} %constant.42.clone.high_ref) | copy-start | bytes 1572868
where the time goes:
time: 130 us; the launch traced here: 129 us
  blocking collectives  57 us (44%)
  starting transfers between devices  29.3 us (23%)
  waiting for transfers between devices  26.7 us (21%)
  Pallas kernels  9.61 us (7%)
  local copies, waits for them, and re-layouts  3.6 us (3%)
  between operations  2.04 us (2%)
    all_to_all x1, blocking collectives, exchange(): return lax.all_to_all(values, axes, split_axis=0, concat_axis=0, tiled=True)  57 us
    all_to_all x2, starting transfers between devices, exchange(): return lax.all_to_all(values, axes, split_axis=0, concat_axis=0, tiled=True)  29.3 us
    all_to_all x2, waiting for transfers between devices, exchange(): return lax.all_to_all(values, axes, split_axis=0, concat_axis=0, tiled=True)  26.7 us
    pallas_call x1, Pallas kernels, shards(): pl.pallas_call(fill_kernel, out_shape=jax.ShapeDtypeStruct((1536, 128), j...  3.36 us
    unnamed x22, local copies, waits for them, and re-layouts  3.05 us
  transfers between devices with their start and end apart: 2, of which 2 were waited for; matrix products, arithmetic and copies ran while one was open for 1% of the time, Pallas kernels for 0%

commit v1 on v0

v1 whole, which is shorter than its diff:
```python
import functools
import math

import jax
import jax.numpy as jnp
import numpy as np
from jax import lax
from jax.experimental import pallas as pl
from jax.experimental.pallas import tpu as pltpu
from jax.sharding import Mesh, PartitionSpec as P

LENGTH = 4096
NODES = 15
FAR = 3
HEIGHT_SQ = 0.0625
SHARED = 3
LIVE_BLOCKS = 24
HALF = 1536
ROWS = 6
PLANES = 4

ROUNDER = 12582912.0


def fit_even(function, degree):
    top = math.pi**2
    grid = (np.cos(np.pi * (np.arange(400) + 0.5) / 400) + 1.0) * 0.5 * top
    series = np.polynomial.chebyshev.Chebyshev.fit(grid, function(np.sqrt(grid)), degree, [0, top])
    return [float(x) for x in series.convert(kind=np.polynomial.Polynomial).coef]


COS_COEF = fit_even(np.cos, 6)
SIN_COEF = fit_even(lambda x: np.sin(x) / x, 5)
COS_TURN = [c * (2.0 * math.pi) ** (2 * k) for k, c in enumerate(COS_COEF)]
SIN_TURN = [c * (2.0 * math.pi) ** (2 * k + 1) for k, c in enumerate(SIN_COEF)]


def split_np(values):
    high = values.astype(np.float32).astype(jnp.bfloat16)
    low = (values - high.astype(np.float64)).astype(jnp.bfloat16)
    return high, low


def tables():
    v1 = np.arange(32)
    cb = np.arange(LIVE_BLOCKS)
    angle = 2.0 * np.pi * (((cb[None, :] - 12) * v1[:, None]) % 32) / 32
    cos, sin = np.cos(angle), np.sin(angle)
    first = np.concatenate(
        [np.concatenate([cos, sin], 1), np.concatenate([-sin, cos], 1)], 0
    )
    high, low = split_np(first)
    first = np.concatenate([high, high, low], 1)
    t = np.arange(128)
    angle = 2.0 * np.pi * (v1[:, None] * t[None, :]) / LENGTH
    turn_one = np.concatenate([np.cos(angle), -np.sin(angle)], 0).astype(np.float32)
    angle = 2.0 * np.pi * ((t[:, None] * t[None, :]) % 128) / 128
    second = split_np(np.concatenate([np.cos(angle), np.sin(angle)], 1) / 64.0)
    c = np.arange(96)
    angle = 2.0 * np.pi * (((c[:, None] - 48) * t[None, :]) % 128) / 128
    third = np.zeros((2, 128, 2, 128))
    third[0, :96, 0] = np.cos(angle)
    third[0, :96, 1] = -np.sin(angle)
    third[1, :96, 0] = np.sin(angle)
    third[1, :96, 1] = np.cos(angle)
    third = split_np(third.reshape(256, 256) / 64.0)
    angle = 2.0 * np.pi * (v1[:, None] * t[None, :]) / LENGTH
    turn_two = np.concatenate([np.cos(angle), -np.sin(angle)], 0).astype(np.float32)
    return first, turn_one, second, third, turn_two


def iota(shape, axis):
    return lax.broadcasted_iota(jnp.int32, shape, axis)


def dot(left, right):
    return jnp.dot(left, right, preferred_element_type=jnp.float32)


def as_mask(chosen):
    return jnp.where(chosen, 1.0, 0.0).astype(jnp.bfloat16)


def split(values):
    high = values.astype(jnp.bfloat16)
    low = (values - high.astype(jnp.float32)).astype(jnp.bfloat16)
    return high, low


def sort_kernel(copy_ref, ids_hbm, counts_hbm, out_ref, ids_ref, counts_ref, sem):
    ids_copy = pltpu.make_async_copy(ids_hbm, ids_ref, sem.at[0])
    ids_copy.start()
    counts_copy = pltpu.make_async_copy(counts_hbm, counts_ref, sem.at[1])
    counts_copy.start()
    base = copy_ref[0] * SHARED
    owner = iota((128, 128), 0)
    lane = iota((128, 128), 1)
    prefix = jnp.concatenate([as_mask(owner < lane), jnp.ones((128, 128), jnp.bfloat16)], 1)
    ids_copy.wait()
    ids = ids_ref[...]
    block = ((ids >> 10) + 48) & 127
    part = block >> 4
    seat = jnp.where(part < 3, part, jnp.where(part < ROWS, part + 1, part * 4 - 21))
    target = ((block & 15) << 3) | seat
    local = ids & 1023
    high = ((local >> 5) + 1).astype(jnp.float32)
    low = (local & 31).astype(jnp.float32)
    pad = jnp.zeros((120, 128), jnp.float32)
    high = jnp.concatenate([high, pad], 0).T
    low = jnp.concatenate([low, pad], 0).T
    here = [owner == target[k : k + 1, :] for k in range(8)]
    sums = [dot(as_mask(here[k]), prefix) for k in range(8)]
    running = jnp.zeros((128, 128), jnp.float32)
    chosen = []
    for k in range(8):
        rank = running + sums[k][:, :128]
        running = running + sums[k][:, 128:]
        chosen.append(
            jnp.concatenate(
                [as_mask(here[k] & (rank == (base + s).astype(jnp.float32))) for s in range(SHARED)],
                0,
            )
        )
    counts_copy.wait()
    picked = jnp.zeros((SHARED * 128, 256), jnp.float32)
    for k in range(0, 8, 2):
        rows = []
        for m in (k, k + 1):
            counts = counts_ref[m * 128 : (m + 1) * 128, :].astype(jnp.float32)
            name = jnp.where(
                lane == 0, high[:, m : m + 1], jnp.where(lane == 1, low[:, m : m + 1], 0.0)
            )
            rows.append(jnp.concatenate([counts, name], 1).astype(jnp.bfloat16))
        picked = picked + dot(
            jnp.concatenate([chosen[k], chosen[k + 1]], 1), jnp.concatenate(rows, 0)
        )
    named = jnp.zeros((128, 128), jnp.float32)
    for s in range(SHARED):
        rows = slice(s * 128, (s + 1) * 128)
        out_ref[pl.ds(s, 128, stride=4), :] = picked[rows, :128].astype(jnp.int32)
        name = picked[rows, 128:129] * 32.0 + picked[rows, 129:130]
        named = jnp.where(lane == s, name, named)
    out_ref[pl.ds(3, 128, stride=4), :] = named.astype(jnp.int32)


def place_kernel(seat_ref, traits_ref, got_ref, out_ref):
    names = got_ref[pl.ds(3, 128, stride=4), :].astype(jnp.float32).T
    row = iota((768, 128), 0)
    masks, counts = [], []
    for s in range(SHARED):
        name = names[s : s + 1, :].astype(jnp.int32)
        column = ((name & 31) + 12) & 31
        valid = (name > 0) & (column < LIVE_BLOCKS)
        key = jnp.where(valid, ((name >> 5) - 1) * LIVE_BLOCKS + column, -1)
        masks.append(as_mask(row == key))
        counts.append(got_ref[pl.ds(s, 128, stride=4), :].astype(jnp.float32).astype(jnp.bfloat16))
    vacant = seat_ref[0] == 3

    @pl.when(vacant)
    def _():
        out_ref[...] = jnp.broadcast_to(traits_ref[0:1, :], (768, 128))

    @pl.when(jnp.logical_not(vacant))
    def _():
        out_ref[...] = dot(jnp.concatenate(masks, 1), jnp.concatenate(counts, 0))


def evaluate(square, wave, strength, weight):
    inverse = lax.rsqrt(square)
    turns = wave * (square * inverse)
    turns = turns - ((turns + ROUNDER) - ROUNDER)
    arg = turns * turns
    cosine = COS_TURN[-1] * arg + COS_TURN[-2]
    for value in COS_TURN[-3::-1]:
        cosine = cosine * arg + value
    sine = SIN_TURN[-1] * arg + SIN_TURN[-2]
    for value in SIN_TURN[-3::-1]:
        sine = sine * arg + value
    amplitude = weight * (1.0 + strength * inverse)
    return amplitude * cosine, amplitude * (turns * sine)


def fill_kernel(
    place_ref,
    got_ref,
    first_ref,
    turn_ref,
    high_ref,
    low_ref,
    out_ref,
    near_ref,
    fill_ref,
    turned_ref,
):
    device = place_ref[0]
    z = device >> 5
    side = (device >> 4) & 1
    base = z * 32 + side * HALF + (device & 15) * 2 - HALF
    column = (
        iota((LIVE_BLOCKS, 128), 0) * 128 + iota((LIVE_BLOCKS, 128), 1) - HALF
    ).astype(jnp.float32)
    traits = [got_ref[(12 + p) * 48 : (12 + p) * 48 + 1, :] for p in range(PLANES)]
    counts = []
    for b in range(ROWS):
        parts = []
        for j in range(4):
            at = ((b // 2) * 4 + j) * 48 + (b % 2) * 24
            parts.append(got_ref[at : at + 24, :])
        counts.append((parts[0] + parts[1]) + (parts[2] + parts[3]))
    right = side == 1
    near_ref[...] = jnp.zeros((8, 128), jnp.float32)
    for m in range(2):
        near_ref[m * 2 : m * 2 + 2, :] = jnp.where(right, counts[m][11:13], counts[4 + m][11:13])
    near_counts = near_ref[...]
    sub = iota((8, 128), 0)
    near_row = (base + jnp.where(right, 0, 1024) + (sub >> 1)).astype(jnp.float32)
    near_col = ((sub & 1) * 128 + iota((8, 128), 1) - 128).astype(jnp.float32)
    node_row = [traits[0][:, 16 + q : 17 + q] for q in range(NODES)]
    node_col = [traits[0][:, 32 + q : 33 + q] for q in range(NODES)]
    node_weight = [traits[0][:, 48 + q : 49 + q] for q in range(NODES)]
    weights = [
        [jnp.where(counts[b] > float(q), node_weight[q], 0.0) for q in range(FAR)]
        for b in range(ROWS)
    ]
    near_weights = [jnp.where(near_counts > float(q), node_weight[q], 0.0) for q in range(NODES)]
    turn_real = turn_ref[0:32, :]
    turn_imag = turn_ref[32:64, :]
    for p in range(PLANES):
        wave, strength = traits[p][:, 0:1] * (0.5 / math.pi), traits[p][:, 1:2]
        shift_row, shift_col = traits[p][:, 2:3], traits[p][:, 3:4]
        col_base = column + shift_col
        col_sq = []
        for q in range(FAR):
            col_pos = col_base + node_col[q]
            col_sq.append(col_pos * col_pos)
        extra_real = jnp.zeros((8, 128), jnp.float32)
        extra_imag = jnp.zeros((8, 128), jnp.float32)
        for q in range(FAR, NODES):
            row_pos = (near_row + shift_row) + node_row[q]
            col_pos = (near_col + shift_col) + node_col[q]
            square = row_pos * row_pos + col_pos * col_pos + HEIGHT_SQ
            real, imag = evaluate(square, wave, strength, near_weights[q])
            extra_real = extra_real + real
            extra_imag = extra_imag + imag
        for b in range(ROWS):
            row_offset = (base + (512 * (b // 2) + b % 2)).astype(jnp.float32)
            total_real = jnp.zeros((LIVE_BLOCKS, 128), jnp.float32)
            total_imag = jnp.zeros((LIVE_BLOCKS, 128), jnp.float32)
            for q in range(FAR):
                row_pos = (row_offset + shift_row) + node_row[q]
                square = col_sq[q] + (row_pos * row_pos + HEIGHT_SQ)
                real, imag = evaluate(square, wave, strength, weights[b][q])
                total_real = total_real + real
                total_imag = total_imag + imag
            lanes = slice((p * ROWS + b) * 128, (p * ROWS + b) * 128 + 128)
            fill_ref[0:24, lanes] = total_real
            fill_ref[24:48, lanes] = -total_imag
            if b // 2 != 1:
                use = right if b // 2 == 0 else jnp.logical_not(right)
                m = (b % 2) * 2
                fill_ref[11:13, lanes] = fill_ref[11:13, lanes] + jnp.where(
                    use, extra_real[m : m + 2], 0.0
                )
                fill_ref[35:37, lanes] = fill_ref[35:37, lanes] - jnp.where(
                    use, extra_imag[m : m + 2], 0.0
                )
        lanes = slice(p * ROWS * 128, (p + 1) * ROWS * 128)
        high, low = split(fill_ref[:, lanes])
        stage = dot(first_ref[...], jnp.concatenate([high, low, high], 0))
        for b in range(ROWS):
            real = stage[0:32, b * 128 : (b + 1) * 128]
            imag = stage[32:64, b * 128 : (b + 1) * 128]
            next_real = real * turn_real - imag * turn_imag
            next_imag = real * turn_imag + imag * turn_real
            for j in range(4):
                rows = slice(j * 8, j * 8 + 8)
                at = ((j * 3 + b // 2) * 4 + (b % 2) * 2) * 32 + p * 8
                turned_ref[at : at + 8, 0:128] = next_real[rows]
                turned_ref[at : at + 8, 128:256] = next_imag[rows]
                turned_ref[at + 32 : at + 40, 0:128] = next_imag[rows]
                turned_ref[at + 32 : at + 40, 128:256] = -next_real[rows]
    contract = (((1,), (1,)), ((), ()))
    for j in range(4):
        high, low = split(turned_ref[j * 384 : (j + 1) * 384, :])
        product = lax.dot_general(
            high_ref[...], high, contract, preferred_element_type=jnp.float32
        )
        product = product + lax.dot_general(
            high_ref[...], low, contract, preferred_element_type=jnp.float32
        )
        product = product + lax.dot_general(
            low_ref[...], high, contract, preferred_element_type=jnp.float32
        )
        for k in range(3):
            out_ref[pl.ds(j * 3 + k, 128, stride=12), :] = product[:, k * 128 : (k + 1) * 128]


def fft_list(values):
    size = len(values)
    if size == 1:
        return values
    even = fft_list(values[0::2])
    odd = fft_list(values[1::2])
    top, bottom = [], []
    for k in range(size // 2):
        real, imag = odd[k]
        if k == 0:
            pass
        elif 4 * k == size:
            real, imag = imag, -real
        elif 8 * k == size:
            half = math.sqrt(0.5)
            real, imag = (real + imag) * half, (imag - real) * half
        elif 8 * k == 3 * size:
            half = math.sqrt(0.5)
            real, imag = (imag - real) * half, -(real + imag) * half
        else:
            cos = math.cos(2.0 * math.pi * k / size)
            sin = math.sin(2.0 * math.pi * k / size)
            real, imag = real * cos + imag * sin, imag * cos - real * sin
        top.append((even[k][0] + real, even[k][1] + imag))
        bottom.append((even[k][0] - real, even[k][1] - imag))
    return top + bottom


def column_kernel(
    got_ref,
    high_ref,
    low_ref,
    turn_ref,
    real_hbm,
    imag_hbm,
    gathered_ref,
    stage_ref,
    real_ref,
    imag_ref,
    sem,
):
    blank = jnp.zeros((32, 128), jnp.float32)
    for pair in range(16):
        parts = []
        for side in range(2):
            for k in range(3):
                parts.append(got_ref[pl.ds((side * 16 + pair) * 3 + k, 16, stride=96), :])
        flipped = jnp.concatenate(parts + [blank], 0).T
        for m in range(2):
            for ri in range(2):
                at = (pair * 2 + m) * 32
                gathered_ref[at : at + 32, ri * 128 : (ri + 1) * 128] = flipped[
                    (m * 2 + ri) * 32 : (m * 2 + ri) * 32 + 32
                ]
    for part in range(4):
        rows = slice(part * 256, (part + 1) * 256)
        high, low = split(gathered_ref[rows, :])
        stage_ref[rows, :] = (
            dot(high, high_ref[...]) + dot(low, high_ref[...]) + dot(high, low_ref[...])
        )
    copies = []
    for p in range(PLANES):
        values = []
        for r in range(32):
            at = r * 32 + p * 8
            real = stage_ref[at : at + 8, 0:128]
            imag = stage_ref[at : at + 8, 128:256]
            if r:
                turn_real = turn_ref[r : r + 1, :]
                turn_imag = turn_ref[32 + r : 33 + r, :]
                real, imag = (
                    real * turn_real - imag * turn_imag,
                    real * turn_imag + imag * turn_real,
                )
            values.append((real, imag))
        for u, (real, imag) in enumerate(fft_list(values)):
            real_ref[p, :, u * 128 : (u + 1) * 128] = real
            imag_ref[p, :, u * 128 : (u + 1) * 128] = imag
        for m, (source, target) in enumerate(((real_ref, real_hbm), (imag_ref, imag_hbm))):
            copy = pltpu.make_async_copy(source.at[p], target.at[p], sem.at[p * 2 + m])
            copy.start()
            copies.append(copy)
    for copy in copies:
        copy.wait()


VMEM = pl.BlockSpec(memory_space=pltpu.VMEM)
SMEM = pl.BlockSpec(memory_space=pltpu.SMEM)
HBM = pl.BlockSpec(memory_space=pltpu.HBM)
PARAMS = pltpu.CompilerParams(vmem_limit_bytes=40 * 1024 * 1024)


def exchange(values, axes):
    return lax.all_to_all(values, axes, split_axis=0, concat_axis=0, tiled=True)


def shards(
    piece_ids, point_counts, wavenumber, strength, displacement, node_position, node_weights
):
    first, turn_one, second, third, turn_two = tables()
    copy = lax.axis_index("y").astype(jnp.int32).reshape(1)
    seat = lax.axis_index(("x_low", "core")).astype(jnp.int32).reshape(1)
    device = lax.axis_index(("z", "x_high", "x_low", "core", "y")).astype(jnp.int32).reshape(1)
    traits = jnp.concatenate([wavenumber, strength, displacement[0], displacement[1]])
    traits = jnp.concatenate(
        [
            jnp.pad(traits, (0, 12)),
            jnp.pad(node_position, ((0, 0), (0, 1))).reshape(32),
            jnp.pad(node_weights, (0, 65)),
        ]
    ).reshape(1, 128)
    sent = pl.pallas_call(
        sort_kernel,
        out_shape=jax.ShapeDtypeStruct((512, 128), jnp.int32),
        in_specs=[SMEM, HBM, HBM],
        out_specs=VMEM,
        scratch_shapes=[
            pltpu.VMEM((8, 128), jnp.int32),
            pltpu.VMEM((1024, 128), jnp.int32),
            pltpu.SemaphoreType.DMA((2,)),
        ],
        compiler_params=PARAMS,
    )(copy, piece_ids.reshape(8, 128), point_counts)
    got = exchange(sent.reshape(128, 4, 128), ("z", "x_high", "x_low", "core")).reshape(512, 128)
    grid = pl.pallas_call(
        place_kernel,
        out_shape=jax.ShapeDtypeStruct((768, 128), jnp.float32),
        in_specs=[SMEM, VMEM, VMEM],
        out_specs=VMEM,
        compiler_params=PARAMS,
    )(seat, traits, got)
    grid = exchange(grid, ("x_low", "core", "y"))
    sent = pl.pallas_call(
        fill_kernel,
        out_shape=jax.ShapeDtypeStruct((1536, 128), jnp.float32),
        in_specs=[SMEM] + [VMEM] * 5,
        out_specs=VMEM,
        scratch_shapes=[
            pltpu.VMEM((8, 128), jnp.float32),
            pltpu.VMEM((48, PLANES * ROWS * 128), jnp.float32),
            pltpu.VMEM((1536, 256), jnp.float32),
        ],
        compiler_params=PARAMS,
    )(device, grid, first, turn_one, second[0], second[1])
    got = exchange(
        sent.reshape(1536, 1, 128), ("z", "x_high", "x_low", "core", "y")
    ).reshape(1536, 128)
    shape = jax.ShapeDtypeStruct((PLANES, 8, LENGTH), jnp.float32)
    return pl.pallas_call(
        column_kernel,
        out_shape=(shape, shape),
        in_specs=[VMEM] * 4,
        out_specs=(HBM, HBM),
        scratch_shapes=[
            pltpu.VMEM((1024, 256), jnp.float32),
            pltpu.VMEM((1024, 256), jnp.float32),
            pltpu.VMEM((PLANES, 8, LENGTH), jnp.float32),
            pltpu.VMEM((PLANES, 8, LENGTH), jnp.float32),
            pltpu.SemaphoreType.DMA((2 * PLANES,)),
        ],
        compiler_params=PARAMS,
    )(got, third[0], third[1], turn_two)


def solution(mesh):
    every = ("z", "x_high", "x_low", "core", "y")
    fine = Mesh(mesh.devices.reshape(16, 2, 2, 2, 4), every)
    wide = every[:4]
    placed = (P(wide), P(wide, None), P("y"), P("y"), P(None, "y"), P(), P())
    return jax.shard_map(
        shards,
        mesh=fine,
        in_specs=placed,
        out_specs=(P(None, every, None), P(None, every, None)),
        check_vma=False,
    )
```

time: 130 us -> 124 us (0.954)
  starting transfers between devices: 29.3 us -> 27.3 us
  Pallas kernels: 9.61 us -> 7.73 us
  waiting for transfers between devices: 26.7 us -> 25.4 us
    all_to_all x2, starting transfers between devices: 29.3 us -> 27.3 us  [exchange(): return lax.all_to_all(values, axes, split_axis=0, concat_axis=0, tiled=True)]
    all_to_all x2, waiting for transfers between devices: 26.7 us -> 25.4 us  [exchange(): return lax.all_to_all(values, axes, split_axis=0, concat_axis=0, tiled=True)]
  transfers between devices with their start and end apart: 2 -> 2, of which waited for: 2 -> 2; matrix products, arithmetic and copies ran while one was open for 1% -> 2% of each run, Pallas kernels for 0% -> 0%
where the time goes in v1:
time: 124 us
  blocking collectives  56.8 us (46%)
  starting transfers between devices  27.3 us (22%)
  waiting for transfers between devices  25.4 us (20%)
  Pallas kernels  7.73 us (6%)
  local copies, waits for them, and re-layouts  3.06 us (2%)
  between operations  2.03 us (2%)
  other arithmetic  1.34 us (1%)
    all_to_all x1, blocking collectives, exchange(): return lax.all_to_all(values, axes, split_axis=0, concat_axis=0, tiled=True)  56.8 us
    all_to_all x2, starting transfers between devices, exchange(): return lax.all_to_all(values, axes, split_axis=0, concat_axis=0, tiled=True)  27.3 us
    all_to_all x2, waiting for transfers between devices, exchange(): return lax.all_to_all(values, axes, split_axis=0, concat_axis=0, tiled=True)  25.4 us
    pallas_call x1, Pallas kernels, shards(): pl.pallas_call(fill_kernel, out_shape=jax.ShapeDtypeStruct((1536, 128), j...  2.66 us
  transfers between devices with their start and end apart: 2, of which 2 were waited for; matrix products, arithmetic and copies ran while one was open for 2% of the time, Pallas kernels for 0%

profile of v1, /device:TPU:1, one launch (start us, length us, event | category | flops | bytes accessed | tf_op | source)
XLA Modules:
  0.0 123.6 jit_solution(11248169437471020000)
XLA Ops:
  0.6 0.0 copy-start.7
  0.6 0.7 copy-done.7
  1.3 1.0 copy-done
  2.4 1.7 %shard_map.149 = s32[512,128]{1,0:T(8,128)} custom-call(s32[1]{0:T(128)} %bitcast.5.copy_ref, s32[8,128]{1,0:T(8,128)S(1)} %bitcast.20, s32[1024,128]{1,0:T(8,128)S(1)} %copy-done), custom_call_target="tpu_custom_call" | custom-call | tf_op jit(solution)/shard_map/pallas_call | solution.py:409
  4.1 20.4 %all-to-all-start = ((s32[128,4,128]{2,1,0:T(4,128)}), s32[128,4,128]{2,1,0:T(4,128)S(1)}, u32[]{:S(2)}, u32[]{:S(2)}) async-start(s32[128,4,128]{2,1,0:T(4,128)} %bitcast.7), calls=%async_computation | async-start | bytes 524288 | tf_op jit(solution)/shard_map/all_to_all | solution.py:391
  25.2 0.0 copy-start.9
  25.8 0.0 copy-done.9
  25.9 0.1 reshape.38
  26.0 0.7 copy-done.8
  26.6 0.6 fusion.2
  27.2 1.3 %select_maximum_fusion = f32[16]{0:T(128)S(1)} fusion(f32[1]{0:T(128)} %bitcast.3, f32[1]{0:T(128)} %bitcast.2, f32[1]{0:T(128)S(6)} %copy.18, f32[1]{0:T(128)S(6)} %copy.17), kind=kLoop, calls=%fused_computation.2 | loop fusion | flops 128 | bytes 80 | tf_op jit(solution)/shard_map/concatenate | solution.py:401
  28.4 0.0 copy-done.10
  28.4 0.1 fusion.1.traits_ref
  28.5 16.5 %all-to-all-done = s32[128,4,128]{2,1,0:T(4,128)S(1)} async-done(((s32[128,4,128]{2,1,0:T(4,128)}), s32[128,4,128]{2,1,0:T(4,128)S(1)}, u32[]{:S(2)}, u32[]{:S(2)}) %all-to-all-start) | async-done | bytes 262176 | tf_op jit(solution)/shard_map/all_to_all | solution.py:391
  45.0 1.3 %shard_map.150 = f32[768,128]{1,0:T(8,128)} custom-call(s32[1]{0:T(128)} %bitcast.1.seat_ref, f32[1,128]{1,0:T(1,128)S(1)} %fusion.1.traits_ref, s32[512,128]{1,0:T(8,128)S(1)} %bitcast.19), custom_call_target="tpu_custom_call" | custom-call | tf_op jit(solution)/shard_map/pallas_call | solution.py:422
  46.3 6.9 %all-to-all-start.1 = ((f32[16,48,128]{2,1,0:T(8,128)}), f32[16,48,128]{2,1,0:T(8,128)S(1)}, u32[]{:S(2)}, u32[]{:S(2)}) async-start(f32[16,48,128]{2,1,0:T(8,128)} %bitcast.9), calls=%async_computation.1 | async-start | bytes 786432 | tf_op jit(solution)/shard_map/all_to_all | solution.py:391
  53.2 8.9 %all-to-all-done.1 = f32[16,48,128]{2,1,0:T(8,128)S(1)} async-done(((f32[16,48,128]{2,1,0:T(8,128)}), f32[16,48,128]{2,1,0:T(8,128)S(1)}, u32[]{:S(2)}, u32[]{:S(2)}) %all-to-all-start.1) | async-done | bytes 393248 | tf_op jit(solution)/shard_map/all_to_all | solution.py:391
  62.1 0.0 copy-done.4
  62.1 2.7 %shard_map.151 = f32[1536,128]{1,0:T(8,128)S(1)} custom-call(s32[1]{0:T(128)} %bitcast.place_ref, f32[768,128]{1,0:T(8,128)S(1)} %bitcast.18, bf16[64,144]{1,0:T(8,128)(2,1)S(1)} %copy-done.6, f32[64,128]{1,0:T(8,128)S(1)} %copy-done.3, bf16[128,256]{1,0:T(8,128)(2,1)S(1)} %copy-done.5, bf16[128,256]{1,0:T(8,128)(2,1)S(1)} %copy-done.4), custom_call_target="tpu_custom_call" | custom-call | tf_op jit(solution)/shard_map/pallas_call | solution.py:430
  64.7 0.0 copy-start.1
  64.7 0.0 copy-start.2
  64.8 56.8 %all_to_all.21 = f32[1536,1,128]{2,1,0:T(1,128)S(1)} all-to-all(f32[1536,1,128]{2,1,0:T(1,128)S(1)} %bitcast.17), channel_id=1, replica_groups=mesh['z'=16,'x_high'=2,'x_low'=2,'core'=2,'y'=4] {'z','x_high','x_low','..., dimensions={0} | all-to-all | bytes 1572864 | tf_op jit(solution)/shard_map/all_to_all | solution.py:391
  121.6 0.0 copy-done.2
  121.6 2.1 %shard_map.152 = (f32[4,8,4096]{2,1,0:T(8,128)}, f32[4,8,4096]{2,1,0:T(8,128)}) custom-call(f32[1536,128]{1,0:T(8,128)S(1)} %bitcast.16, bf16[256,256]{1,0:T(8,128)(2,1)S(1)} %copy-done.2, bf16[256,256]{1,0:T(8,128)(2,1)S(1)} %copy-done.1, f32[64,128]{1,0:T(8,128)S(1)} %copy-done.3), custom_call_target="tpu_custom_call" | custom-call | tf_op jit(solution)/shard_map/pallas_call | solution.py:446
  (12 shorter events, 0.0 us)
Async XLA Ops:
  0.6 0.7 copy-start.7
  1.3 1.0 copy-start
  4.1 40.9 %all-to-all-start = ((s32[128,4,128]{2,1,0:T(4,128)}), s32[128,4,128]{2,1,0:T(4,128)S(1)}, u32[]{:S(2)}, u32[]{:S(2)}) async-start(s32[128,4,128]{2,1,0:T(4,128)} %bitcast.7), calls=%async_computation | async-start | bytes 524288 | tf_op jit(solution)/shard_map/all_to_all | solution.py:391
  25.2 0.7 copy-start.9
  25.9 0.7 copy-start.8
  27.2 1.3 %copy-start.10 = (f32[15]{0:T(128)S(1)}, f32[15]{0:T(128)}, u32[]{:S(2)}) copy-start(f32[15]{0:T(128)} %param.20) | copy-start | bytes 184
  46.3 15.8 %copy-start.3 = (f32[64,128]{1,0:T(8,128)S(1)}, f32[64,128]{1,0:T(8,128)}, u32[]{:S(2)}) copy-start(f32[64,128]{1,0:T(8,128)} %constant.47.clone.turn_ref) | copy-start | bytes 98308
  46.3 15.8 %copy-start.4 = (bf16[128,256]{1,0:T(8,128)(2,1)S(1)}, bf16[128,256]{1,0:T(8,128)(2,1)}, u32[]{:S(2)}) copy-start(bf16[128,256]{1,0:T(8,128)(2,1)} %constant.49.clone.low_ref) | copy-start | bytes 196612
  46.3 15.8 %copy-start.5 = (bf16[128,256]{1,0:T(8,128)(2,1)S(1)}, bf16[128,256]{1,0:T(8,128)(2,1)}, u32[]{:S(2)}) copy-start(bf16[128,256]{1,0:T(8,128)(2,1)} %constant.48.clone.high_ref) | copy-start | bytes 196612
  46.3 15.8 %copy-start.6 = (bf16[64,144]{1,0:T(8,128)(2,1)S(1)}, bf16[64,144]{1,0:T(8,128)(2,1)}, u32[]{:S(2)}) copy-start(bf16[64,144]{1,0:T(8,128)(2,1)} %constant.46.clone.first_ref) | copy-start | bytes 55300
  46.3 15.8 %all-to-all-start.1 = ((f32[16,48,128]{2,1,0:T(8,128)}), f32[16,48,128]{2,1,0:T(8,128)S(1)}, u32[]{:S(2)}, u32[]{:S(2)}) async-start(f32[16,48,128]{2,1,0:T(8,128)} %bitcast.9), calls=%async_computation.1 | async-start | bytes 786432 | tf_op jit(solution)/shard_map/all_to_all | solution.py:391
  64.7 56.8 %copy-start.1 = (bf16[256,256]{1,0:T(8,128)(2,1)S(1)}, bf16[256,256]{1,0:T(8,128)(2,1)}, u32[]{:S(2)}) copy-start(bf16[256,256]{1,0:T(8,128)(2,1)} %constant.51.clone.low_ref) | copy-start | bytes 393220
  64.7 56.8 %copy-start.2 = (bf16[256,256]{1,0:T(8,128)(2,1)S(1)}, bf16[256,256]{1,0:T(8,128)(2,1)}, u32[]{:S(2)}) copy-start(bf16[256,256]{1,0:T(8,128)(2,1)} %constant.50.clone.high_ref) | copy-start | bytes 393220

commit v2 on v1

--- a/solution.py
+++ b/solution.py
@@ -100,8 +100,9 @@
     ids = ids_ref[...]
     block = ((ids >> 10) + 48) & 127
     part = block >> 4
-    seat = jnp.where(part < 3, part, jnp.where(part < ROWS, part + 1, part * 4 - 21))
-    target = ((block & 15) << 3) | seat
+    side = jnp.where(part < 3, 0, 1)
+    target = (part - 3 * side) * 32 + ((block & 15) << 1) + side
+    target = jnp.where(part < ROWS, target, block)
     local = ids & 1023
     high = ((local >> 5) + 1).astype(jnp.float32)
     low = (local & 31).astype(jnp.float32)
@@ -134,35 +135,43 @@
         picked = picked + dot(
             jnp.concatenate([chosen[k], chosen[k + 1]], 1), jnp.concatenate(rows, 0)
         )
-    named = jnp.zeros((128, 128), jnp.float32)
-    for s in range(SHARED):
-        rows = slice(s * 128, (s + 1) * 128)
-        out_ref[pl.ds(s, 128, stride=4), :] = picked[rows, :128].astype(jnp.int32)
-        name = picked[rows, 128:129] * 32.0 + picked[rows, 129:130]
-        named = jnp.where(lane == s, name, named)
-    out_ref[pl.ds(3, 128, stride=4), :] = named.astype(jnp.int32)
-
-
-def place_kernel(seat_ref, traits_ref, got_ref, out_ref):
-    names = got_ref[pl.ds(3, 128, stride=4), :].astype(jnp.float32).T
-    row = iota((768, 128), 0)
-    masks, counts = [], []
-    for s in range(SHARED):
-        name = names[s : s + 1, :].astype(jnp.int32)
-        column = ((name & 31) + 12) & 31
-        valid = (name > 0) & (column < LIVE_BLOCKS)
-        key = jnp.where(valid, ((name >> 5) - 1) * LIVE_BLOCKS + column, -1)
-        masks.append(as_mask(row == key))
-        counts.append(got_ref[pl.ds(s, 128, stride=4), :].astype(jnp.float32).astype(jnp.bfloat16))
-    vacant = seat_ref[0] == 3
-
-    @pl.when(vacant)
-    def _():
-        out_ref[...] = jnp.broadcast_to(traits_ref[0:1, :], (768, 128))
-
-    @pl.when(jnp.logical_not(vacant))
-    def _():
-        out_ref[...] = dot(jnp.concatenate(masks, 1), jnp.concatenate(counts, 0))
+    named = jnp.zeros((32, 128), jnp.float32)
+    for i in range(3):
+        for s in range(SHARED):
+            rows = slice(s * 128 + i * 32, s * 128 + i * 32 + 32)
+            out_ref[pl.ds(i * SHARED + s, 32, stride=10), :] = picked[rows, :128]
+            name = picked[rows, 128:129] * 32.0 + picked[rows, 129:130]
+            named = jnp.where(lane[:32] == i * SHARED + s, name, named)
+    out_ref[pl.ds(9, 32, stride=10), :] = named
+
+
+def place_kernel(core_ref, traits_ref, got_ref, out_ref):
+    names = got_ref[pl.ds(9, 64, stride=10), :]
+    names = jnp.concatenate([names, pltpu.roll(names, 127, 1)], 0).T
+    cell = iota((384, 128), 0)
+    row = iota((48, 128), 0)
+    first_lane = iota((48, 128), 1) == 0
+    for i in range(3):
+        masks, counts = [], []
+        for s, width in ((0, 128), (2, 64)):
+            name = names[i * SHARED + s : i * SHARED + s + 1, :width].astype(jnp.int32)
+            line = (name >> 5) - 1
+            column = ((name & 31) + 12) & 31
+            valid = (name > 0) & (column < LIVE_BLOCKS) & (((line >> 3) & 1) == core_ref[0])
+            seat = (line >> 4) * 4 + ((line >> 1) & 3)
+            key = jnp.where(valid, seat * 48 + (line & 1) * 24 + column, -1)
+            masks.append(as_mask(cell[:, :width] == key))
+        for s in range(SHARED):
+            counts.append(got_ref[pl.ds(i * SHARED + s, 64, stride=10), :].astype(jnp.bfloat16))
+        grid = dot(jnp.concatenate(masks, 1), jnp.concatenate(counts, 0))
+        extra = jnp.zeros((48, 128), jnp.float32)
+        if i < 2:
+            for m in range(2):
+                extra = jnp.where(first_lane & (row == m * 24), traits_ref[i * 2 + m], extra)
+        for d in range(8):
+            out_ref[d * 144 + i * 48 : d * 144 + i * 48 + 48, :] = (
+                grid[d * 48 : d * 48 + 48] + extra
+            )
 
 
 def evaluate(square, wave, strength, weight):
@@ -182,6 +191,7 @@
 
 def fill_kernel(
     place_ref,
+    nodes_ref,
     got_ref,
     first_ref,
     turn_ref,
@@ -192,56 +202,66 @@
     fill_ref,
     turned_ref,
 ):
-    device = place_ref[0]
-    z = device >> 5
-    side = (device >> 4) & 1
-    base = z * 32 + side * HALF + (device & 15) * 2 - HALF
+    base = place_ref[0]
+    right = place_ref[1] == 1
     column = (
         iota((LIVE_BLOCKS, 128), 0) * 128 + iota((LIVE_BLOCKS, 128), 1) - HALF
     ).astype(jnp.float32)
-    traits = [got_ref[(12 + p) * 48 : (12 + p) * 48 + 1, :] for p in range(PLANES)]
+    traits = [
+        [got_ref[p * 144 + e * 24 : p * 144 + e * 24 + 1, 0:1] for e in range(4)]
+        for p in range(PLANES)
+    ]
     counts = []
     for b in range(ROWS):
-        parts = []
-        for j in range(4):
-            at = ((b // 2) * 4 + j) * 48 + (b % 2) * 24
-            parts.append(got_ref[at : at + 24, :])
-        counts.append((parts[0] + parts[1]) + (parts[2] + parts[3]))
-    right = side == 1
-    near_ref[...] = jnp.zeros((8, 128), jnp.float32)
+        parts = [got_ref[m * 144 + b * 24 : m * 144 + b * 24 + 24, :] for m in range(8)]
+        while len(parts) > 1:
+            parts = [parts[m] + parts[m + 1] for m in range(0, len(parts), 2)]
+        counts.append(jnp.where(column > -float(HALF), parts[0], 0.0))
+    lane = iota((8, 128), 1)
+    inner = lane < 64
     for m in range(2):
-        near_ref[m * 2 : m * 2 + 2, :] = jnp.where(right, counts[m][11:13], counts[4 + m][11:13])
-    near_counts = near_ref[...]
-    sub = iota((8, 128), 0)
-    near_row = (base + jnp.where(right, 0, 1024) + (sub >> 1)).astype(jnp.float32)
-    near_col = ((sub & 1) * 128 + iota((8, 128), 1) - 128).astype(jnp.float32)
-    node_row = [traits[0][:, 16 + q : 17 + q] for q in range(NODES)]
-    node_col = [traits[0][:, 32 + q : 33 + q] for q in range(NODES)]
-    node_weight = [traits[0][:, 48 + q : 49 + q] for q in range(NODES)]
+        pair = jnp.where(right, counts[m][11:13], counts[4 + m][11:13])
+        merged = jnp.where(inner[0:1], pair[1:2], pair[0:1])
+        for p in range(PLANES):
+            near_ref[p * 2 + m : p * 2 + m + 1, :] = merged
+    for p in range(PLANES):
+        for e in range(4):
+            at = 8 + e * 8 + p * 2
+            near_ref[at : at + 2, :] = jnp.broadcast_to(traits[p][e], (2, 128))
+    near_counts = near_ref[0:8, :]
+    near_row = (base + jnp.where(right, 0, 1024) + (iota((8, 128), 0) & 1)).astype(jnp.float32)
+    near_row = near_row + near_ref[24:32, :]
+    near_col = jnp.where(inner, lane, lane - 128).astype(jnp.float32) + near_ref[32:40, :]
+    near_wave = near_ref[8:16, :] * (0.5 / math.pi)
+    near_strength = near_ref[16:24, :]
+    node_row = [nodes_ref[:, q : q + 1] for q in range(NODES)]
+    node_col = [nodes_ref[:, 16 + q : 17 + q] for q in range(NODES)]
+    node_weight = [nodes_ref[:, 32 + q : 33 + q] for q in range(NODES)]
     weights = [
         [jnp.where(counts[b] > float(q), node_weight[q], 0.0) for q in range(FAR)]
         for b in range(ROWS)
     ]
-    near_weights = [jnp.where(near_counts > float(q), node_weight[q], 0.0) for q in range(NODES)]
+    extra_real = jnp.zeros((8, 128), jnp.float32)
+    extra_imag = jnp.zeros((8, 128), jnp.float32)
+    for q in range(FAR, NODES):
+        row_pos = near_row + node_row[q]
+        col_pos = near_col + node_col[q]
+        square = row_pos * row_pos + col_pos * col_pos + HEIGHT_SQ
+        weight = jnp.where(near_counts > float(q), node_weight[q], 0.0)
+        real, imag = evaluate(square, near_wave, near_strength, weight)
+        extra_real = extra_real + real
+        extra_imag = extra_imag + imag
+    inner_pair = (iota((2, 128), 0) == 1) == inner[0:2]
     turn_real = turn_ref[0:32, :]
     turn_imag = turn_ref[32:64, :]
     for p in range(PLANES):
-        wave, strength = traits[p][:, 0:1] * (0.5 / math.pi), traits[p][:, 1:2]
-        shift_row, shift_col = traits[p][:, 2:3], traits[p][:, 3:4]
+        wave, strength = traits[p][0] * (0.5 / math.pi), traits[p][1]
+        shift_row, shift_col = traits[p][2], traits[p][3]
         col_base = column + shift_col
         col_sq = []
         for q in range(FAR):
             col_pos = col_base + node_col[q]
             col_sq.append(col_pos * col_pos)
-        extra_real = jnp.zeros((8, 128), jnp.float32)
-        extra_imag = jnp.zeros((8, 128), jnp.float32)
-        for q in range(FAR, NODES):
-            row_pos = (near_row + shift_row) + node_row[q]
-            col_pos = (near_col + shift_col) + node_col[q]
-            square = row_pos * row_pos + col_pos * col_pos + HEIGHT_SQ
-            real, imag = evaluate(square, wave, strength, near_weights[q])
-            extra_real = extra_real + real
-            extra_imag = extra_imag + imag
         for b in range(ROWS):
             row_offset = (base + (512 * (b // 2) + b % 2)).astype(jnp.float32)
             total_real = jnp.zeros((LIVE_BLOCKS, 128), jnp.float32)
@@ -257,12 +277,13 @@
             fill_ref[24:48, lanes] = -total_imag
             if b // 2 != 1:
                 use = right if b // 2 == 0 else jnp.logical_not(right)
-                m = (b % 2) * 2
+                use = use & inner_pair
+                m = p * 2 + b % 2
                 fill_ref[11:13, lanes] = fill_ref[11:13, lanes] + jnp.where(
-                    use, extra_real[m : m + 2], 0.0
+                    use, extra_real[m : m + 1], 0.0
                 )
                 fill_ref[35:37, lanes] = fill_ref[35:37, lanes] - jnp.where(
-                    use, extra_imag[m : m + 2], 0.0
+                    use, extra_imag[m : m + 1], 0.0
                 )
         lanes = slice(p * ROWS * 128, (p + 1) * ROWS * 128)
         high, low = split(fill_ref[:, lanes])
@@ -395,20 +416,21 @@
     piece_ids, point_counts, wavenumber, strength, displacement, node_position, node_weights
 ):
     first, turn_one, second, third, turn_two = tables()
-    copy = lax.axis_index("y").astype(jnp.int32).reshape(1)
-    seat = lax.axis_index(("x_low", "core")).astype(jnp.int32).reshape(1)
-    device = lax.axis_index(("z", "x_high", "x_low", "core", "y")).astype(jnp.int32).reshape(1)
+    copy = lax.axis_index("y").astype(jnp.int32)
+    core = lax.axis_index("core").astype(jnp.int32)
+    side = lax.axis_index("x_high").astype(jnp.int32)
+    seat = lax.axis_index(("x_low", "core", "y")).astype(jnp.int32)
+    base = lax.axis_index("z").astype(jnp.int32) * 32 + (side - 1) * HALF + seat * 2
     traits = jnp.concatenate([wavenumber, strength, displacement[0], displacement[1]])
-    traits = jnp.concatenate(
+    nodes = jnp.concatenate(
         [
-            jnp.pad(traits, (0, 12)),
             jnp.pad(node_position, ((0, 0), (0, 1))).reshape(32),
-            jnp.pad(node_weights, (0, 65)),
+            jnp.pad(node_weights, (0, 81)),
         ]
     ).reshape(1, 128)
     sent = pl.pallas_call(
         sort_kernel,
-        out_shape=jax.ShapeDtypeStruct((512, 128), jnp.int32),
+        out_shape=jax.ShapeDtypeStruct((320, 128), jnp.float32),
         in_specs=[SMEM, HBM, HBM],
         out_specs=VMEM,
         scratch_shapes=[
@@ -416,29 +438,30 @@
             pltpu.VMEM((1024, 128), jnp.int32),
             pltpu.SemaphoreType.DMA((2,)),
         ],
-        compiler_params=PARAMS,
-    )(copy, piece_ids.reshape(8, 128), point_counts)
-    got = exchange(sent.reshape(128, 4, 128), ("z", "x_high", "x_low", "core")).reshape(512, 128)
+        compiler_params=pltpu.CompilerParams(vmem_limit_bytes=62 * 1024 * 1024),
+    )(copy.reshape(1), piece_ids.reshape(8, 128), point_counts)
+    got = exchange(sent.reshape(320, 1, 128), ("z", "x_high")).reshape(320, 128)
+    got = lax.all_gather(got, "core", axis=0, tiled=True)
     grid = pl.pallas_call(
         place_kernel,
-        out_shape=jax.ShapeDtypeStruct((768, 128), jnp.float32),
-        in_specs=[SMEM, VMEM, VMEM],
+        out_shape=jax.ShapeDtypeStruct((1152, 128), jnp.float32),
+        in_specs=[SMEM, SMEM, VMEM],
         out_specs=VMEM,
         compiler_params=PARAMS,
-    )(seat, traits, got)
-    grid = exchange(grid, ("x_low", "core", "y"))
+    )(core.reshape(1), traits, got)
+    grid = exchange(grid.reshape(1152, 1, 128), ("x_low", "y")).reshape(1152, 128)
     sent = pl.pallas_call(
         fill_kernel,
         out_shape=jax.ShapeDtypeStruct((1536, 128), jnp.float32),
-        in_specs=[SMEM] + [VMEM] * 5,
+        in_specs=[SMEM] + [VMEM] * 6,
         out_specs=VMEM,
         scratch_shapes=[
-            pltpu.VMEM((8, 128), jnp.float32),
+            pltpu.VMEM((40, 128), jnp.float32),
             pltpu.VMEM((48, PLANES * ROWS * 128), jnp.float32),
             pltpu.VMEM((1536, 256), jnp.float32),
         ],
         compiler_params=PARAMS,
-    )(device, grid, first, turn_one, second[0], second[1])
+    )(jnp.stack([base, side]), nodes, grid, first, turn_one, second[0], second[1])
     got = exchange(
         sent.reshape(1536, 1, 128), ("z", "x_high", "x_low", "core", "y")
     ).reshape(1536, 128)

time: 124 us -> 122 us (0.984)
  blocking collectives: 56.8 us -> 63.8 us
  waiting for transfers between devices: 25.4 us -> 20.4 us
  starting transfers between devices: 27.3 us -> 22.9 us
  local copies, waits for them, and re-layouts: 3.06 us -> 1.32 us
  Pallas kernels: 7.73 us -> 9.28 us
    all_gather x0 -> x1, blocking collectives: none -> 5.29 us  [shards(): got = lax.all_gather(got, 'core', axis=0, tiled=True)]
    all_to_all x2, waiting for transfers between devices: 25.4 us -> 20.4 us  [exchange(): return lax.all_to_all(values, axes, split_axis=0, concat_axis=0, tiled=True)]
    all_to_all x2, starting transfers between devices: 27.3 us -> 22.9 us  [exchange(): return lax.all_to_all(values, axes, split_axis=0, concat_axis=0, tiled=True)]
    unnamed x22 -> x18, local copies, waits for them, and re-layouts: 2.42 us -> 0.62 us
    all_to_all x1, blocking collectives: 56.8 us -> 58.5 us  [exchange(): return lax.all_to_all(values, axes, split_axis=0, concat_axis=0, tiled=True)]
where the time goes in v2:
time: 122 us; the launch traced here: 121 us
  blocking collectives  63.8 us (52%)
  starting transfers between devices  22.9 us (19%)
  waiting for transfers between devices  20.4 us (17%)
  Pallas kernels  9.28 us (8%)
  between operations  2.06 us (2%)
  other arithmetic  1.41 us (1%)
  local copies, waits for them, and re-layouts  1.32 us (1%)
    all_to_all x1, blocking collectives, exchange(): return lax.all_to_all(values, axes, split_axis=0, concat_axis=0, tiled=True)  58.5 us
    all_to_all x2, starting transfers between devices, exchange(): return lax.all_to_all(values, axes, split_axis=0, concat_axis=0, tiled=True)  22.9 us
    all_to_all x2, waiting for transfers between devices, exchange(): return lax.all_to_all(values, axes, split_axis=0, concat_axis=0, tiled=True)  20.4 us
    all_gather x1, blocking collectives, shards(): got = lax.all_gather(got, 'core', axis=0, tiled=True)  5.29 us
    pallas_call x1, Pallas kernels, shards(): pl.pallas_call(fill_kernel, out_shape=jax.ShapeDtypeStruct((1536, 128), j...  3.03 us
  transfers between devices with their start and end apart: 2, of which 2 were waited for; matrix products, arithmetic and copies ran while one was open for 2% of the time, Pallas kernels for 0%

profile of v2, /device:TPU:1, one launch (start us, length us, event | category | flops | bytes accessed | tf_op | source)
XLA Modules:
  0.0 121.2 jit_solution(7187746079934088711)
XLA Ops:
  0.6 2.4 %shard_map.149 = f32[320,128]{1,0:T(8,128)} custom-call(s32[1]{0:T(128)} %bitcast.6.copy_ref, s32[8,128]{1,0:T(8,128)} %bitcast.28, s32[1024,128]{1,0:T(8,128)} %counts_hbm.1), custom_call_target="tpu_custom_call" | custom-call | tf_op jit(solution)/shard_map/pallas_call | solution.py:431
  3.0 18.5 %all-to-all-start = ((f32[320,1,128]{2,1,0:T(1,128)}), f32[320,1,128]{2,1,0:T(1,128)S(1)}, u32[]{:S(2)}, u32[]{:S(2)}) async-start(f32[320,1,128]{2,1,0:T(1,128)} %bitcast.27), calls=%async_computation | async-start | bytes 327680 | tf_op jit(solution)/shard_map/all_to_all | solution.py:412
  22.2 0.0 copy-start.6
  22.9 0.0 copy-done.6
  22.9 0.6 fusion.2
  23.5 1.3 %pad_maximum_fusion.traits_ref = f32[4]{0:T(128)S(1)} fusion(f32[1]{0:T(128)} %bitcast.5, f32[1]{0:T(128)} %bitcast.4, f32[1]{0:T(128)S(6)} %copy.21, f32[1]{0:T(128)S(6)} %copy.20), kind=kLoop, calls=%fused_computation.3 | loop fusion | flops 12 | bytes 32 | tf_op jit(solution)/shard_map/concatenate | solution.py:424
  24.8 12.6 %all-to-all-done = f32[320,1,128]{2,1,0:T(1,128)S(1)} async-done(((f32[320,1,128]{2,1,0:T(1,128)}), f32[320,1,128]{2,1,0:T(1,128)S(1)}, u32[]{:S(2)}, u32[]{:S(2)}) %all-to-all-start) | async-done | bytes 163872 | tf_op jit(solution)/shard_map/all_to_all | solution.py:412
  37.3 5.3 %all-gather = f32[640,1,128]{2,0,1:T(8,128)S(1)} all-gather(f32[320,1,128]{2,0,1:T(8,128)S(1)} %bitcast.26), channel_id=2, replica_groups=mesh['z'=16,'x_high'=2,'x_low'=2,'core'=2,'y'=4] {'core'}, dimensions={0}, use_global_device_ids=true | all-gather | bytes 491520 | tf_op jit(solution)/shard_map/all_gather | solution.py:444
  42.6 1.8 %shard_map.150 = f32[1152,128]{1,0:T(8,128)} custom-call(s32[1]{0:T(128)} %bitcast.3.core_ref, f32[4]{0:T(128)S(1)} %pad_maximum_fusion.traits_ref, f32[640,128]{1,0:T(8,128)S(1)} %bitcast.25), custom_call_target="tpu_custom_call" | custom-call | tf_op jit(solution)/shard_map/pallas_call | solution.py:445
  44.4 4.4 %all-to-all-start.1 = ((f32[1152,1,128]{2,1,0:T(1,128)}), f32[1152,1,128]{2,1,0:T(1,128)S(1)}, u32[]{:S(2)}, u32[]{:S(2)}) async-start(f32[1152,1,128]{2,1,0:T(1,128)} %bitcast.13), calls=%async_computation.1 | async-start | bytes 1179648 | tf_op jit(solution)/shard_map/all_to_all | solution.py:412
  48.8 0.0 copy-done.7
  48.8 0.1 reshape.37
  48.9 0.1 pad_add_fusion.place_ref
  49.0 0.6 copy-done.8
  49.6 0.1 fusion.1.nodes_ref
  49.6 7.9 %all-to-all-done.1 = f32[1152,1,128]{2,1,0:T(1,128)S(1)} async-done(((f32[1152,1,128]{2,1,0:T(1,128)}), f32[1152,1,128]{2,1,0:T(1,128)S(1)}, u32[]{:S(2)}, u32[]{:S(2)}) %all-to-all-start.1) | async-done | bytes 589856 | tf_op jit(solution)/shard_map/all_to_all | solution.py:412
  57.5 0.0 copy-done.3
  57.5 0.0 copy-done.4
  57.5 3.0 %shard_map.151 = f32[1536,128]{1,0:T(8,128)S(1)} custom-call(s32[2]{0:T(128)S(1)} %pad_add_fusion.place_ref, f32[1,128]{1,0:T(1,128)S(1)} %fusion.1.nodes_ref, f32[1152,128]{1,0:T(8,128)S(1)} %bitcast.24, bf16[64,144]{1,0:T(8,128)(2,1)S(1)} %copy-done.5, f32[64,128]{1,0:T(8,128)S(1)} %copy-done.2, bf16[128,256]{1,0:T(8,128)(2,1)S(1)} %copy-done.4, ...), custom_call_target="tpu_custom_call" | custom-call | tf_op jit(solution)/shard_map/pallas_call | solution.py:453
  60.6 0.0 copy-start
  60.6 0.0 copy-start.1
  60.6 58.5 %all_to_all.15 = f32[1536,1,128]{2,1,0:T(1,128)S(1)} all-to-all(f32[1536,1,128]{2,1,0:T(1,128)S(1)} %bitcast.23), channel_id=1, replica_groups=mesh['z'=16,'x_high'=2,'x_low'=2,'core'=2,'y'=4] {'z','x_high','x_low','..., dimensions={0} | all-to-all | bytes 1572864 | tf_op jit(solution)/shard_map/all_to_all | solution.py:412
  119.1 0.0 copy-done
  119.1 2.1 %shard_map.152 = (f32[4,8,4096]{2,1,0:T(8,128)}, f32[4,8,4096]{2,1,0:T(8,128)}) custom-call(f32[1536,128]{1,0:T(8,128)S(1)} %bitcast.22, bf16[256,256]{1,0:T(8,128)(2,1)S(1)} %copy-done.1, bf16[256,256]{1,0:T(8,128)(2,1)S(1)} %copy-done, f32[64,128]{1,0:T(8,128)S(1)} %copy-done.2), custom_call_target="tpu_custom_call" | custom-call | tf_op jit(solution)/shard_map/pallas_call | solution.py:469
  (10 shorter events, 0.0 us)
Async XLA Ops:
  3.0 34.3 %all-to-all-start = ((f32[320,1,128]{2,1,0:T(1,128)}), f32[320,1,128]{2,1,0:T(1,128)S(1)}, u32[]{:S(2)}, u32[]{:S(2)}) async-start(f32[320,1,128]{2,1,0:T(1,128)} %bitcast.27), calls=%async_computation | async-start | bytes 327680 | tf_op jit(solution)/shard_map/all_to_all | solution.py:412
  22.2 0.7 copy-start.6
  44.4 4.4 %copy-start.7 = (f32[2,15]{1,0:T(2,128)S(1)}, f32[2,15]{1,0:T(2,128)}, u32[]{:S(2)}) copy-start(f32[2,15]{1,0:T(2,128)} %param.19) | copy-start | bytes 364
  44.4 13.1 %copy-start.3 = (bf16[128,256]{1,0:T(8,128)(2,1)S(1)}, bf16[128,256]{1,0:T(8,128)(2,1)}, u32[]{:S(2)}) copy-start(bf16[128,256]{1,0:T(8,128)(2,1)} %constant.52.clone.low_ref) | copy-start | bytes 196612
  44.4 13.1 %copy-start.4 = (bf16[128,256]{1,0:T(8,128)(2,1)S(1)}, bf16[128,256]{1,0:T(8,128)(2,1)}, u32[]{:S(2)}) copy-start(bf16[128,256]{1,0:T(8,128)(2,1)} %constant.51.clone.high_ref) | copy-start | bytes 196612
  44.4 13.1 %copy-start.5 = (bf16[64,144]{1,0:T(8,128)(2,1)S(1)}, bf16[64,144]{1,0:T(8,128)(2,1)}, u32[]{:S(2)}) copy-start(bf16[64,144]{1,0:T(8,128)(2,1)} %constant.49.clone.first_ref) | copy-start | bytes 55300
  44.4 13.1 %all-to-all-start.1 = ((f32[1152,1,128]{2,1,0:T(1,128)}), f32[1152,1,128]{2,1,0:T(1,128)S(1)}, u32[]{:S(2)}, u32[]{:S(2)}) async-start(f32[1152,1,128]{2,1,0:T(1,128)} %bitcast.13), calls=%async_computation.1 | async-start | bytes 1179648 | tf_op jit(solution)/shard_map/all_to_all | solution.py:412
  48.8 8.7 %copy-start.2 = (f32[64,128]{1,0:T(8,128)S(1)}, f32[64,128]{1,0:T(8,128)}, u32[]{:S(2)}) copy-start(f32[64,128]{1,0:T(8,128)} %constant.50.clone.turn_ref) | copy-start | bytes 98308
  48.9 0.7 copy-start.8
  60.6 58.6 %copy-start = (bf16[256,256]{1,0:T(8,128)(2,1)S(1)}, bf16[256,256]{1,0:T(8,128)(2,1)}, u32[]{:S(2)}) copy-start(bf16[256,256]{1,0:T(8,128)(2,1)} %constant.54.clone.low_ref) | copy-start | bytes 393220
  60.6 58.6 %copy-start.1 = (bf16[256,256]{1,0:T(8,128)(2,1)S(1)}, bf16[256,256]{1,0:T(8,128)(2,1)}, u32[]{:S(2)}) copy-start(bf16[256,256]{1,0:T(8,128)(2,1)} %constant.53.clone.high_ref) | copy-start | bytes 393220

commit v3 on v2

--- a/solution.py
+++ b/solution.py
@@ -55,7 +55,9 @@
     angle = 2.0 * np.pi * (v1[:, None] * t[None, :]) / LENGTH
     turn_one = np.concatenate([np.cos(angle), -np.sin(angle)], 0).astype(np.float32)
     angle = 2.0 * np.pi * ((t[:, None] * t[None, :]) % 128) / 128
-    second = split_np(np.concatenate([np.cos(angle), np.sin(angle)], 1) / 64.0)
+    cos, sin = np.cos(angle), np.sin(angle)
+    second = np.concatenate([np.concatenate([cos, sin], 1), np.concatenate([-sin, cos], 1)], 0)
+    second = np.concatenate(split_np(second / 64.0), 0)
     c = np.arange(96)
     angle = 2.0 * np.pi * (((c[:, None] - 48) * t[None, :]) % 128) / 128
     third = np.zeros((2, 128, 2, 128))
@@ -87,15 +89,17 @@
     return high, low
 
 
-def sort_kernel(copy_ref, ids_hbm, counts_hbm, out_ref, ids_ref, counts_ref, sem):
+def sort_kernel(ids_hbm, counts_hbm, out_ref, ids_ref, counts_ref, sem):
     ids_copy = pltpu.make_async_copy(ids_hbm, ids_ref, sem.at[0])
     ids_copy.start()
     counts_copy = pltpu.make_async_copy(counts_hbm, counts_ref, sem.at[1])
     counts_copy.start()
-    base = copy_ref[0] * SHARED
-    owner = iota((128, 128), 0)
+    base = (lax.axis_index("y") * SHARED).astype(jnp.float32)
+    live = iota((96, 128), 0)
     lane = iota((128, 128), 1)
-    prefix = jnp.concatenate([as_mask(owner < lane), jnp.ones((128, 128), jnp.bfloat16)], 1)
+    prefix = jnp.concatenate(
+        [as_mask(iota((128, 128), 0) < lane), jnp.ones((128, 128), jnp.bfloat16)], 1
+    )
     ids_copy.wait()
     ids = ids_ref[...]
     block = ((ids >> 10) + 48) & 127
@@ -103,49 +107,48 @@
     side = jnp.where(part < 3, 0, 1)
     target = (part - 3 * side) * 32 + ((block & 15) << 1) + side
     target = jnp.where(part < ROWS, target, block)
+    here = [live == target[k : k + 1, :] for k in range(8)]
+    sums = dot(jnp.concatenate([as_mask(mask) for mask in here], 0), prefix)
     local = ids & 1023
     high = ((local >> 5) + 1).astype(jnp.float32)
     low = (local & 31).astype(jnp.float32)
-    pad = jnp.zeros((120, 128), jnp.float32)
-    high = jnp.concatenate([high, pad], 0).T
-    low = jnp.concatenate([low, pad], 0).T
-    here = [owner == target[k : k + 1, :] for k in range(8)]
-    sums = [dot(as_mask(here[k]), prefix) for k in range(8)]
-    running = jnp.zeros((128, 128), jnp.float32)
+    pad = jnp.zeros((112, 128), jnp.float32)
+    named = jnp.concatenate([high, low, pad], 0).T
+    running = jnp.zeros((96, 128), jnp.float32) - base
     chosen = []
     for k in range(8):
-        rank = running + sums[k][:, :128]
-        running = running + sums[k][:, 128:]
+        rows = slice(k * 96, (k + 1) * 96)
+        rank = running + sums[rows, :128]
+        running = running + sums[rows, 128:]
         chosen.append(
-            jnp.concatenate(
-                [as_mask(here[k] & (rank == (base + s).astype(jnp.float32))) for s in range(SHARED)],
-                0,
-            )
+            jnp.concatenate([as_mask(here[k] & (rank == float(s))) for s in range(SHARED)], 0)
         )
     counts_copy.wait()
-    picked = jnp.zeros((SHARED * 128, 256), jnp.float32)
+    picked = jnp.zeros((SHARED * 96, 256), jnp.float32)
     for k in range(0, 8, 2):
         rows = []
         for m in (k, k + 1):
             counts = counts_ref[m * 128 : (m + 1) * 128, :].astype(jnp.float32)
             name = jnp.where(
-                lane == 0, high[:, m : m + 1], jnp.where(lane == 1, low[:, m : m + 1], 0.0)
+                lane == 0, named[:, m : m + 1], jnp.where(lane == 1, named[:, 8 + m : 9 + m], 0.0)
             )
             rows.append(jnp.concatenate([counts, name], 1).astype(jnp.bfloat16))
         picked = picked + dot(
             jnp.concatenate([chosen[k], chosen[k + 1]], 1), jnp.concatenate(rows, 0)
         )
-    named = jnp.zeros((32, 128), jnp.float32)
+    names = jnp.zeros((32, 128), jnp.float32)
     for i in range(3):
         for s in range(SHARED):
-            rows = slice(s * 128 + i * 32, s * 128 + i * 32 + 32)
+            rows = slice(s * 96 + i * 32, s * 96 + i * 32 + 32)
             out_ref[pl.ds(i * SHARED + s, 32, stride=10), :] = picked[rows, :128]
             name = picked[rows, 128:129] * 32.0 + picked[rows, 129:130]
-            named = jnp.where(lane[:32] == i * SHARED + s, name, named)
-    out_ref[pl.ds(9, 32, stride=10), :] = named
-
-
-def place_kernel(core_ref, traits_ref, got_ref, out_ref):
+            names = jnp.where(lane[:32] == i * SHARED + s, name, names)
+    out_ref[pl.ds(9, 32, stride=10), :] = names
+
+
+def place_kernel(traits_ref, got_ref, out_ref):
+    core = lax.axis_index("core")
+    traits = [traits_ref[0:1, m : m + 1] for m in range(4)]
     names = got_ref[pl.ds(9, 64, stride=10), :]
     names = jnp.concatenate([names, pltpu.roll(names, 127, 1)], 0).T
     cell = iota((384, 128), 0)
@@ -157,7 +160,7 @@
             name = names[i * SHARED + s : i * SHARED + s + 1, :width].astype(jnp.int32)
             line = (name >> 5) - 1
             column = ((name & 31) + 12) & 31
-            valid = (name > 0) & (column < LIVE_BLOCKS) & (((line >> 3) & 1) == core_ref[0])
+            valid = (name > 0) & (column < LIVE_BLOCKS) & (((line >> 3) & 1) == core)
             seat = (line >> 4) * 4 + ((line >> 1) & 3)
             key = jnp.where(valid, seat * 48 + (line & 1) * 24 + column, -1)
             masks.append(as_mask(cell[:, :width] == key))
@@ -167,7 +170,7 @@
         extra = jnp.zeros((48, 128), jnp.float32)
         if i < 2:
             for m in range(2):
-                extra = jnp.where(first_lane & (row == m * 24), traits_ref[i * 2 + m], extra)
+                extra = jnp.where(first_lane & (row == m * 24), traits[i * 2 + m], extra)
         for d in range(8):
             out_ref[d * 144 + i * 48 : d * 144 + i * 48 + 48, :] = (
                 grid[d * 48 : d * 48 + 48] + extra
@@ -190,20 +193,20 @@
 
 
 def fill_kernel(
-    place_ref,
     nodes_ref,
     got_ref,
     first_ref,
     turn_ref,
-    high_ref,
-    low_ref,
+    second_ref,
     out_ref,
     near_ref,
     fill_ref,
     turned_ref,
 ):
-    base = place_ref[0]
-    right = place_ref[1] == 1
+    side = lax.axis_index("x_high")
+    seat = (lax.axis_index("x_low") * 2 + lax.axis_index("core")) * 4 + lax.axis_index("y")
+    base = lax.axis_index("z") * 32 + (side - 1) * HALF + seat * 2
+    right = side == 1
     column = (
         iota((LIVE_BLOCKS, 128), 0) * 128 + iota((LIVE_BLOCKS, 128), 1) - HALF
     ).astype(jnp.float32)
@@ -234,9 +237,9 @@
     near_col = jnp.where(inner, lane, lane - 128).astype(jnp.float32) + near_ref[32:40, :]
     near_wave = near_ref[8:16, :] * (0.5 / math.pi)
     near_strength = near_ref[16:24, :]
-    node_row = [nodes_ref[:, q : q + 1] for q in range(NODES)]
-    node_col = [nodes_ref[:, 16 + q : 17 + q] for q in range(NODES)]
-    node_weight = [nodes_ref[:, 32 + q : 33 + q] for q in range(NODES)]
+    node_row = [nodes_ref[0:1, 16 + q : 17 + q] for q in range(NODES)]
+    node_col = [nodes_ref[0:1, 32 + q : 33 + q] for q in range(NODES)]
+    node_weight = [nodes_ref[0:1, 48 + q : 49 + q] for q in range(NODES)]
     weights = [
         [jnp.where(counts[b] > float(q), node_weight[q], 0.0) for q in range(FAR)]
         for b in range(ROWS)
@@ -295,25 +298,25 @@
             next_imag = real * turn_imag + imag * turn_real
             for j in range(4):
                 rows = slice(j * 8, j * 8 + 8)
-                at = ((j * 3 + b // 2) * 4 + (b % 2) * 2) * 32 + p * 8
+                at = (((b // 2) * 4 + j) * 2 + b % 2) * 32 + p * 8
                 turned_ref[at : at + 8, 0:128] = next_real[rows]
                 turned_ref[at : at + 8, 128:256] = next_imag[rows]
-                turned_ref[at + 32 : at + 40, 0:128] = next_imag[rows]
-                turned_ref[at + 32 : at + 40, 128:256] = -next_real[rows]
     contract = (((1,), (1,)), ((), ()))
-    for j in range(4):
-        high, low = split(turned_ref[j * 384 : (j + 1) * 384, :])
-        product = lax.dot_general(
-            high_ref[...], high, contract, preferred_element_type=jnp.float32
+    left = iota((128, 128), 1) < 64
+    for i in range(3):
+        high, low = split(turned_ref[i * 256 : (i + 1) * 256, :])
+        both = lax.dot_general(second_ref[...], high, contract, preferred_element_type=jnp.float32)
+        rest = lax.dot_general(
+            second_ref[0:256, :], low, contract, preferred_element_type=jnp.float32
         )
-        product = product + lax.dot_general(
-            high_ref[...], low, contract, preferred_element_type=jnp.float32
-        )
-        product = product + lax.dot_general(
-            low_ref[...], high, contract, preferred_element_type=jnp.float32
-        )
-        for k in range(3):
-            out_ref[pl.ds(j * 3 + k, 128, stride=12), :] = product[:, k * 128 : (k + 1) * 128]
+        product = (both[0:256] + both[256:512]) + rest
+        for m in range(2):
+            real = product[0:128, m * 128 : (m + 1) * 128]
+            imag = product[128:256, m * 128 : (m + 1) * 128]
+            even = jnp.where(left, real, pltpu.roll(imag, 64, 1))
+            odd = jnp.where(left, pltpu.roll(real, 64, 1), imag)
+            out_ref[pl.ds(m * 6 + i, 128, stride=12), :] = even
+            out_ref[pl.ds(m * 6 + 3 + i, 128, stride=12), :] = odd
 
 
 def fft_list(values):
@@ -352,7 +355,6 @@
     real_hbm,
     imag_hbm,
     gathered_ref,
-    stage_ref,
     real_ref,
     imag_ref,
     sem,
@@ -366,23 +368,20 @@
         flipped = jnp.concatenate(parts + [blank], 0).T
         for m in range(2):
             for ri in range(2):
-                at = (pair * 2 + m) * 32
-                gathered_ref[at : at + 32, ri * 128 : (ri + 1) * 128] = flipped[
-                    (m * 2 + ri) * 32 : (m * 2 + ri) * 32 + 32
-                ]
-    for part in range(4):
-        rows = slice(part * 256, (part + 1) * 256)
-        high, low = split(gathered_ref[rows, :])
-        stage_ref[rows, :] = (
-            dot(high, high_ref[...]) + dot(low, high_ref[...]) + dot(high, low_ref[...])
-        )
+                for p in range(PLANES):
+                    at = (p * 32 + pair * 2 + m) * 8
+                    gathered_ref[at : at + 8, ri * 128 : (ri + 1) * 128] = flipped[
+                        ((ri * 2 + m) * 4 + p) * 8 : ((ri * 2 + m) * 4 + p) * 8 + 8
+                    ]
+    high, low = split(gathered_ref[...])
+    stage = dot(high, high_ref[...]) + dot(low, high_ref[...]) + dot(high, low_ref[...])
     copies = []
     for p in range(PLANES):
         values = []
         for r in range(32):
-            at = r * 32 + p * 8
-            real = stage_ref[at : at + 8, 0:128]
-            imag = stage_ref[at : at + 8, 128:256]
+            at = (p * 32 + r) * 8
+            real = stage[at : at + 8, 0:128]
+            imag = stage[at : at + 8, 128:256]
             if r:
                 turn_real = turn_ref[r : r + 1, :]
                 turn_imag = turn_ref[32 + r : 33 + r, :]
@@ -416,22 +415,25 @@
     piece_ids, point_counts, wavenumber, strength, displacement, node_position, node_weights
 ):
     first, turn_one, second, third, turn_two = tables()
-    copy = lax.axis_index("y").astype(jnp.int32)
-    core = lax.axis_index("core").astype(jnp.int32)
-    side = lax.axis_index("x_high").astype(jnp.int32)
-    seat = lax.axis_index(("x_low", "core", "y")).astype(jnp.int32)
-    base = lax.axis_index("z").astype(jnp.int32) * 32 + (side - 1) * HALF + seat * 2
-    traits = jnp.concatenate([wavenumber, strength, displacement[0], displacement[1]])
     nodes = jnp.concatenate(
         [
-            jnp.pad(node_position, ((0, 0), (0, 1))).reshape(32),
-            jnp.pad(node_weights, (0, 81)),
+            wavenumber,
+            strength,
+            displacement[0],
+            displacement[1],
+            jnp.zeros((12,), jnp.float32),
+            node_position[0],
+            jnp.zeros((1,), jnp.float32),
+            node_position[1],
+            jnp.zeros((1,), jnp.float32),
+            node_weights,
+            jnp.zeros((65,), jnp.float32),
         ]
     ).reshape(1, 128)
     sent = pl.pallas_call(
         sort_kernel,
         out_shape=jax.ShapeDtypeStruct((320, 128), jnp.float32),
-        in_specs=[SMEM, HBM, HBM],
+        in_specs=[HBM, HBM],
         out_specs=VMEM,
         scratch_shapes=[
             pltpu.VMEM((8, 128), jnp.int32),
@@ -439,29 +441,29 @@
             pltpu.SemaphoreType.DMA((2,)),
         ],
         compiler_params=pltpu.CompilerParams(vmem_limit_bytes=62 * 1024 * 1024),
-    )(copy.reshape(1), piece_ids.reshape(8, 128), point_counts)
+    )(piece_ids.reshape(8, 128), point_counts)
     got = exchange(sent.reshape(320, 1, 128), ("z", "x_high")).reshape(320, 128)
     got = lax.all_gather(got, "core", axis=0, tiled=True)
     grid = pl.pallas_call(
         place_kernel,
         out_shape=jax.ShapeDtypeStruct((1152, 128), jnp.float32),
-        in_specs=[SMEM, SMEM, VMEM],
+        in_specs=[VMEM, VMEM],
         out_specs=VMEM,
         compiler_params=PARAMS,
-    )(core.reshape(1), traits, got)
+    )(nodes, got)
     grid = exchange(grid.reshape(1152, 1, 128), ("x_low", "y")).reshape(1152, 128)
     sent = pl.pallas_call(
         fill_kernel,
         out_shape=jax.ShapeDtypeStruct((1536, 128), jnp.float32),
-        in_specs=[SMEM] + [VMEM] * 6,
+        in_specs=[VMEM] * 5,
         out_specs=VMEM,
         scratch_shapes=[
             pltpu.VMEM((40, 128), jnp.float32),
             pltpu.VMEM((48, PLANES * ROWS * 128), jnp.float32),
-            pltpu.VMEM((1536, 256), jnp.float32),
+            pltpu.VMEM((768, 256), jnp.float32),
         ],
         compiler_params=PARAMS,
-    )(jnp.stack([base, side]), nodes, grid, first, turn_one, second[0], second[1])
+    )(nodes, grid, first, turn_one, second)
     got = exchange(
         sent.reshape(1536, 1, 128), ("z", "x_high", "x_low", "core", "y")
     ).reshape(1536, 128)
@@ -472,7 +474,6 @@
         in_specs=[VMEM] * 4,
         out_specs=(HBM, HBM),
         scratch_shapes=[
-            pltpu.VMEM((1024, 256), jnp.float32),
             pltpu.VMEM((1024, 256), jnp.float32),
             pltpu.VMEM((PLANES, 8, LENGTH), jnp.float32),
             pltpu.VMEM((PLANES, 8, LENGTH), jnp.float32),

time: 122 us -> 120 us (0.984)
  blocking collectives: 63.8 us -> 77.6 us
  waiting for transfers between devices: 20.4 us -> 11.8 us
  starting transfers between devices: 22.9 us -> 18.5 us
  Pallas kernels: 9.28 us -> 7.07 us
  other arithmetic: 1.41 us -> 0 us
  local copies, waits for them, and re-layouts: 1.32 us -> 2.71 us
    all_to_all x1 -> x2, blocking collectives: 58.5 us -> 72.3 us  [exchange(): return lax.all_to_all(values, axes, split_axis=0, concat_axis=0, tiled=True)]
    all_to_all x2 -> x1, waiting for transfers between devices: 20.4 us -> 11.8 us  [exchange(): return lax.all_to_all(values, axes, split_axis=0, concat_axis=0, tiled=True)]
    all_to_all x2 -> x1, starting transfers between devices: 22.9 us -> 18.5 us  [exchange(): return lax.all_to_all(values, axes, split_axis=0, concat_axis=0, tiled=True)]
    pallas_call x1, Pallas kernels: 1.79 us -> 0.45 us  [shards(): pl.pallas_call(place_kernel, out_shape=jax.ShapeDtypeStruct((1152, 128),...]
    concatenate x0 -> x1, local copies, waits for them, and re-layouts: none -> 1.34 us  [shards(): jnp.concatenate([wavenumber, strength, displacement[0], displacement[1],...]
    concatenate x1 -> x0, other arithmetic: 1.26 us -> none  [shards(): jnp.concatenate([wavenumber, strength, displacement[0], displacement[1]])]
  transfers between devices with their start and end apart: 2 -> 1, of which waited for: 2 -> 1; matrix products, arithmetic and copies ran while one was open for 2% -> 2% of each run, Pallas kernels for 0% -> 0%
where the time goes in v3:
time: 120 us
  blocking collectives  77.6 us (65%)
  starting transfers between devices  18.5 us (15%)
  waiting for transfers between devices  11.8 us (10%)
  Pallas kernels  7.07 us (6%)
  local copies, waits for them, and re-layouts  2.71 us (2%)
  between operations  2.04 us (2%)
    all_to_all x2, blocking collectives, exchange(): return lax.all_to_all(values, axes, split_axis=0, concat_axis=0, tiled=True)  72.3 us
    all_to_all x1, starting transfers between devices, exchange(): return lax.all_to_all(values, axes, split_axis=0, concat_axis=0, tiled=True)  18.5 us
    all_to_all x1, waiting for transfers between devices, exchange(): return lax.all_to_all(values, axes, split_axis=0, concat_axis=0, tiled=True)  11.8 us
    all_gather x1, blocking collectives, shards(): got = lax.all_gather(got, 'core', axis=0, tiled=True)  5.29 us
  transfers between devices with their start and end apart: 1, of which 1 were waited for; matrix products, arithmetic and copies ran while one was open for 2% of the time, Pallas kernels for 0%

profile of v3, /device:TPU:1, one launch (start us, length us, event | category | flops | bytes accessed | tf_op | source)
XLA Modules:
  0.0 119.7 jit_solution(12478359052356660734)
XLA Ops:
  0.6 2.4 %shard_map.140 = f32[320,128]{1,0:T(8,128)} custom-call(s32[8,128]{1,0:T(8,128)} %bitcast.30, s32[1024,128]{1,0:T(8,128)} %counts_hbm.1), custom_call_target="tpu_custom_call" | custom-call | tf_op jit(solution)/shard_map/pallas_call | solution.py:433
  3.0 18.5 %all-to-all-start = ((f32[320,1,128]{2,1,0:T(1,128)}), f32[320,1,128]{2,1,0:T(1,128)S(1)}, u32[]{:S(2)}, u32[]{:S(2)}) async-start(f32[320,1,128]{2,1,0:T(1,128)} %bitcast.29), calls=%async_computation | async-start | bytes 327680 | tf_op jit(solution)/shard_map/all_to_all | solution.py:411
  22.2 0.0 copy-start.5
  22.9 0.0 copy-done.5
  22.9 0.0 copy-start.6
  22.9 0.6 fusion
  23.5 0.1 copy-done.6
  23.6 0.6 copy-done.7
  24.2 1.3 %concatenate.3 = f32[128]{0:T(128)S(1)} concatenate(f32[1]{0:T(128)S(6)} %copy.19, f32[1]{0:T(128)S(6)} %copy.20, f32[1]{0:T(128)} %bitcast, f32[1]{0:T(128)} %bitcast.1, f32[12]{0:T(128)S(1)} %broadcast.3, f32[15]{0:T(128)S(1)} %get-tuple-element.3, f32[1]{0:T(128)} %constant.5.clone.1, f32[15]{0:T(128)S(1)} %get-tuple-element.2, f32[1]{0:T(128)} %constant.5.clone.1, ...), dimensions={0} | concatenate | bytes 1024 | tf_op jit(solution)/shard_map/concatenate | solution.py:418
  25.6 11.8 %all-to-all-done = f32[320,1,128]{2,1,0:T(1,128)S(1)} async-done(((f32[320,1,128]{2,1,0:T(1,128)}), f32[320,1,128]{2,1,0:T(1,128)S(1)}, u32[]{:S(2)}, u32[]{:S(2)}) %all-to-all-start) | async-done | bytes 163872 | tf_op jit(solution)/shard_map/all_to_all | solution.py:411
  37.3 5.3 %all-gather = f32[640,1,128]{2,0,1:T(8,128)S(1)} all-gather(f32[320,1,128]{2,0,1:T(8,128)S(1)} %bitcast.28), channel_id=2, replica_groups=mesh['z'=16,'x_high'=2,'x_low'=2,'core'=2,'y'=4] {'core'}, dimensions={0}, use_global_device_ids=true | all-gather | bytes 491520 | tf_op jit(solution)/shard_map/all_gather | solution.py:446
  42.6 0.4 shard_map.141
  43.1 0.0 copy-start
  43.1 0.0 copy-start.3
  43.1 0.0 copy-start.4
  43.1 14.3 %all_to_all.15 = f32[1152,1,128]{2,1,0:T(1,128)S(1)} all-to-all(f32[1152,1,128]{2,1,0:T(1,128)S(1)} %bitcast.24), channel_id=1, replica_groups=mesh['z'=16,'x_high'=2,'x_low'=2,'core'=2,'y'=4] {'x_low','y'}, dimensions={0} | all-to-all | bytes 1179648 | tf_op jit(solution)/shard_map/all_to_all | solution.py:411
  57.4 0.0 copy-done
  57.4 0.0 copy-done.3
  57.4 2.2 %shard_map.142 = f32[1536,128]{1,0:T(8,128)S(1)} custom-call(f32[1,128]{1,0:T(1,128)S(1)} %bitcast.27, f32[1152,128]{1,0:T(8,128)S(1)} %bitcast.23, bf16[64,144]{1,0:T(8,128)(2,1)S(1)} %copy-done.4, f32[64,128]{1,0:T(8,128)S(1)} %copy-done.3, bf16[512,256]{1,0:T(8,128)(2,1)S(1)} %copy-done), custom_call_target="tpu_custom_call" | custom-call | tf_op jit(solution)/shard_map/pallas_call | solution.py:455
  59.6 0.0 copy-start.1
  59.6 0.0 copy-start.2
  59.6 58.0 %all_to_all.16 = f32[1536,1,128]{2,1,0:T(1,128)S(1)} all-to-all(f32[1536,1,128]{2,1,0:T(1,128)S(1)} %bitcast.22), channel_id=1, replica_groups=mesh['z'=16,'x_high'=2,'x_low'=2,'core'=2,'y'=4] {'z','x_high','x_low','..., dimensions={0} | all-to-all | bytes 1572864 | tf_op jit(solution)/shard_map/all_to_all | solution.py:411
  117.6 0.0 copy-done.1
  117.6 2.0 %shard_map.143 = (f32[4,8,4096]{2,1,0:T(8,128)}, f32[4,8,4096]{2,1,0:T(8,128)}) custom-call(f32[1536,128]{1,0:T(8,128)S(1)} %bitcast.21, bf16[256,256]{1,0:T(8,128)(2,1)S(1)} %copy-done.2, bf16[256,256]{1,0:T(8,128)(2,1)S(1)} %copy-done.1, f32[64,128]{1,0:T(8,128)S(1)} %copy-done.3), custom_call_target="tpu_custom_call" | custom-call | tf_op jit(solution)/shard_map/pallas_call | solution.py:471
  (6 shorter events, 0.0 us)
Async XLA Ops:
  3.0 34.3 %all-to-all-start = ((f32[320,1,128]{2,1,0:T(1,128)}), f32[320,1,128]{2,1,0:T(1,128)S(1)}, u32[]{:S(2)}, u32[]{:S(2)}) async-start(f32[320,1,128]{2,1,0:T(1,128)} %bitcast.29), calls=%async_computation | async-start | bytes 327680 | tf_op jit(solution)/shard_map/all_to_all | solution.py:411
  22.2 0.7 copy-start.5
  22.9 0.7 copy-start.6
  23.6 0.7 copy-start.7
  43.1 14.3 %copy-start = (bf16[512,256]{1,0:T(8,128)(2,1)S(1)}, bf16[512,256]{1,0:T(8,128)(2,1)}, u32[]{:S(2)}) copy-start(bf16[512,256]{1,0:T(8,128)(2,1)} %constant.17.clone.second_ref) | copy-start | bytes 786436
  43.1 14.3 %copy-start.3 = (f32[64,128]{1,0:T(8,128)S(1)}, f32[64,128]{1,0:T(8,128)}, u32[]{:S(2)}) copy-start(f32[64,128]{1,0:T(8,128)} %constant.16.clone.turn_ref) | copy-start | bytes 98308
  43.1 14.3 %copy-start.4 = (bf16[64,144]{1,0:T(8,128)(2,1)S(1)}, bf16[64,144]{1,0:T(8,128)(2,1)}, u32[]{:S(2)}) copy-start(bf16[64,144]{1,0:T(8,128)(2,1)} %constant.6.clone.first_ref) | copy-start | bytes 55300
  59.6 58.0 %copy-start.1 = (bf16[256,256]{1,0:T(8,128)(2,1)S(1)}, bf16[256,256]{1,0:T(8,128)(2,1)}, u32[]{:S(2)}) copy-start(bf16[256,256]{1,0:T(8,128)(2,1)} %constant.19.clone.low_ref) | copy-start | bytes 393220
  59.6 58.0 %copy-start.2 = (bf16[256,256]{1,0:T(8,128)(2,1)S(1)}, bf16[256,256]{1,0:T(8,128)(2,1)}, u32[]{:S(2)}) copy-start(bf16[256,256]{1,0:T(8,128)(2,1)} %constant.18.clone.high_ref) | copy-start | bytes 393220

commit v4 on v3

--- a/solution.py
+++ b/solution.py
@@ -13,7 +13,7 @@
 NODES = 15
 FAR = 3
 HEIGHT_SQ = 0.0625
-SHARED = 3
+RANKS = 12
 LIVE_BLOCKS = 24
 HALF = 1536
 ROWS = 6
@@ -58,7 +58,9 @@
     cos, sin = np.cos(angle), np.sin(angle)
     second = np.concatenate([np.concatenate([cos, sin], 1), np.concatenate([-sin, cos], 1)], 0)
     second = np.concatenate(split_np(second / 64.0), 0)
-    c = np.arange(96)
+    j, z = np.arange(4)[:, None], np.arange(16)[None, :]
+    whole = ((z & 1) * 32 + (z >> 1) * 4 + j).reshape(64)
+    c = np.concatenate([whole, (64 + z[:, :8] * 4 + j).reshape(32)])
     angle = 2.0 * np.pi * (((c[:, None] - 48) * t[None, :]) % 128) / 128
     third = np.zeros((2, 128, 2, 128))
     third[0, :96, 0] = np.cos(angle)
@@ -89,42 +91,43 @@
     return high, low
 
 
-def sort_kernel(ids_hbm, counts_hbm, out_ref, ids_ref, counts_ref, sem):
+def sort_kernel(ids_hbm, counts_hbm, out_ref, mark_ref, ids_ref, counts_ref, sem):
     ids_copy = pltpu.make_async_copy(ids_hbm, ids_ref, sem.at[0])
     ids_copy.start()
     counts_copy = pltpu.make_async_copy(counts_hbm, counts_ref, sem.at[1])
     counts_copy.start()
-    base = (lax.axis_index("y") * SHARED).astype(jnp.float32)
-    live = iota((96, 128), 0)
+    mark_ref[...] = jnp.zeros((8, 128), jnp.float32)
+    group = lax.axis_index("y")
+    seat = iota((32, 128), 0)
     lane = iota((128, 128), 1)
     prefix = jnp.concatenate(
         [as_mask(iota((128, 128), 0) < lane), jnp.ones((128, 128), jnp.bfloat16)], 1
     )
     ids_copy.wait()
     ids = ids_ref[...]
+    local = ids & 1023
     block = ((ids >> 10) + 48) & 127
-    part = block >> 4
-    side = jnp.where(part < 3, 0, 1)
-    target = (part - 3 * side) * 32 + ((block & 15) << 1) + side
-    target = jnp.where(part < ROWS, target, block)
-    here = [live == target[k : k + 1, :] for k in range(8)]
+    role = block >> 5
+    low_bit = jnp.where(role == 2, local >> 9, role)
+    target = ((block >> 2) & 7) * 2 + low_bit + jnp.where(role == 2, 16, 0)
+    target = jnp.where(((block & 3) == group) & (role < 3), target, -1)
+    here = [seat == target[k : k + 1, :] for k in range(8)]
     sums = dot(jnp.concatenate([as_mask(mask) for mask in here], 0), prefix)
-    local = ids & 1023
     high = ((local >> 5) + 1).astype(jnp.float32)
     low = (local & 31).astype(jnp.float32)
     pad = jnp.zeros((112, 128), jnp.float32)
     named = jnp.concatenate([high, low, pad], 0).T
-    running = jnp.zeros((96, 128), jnp.float32) - base
+    running = jnp.zeros((32, 128), jnp.float32)
     chosen = []
     for k in range(8):
-        rows = slice(k * 96, (k + 1) * 96)
+        rows = slice(k * 32, (k + 1) * 32)
         rank = running + sums[rows, :128]
         running = running + sums[rows, 128:]
         chosen.append(
-            jnp.concatenate([as_mask(here[k] & (rank == float(s))) for s in range(SHARED)], 0)
+            jnp.concatenate([as_mask(here[k] & (rank == float(s))) for s in range(RANKS)], 0)
         )
     counts_copy.wait()
-    picked = jnp.zeros((SHARED * 96, 256), jnp.float32)
+    picked = jnp.zeros((RANKS * 32, 256), jnp.float32)
     for k in range(0, 8, 2):
         rows = []
         for m in (k, k + 1):
@@ -136,45 +139,39 @@
         picked = picked + dot(
             jnp.concatenate([chosen[k], chosen[k + 1]], 1), jnp.concatenate(rows, 0)
         )
-    names = jnp.zeros((32, 128), jnp.float32)
-    for i in range(3):
-        for s in range(SHARED):
-            rows = slice(s * 96 + i * 32, s * 96 + i * 32 + 32)
-            out_ref[pl.ds(i * SHARED + s, 32, stride=10), :] = picked[rows, :128]
+    names = jnp.zeros((16, 128), jnp.float32)
+    for kind in range(2):
+        for s in range(RANKS):
+            rows = slice(s * 32 + kind * 16, s * 32 + kind * 16 + 16)
+            out_ref[pl.ds(kind * RANKS + s, 16, stride=25), :] = picked[rows, :128]
             name = picked[rows, 128:129] * 32.0 + picked[rows, 129:130]
-            names = jnp.where(lane[:32] == i * SHARED + s, name, names)
-    out_ref[pl.ds(9, 32, stride=10), :] = names
-
-
-def place_kernel(traits_ref, got_ref, out_ref):
-    core = lax.axis_index("core")
-    traits = [traits_ref[0:1, m : m + 1] for m in range(4)]
-    names = got_ref[pl.ds(9, 64, stride=10), :]
-    names = jnp.concatenate([names, pltpu.roll(names, 127, 1)], 0).T
-    cell = iota((384, 128), 0)
-    row = iota((48, 128), 0)
-    first_lane = iota((48, 128), 1) == 0
-    for i in range(3):
+            names = jnp.where(lane[:16] == kind * RANKS + s, name, names)
+    out_ref[pl.ds(24, 16, stride=25), :] = names
+
+
+def place_kernel(nodes_ref, got_ref, out_ref):
+    names = got_ref[pl.ds(24, 16, stride=25), :]
+    names = [names] + [pltpu.roll(names, 128 - s, 1) for s in range(1, 8)]
+    names = jnp.concatenate(names, 0).T
+    for kind, cells, start, stop in ((0, 768, 0, 96), (1, 384, 96, 144)):
+        cell = iota((cells, 128), 0)
         masks, counts = [], []
-        for s, width in ((0, 128), (2, 64)):
-            name = names[i * SHARED + s : i * SHARED + s + 1, :width].astype(jnp.int32)
-            line = (name >> 5) - 1
+        for s, width in ((0, 128), (8, 64)):
+            at = kind * RANKS + s
+            name = names[at : at + 1, :width].astype(jnp.int32)
             column = ((name & 31) + 12) & 31
-            valid = (name > 0) & (column < LIVE_BLOCKS) & (((line >> 3) & 1) == core)
-            seat = (line >> 4) * 4 + ((line >> 1) & 3)
-            key = jnp.where(valid, seat * 48 + (line & 1) * 24 + column, -1)
+            line = ((name >> 5) - 1) & (31 if kind == 0 else 15)
+            key = jnp.where(
+                (name > 0) & (column < LIVE_BLOCKS), line * LIVE_BLOCKS + column, -1
+            )
             masks.append(as_mask(cell[:, :width] == key))
-        for s in range(SHARED):
-            counts.append(got_ref[pl.ds(i * SHARED + s, 64, stride=10), :].astype(jnp.bfloat16))
+        for s in range(RANKS):
+            rows = got_ref[pl.ds(kind * RANKS + s, 16, stride=25), :]
+            counts.append(rows.astype(jnp.bfloat16))
         grid = dot(jnp.concatenate(masks, 1), jnp.concatenate(counts, 0))
-        extra = jnp.zeros((48, 128), jnp.float32)
-        if i < 2:
-            for m in range(2):
-                extra = jnp.where(first_lane & (row == m * 24), traits[i * 2 + m], extra)
+        size = stop - start
         for d in range(8):
-            out_ref[d * 144 + i * 48 : d * 144 + i * 48 + 48, :] = (
-                grid[d * 48 : d * 48 + 48] + extra
-            )
+            out_ref[d * 144 + start : d * 144 + stop, :] = grid[d * size : (d + 1) * size]
 
 
 def evaluate(square, wave, strength, weight):
@@ -203,40 +200,37 @@
     fill_ref,
     turned_ref,
 ):
-    side = lax.axis_index("x_high")
-    seat = (lax.axis_index("x_low") * 2 + lax.axis_index("core")) * 4 + lax.axis_index("y")
-    base = lax.axis_index("z") * 32 + (side - 1) * HALF + seat * 2
-    right = side == 1
+    z, group = lax.axis_index("z"), lax.axis_index("y")
+    seat = lax.axis_index("x") * 2 + lax.axis_index("core")
+    cluster = (z >> 1) * 4 + group
+    base = ((z & 1) * 32 + cluster) * 32 + seat * 4 - HALF
+    base_split = (64 + cluster) * 32 + (z & 1) * 16 + seat * 2 - HALF
     column = (
         iota((LIVE_BLOCKS, 128), 0) * 128 + iota((LIVE_BLOCKS, 128), 1) - HALF
     ).astype(jnp.float32)
-    traits = [
-        [got_ref[p * 144 + e * 24 : p * 144 + e * 24 + 1, 0:1] for e in range(4)]
-        for p in range(PLANES)
-    ]
+    traits = [[nodes_ref[p : p + 1, e : e + 1] for e in range(4)] for p in range(PLANES)]
     counts = []
     for b in range(ROWS):
         parts = [got_ref[m * 144 + b * 24 : m * 144 + b * 24 + 24, :] for m in range(8)]
         while len(parts) > 1:
             parts = [parts[m] + parts[m + 1] for m in range(0, len(parts), 2)]
-        counts.append(jnp.where(column > -float(HALF), parts[0], 0.0))
-    lane = iota((8, 128), 1)
+        counts.append(parts[0])
+    lane = iota((16, 128), 1)
     inner = lane < 64
-    for m in range(2):
-        pair = jnp.where(right, counts[m][11:13], counts[4 + m][11:13])
+    for m in range(4):
+        pair = counts[m][11:13]
         merged = jnp.where(inner[0:1], pair[1:2], pair[0:1])
         for p in range(PLANES):
-            near_ref[p * 2 + m : p * 2 + m + 1, :] = merged
+            near_ref[p * 4 + m : p * 4 + m + 1, :] = merged
     for p in range(PLANES):
         for e in range(4):
-            at = 8 + e * 8 + p * 2
-            near_ref[at : at + 2, :] = jnp.broadcast_to(traits[p][e], (2, 128))
-    near_counts = near_ref[0:8, :]
-    near_row = (base + jnp.where(right, 0, 1024) + (iota((8, 128), 0) & 1)).astype(jnp.float32)
-    near_row = near_row + near_ref[24:32, :]
-    near_col = jnp.where(inner, lane, lane - 128).astype(jnp.float32) + near_ref[32:40, :]
-    near_wave = near_ref[8:16, :] * (0.5 / math.pi)
-    near_strength = near_ref[16:24, :]
+            at = 16 + e * 16 + p * 4
+            near_ref[at : at + 4, :] = jnp.broadcast_to(traits[p][e], (4, 128))
+    near_counts = near_ref[0:16, :]
+    near_row = (base + (iota((16, 128), 0) & 3)).astype(jnp.float32) + near_ref[48:64, :]
+    near_col = jnp.where(inner, lane, lane - 128).astype(jnp.float32) + near_ref[64:80, :]
+    near_wave = near_ref[16:32, :] * (0.5 / math.pi)
+    near_strength = near_ref[32:48, :]
     node_row = [nodes_ref[0:1, 16 + q : 17 + q] for q in range(NODES)]
     node_col = [nodes_ref[0:1, 32 + q : 33 + q] for q in range(NODES)]
     node_weight = [nodes_ref[0:1, 48 + q : 49 + q] for q in range(NODES)]
@@ -244,8 +238,8 @@
         [jnp.where(counts[b] > float(q), node_weight[q], 0.0) for q in range(FAR)]
         for b in range(ROWS)
     ]
-    extra_real = jnp.zeros((8, 128), jnp.float32)
-    extra_imag = jnp.zeros((8, 128), jnp.float32)
+    extra_real = jnp.zeros((16, 128), jnp.float32)
+    extra_imag = jnp.zeros((16, 128), jnp.float32)
     for q in range(FAR, NODES):
         row_pos = near_row + node_row[q]
         col_pos = near_col + node_col[q]
@@ -266,7 +260,7 @@
             col_pos = col_base + node_col[q]
             col_sq.append(col_pos * col_pos)
         for b in range(ROWS):
-            row_offset = (base + (512 * (b // 2) + b % 2)).astype(jnp.float32)
+            row_offset = (base + b if b < 4 else base_split + (b - 4)).astype(jnp.float32)
             total_real = jnp.zeros((LIVE_BLOCKS, 128), jnp.float32)
             total_imag = jnp.zeros((LIVE_BLOCKS, 128), jnp.float32)
             for q in range(FAR):
@@ -278,15 +272,13 @@
             lanes = slice((p * ROWS + b) * 128, (p * ROWS + b) * 128 + 128)
             fill_ref[0:24, lanes] = total_real
             fill_ref[24:48, lanes] = -total_imag
-            if b // 2 != 1:
-                use = right if b // 2 == 0 else jnp.logical_not(right)
-                use = use & inner_pair
-                m = p * 2 + b % 2
+            if b < 4:
+                m = p * 4 + b
                 fill_ref[11:13, lanes] = fill_ref[11:13, lanes] + jnp.where(
-                    use, extra_real[m : m + 1], 0.0
+                    inner_pair, extra_real[m : m + 1], 0.0
                 )
                 fill_ref[35:37, lanes] = fill_ref[35:37, lanes] - jnp.where(
-                    use, extra_imag[m : m + 1], 0.0
+                    inner_pair, extra_imag[m : m + 1], 0.0
                 )
         lanes = slice(p * ROWS * 128, (p + 1) * ROWS * 128)
         high, low = split(fill_ref[:, lanes])
@@ -362,9 +354,12 @@
     blank = jnp.zeros((32, 128), jnp.float32)
     for pair in range(16):
         parts = []
-        for side in range(2):
-            for k in range(3):
-                parts.append(got_ref[pl.ds((side * 16 + pair) * 3 + k, 16, stride=96), :])
+        for j in range(4):
+            at = ((pair >> 1) * 4 + j) * 3 + (pair & 1)
+            parts.append(got_ref[pl.ds(at, 16, stride=96), :])
+        for j in range(4):
+            at = ((pair >> 3) * 32 + (pair & 7) * 4 + j) * 3 + 2
+            parts.append(got_ref[pl.ds(at, 8, stride=192), :])
         flipped = jnp.concatenate(parts + [blank], 0).T
         for m in range(2):
             for ri in range(2):
@@ -415,6 +410,22 @@
     piece_ids, point_counts, wavenumber, strength, displacement, node_position, node_weights
 ):
     first, turn_one, second, third, turn_two = tables()
+    sent, mark = pl.pallas_call(
+        sort_kernel,
+        out_shape=(
+            jax.ShapeDtypeStruct((400, 128), jnp.float32),
+            jax.ShapeDtypeStruct((8, 128), jnp.float32),
+        ),
+        in_specs=[HBM, HBM],
+        out_specs=(VMEM, VMEM),
+        scratch_shapes=[
+            pltpu.VMEM((8, 128), jnp.int32),
+            pltpu.VMEM((1024, 128), jnp.int32),
+            pltpu.SemaphoreType.DMA((2,)),
+        ],
+        compiler_params=pltpu.CompilerParams(vmem_limit_bytes=62 * 1024 * 1024),
+    )(piece_ids.reshape(8, 128), point_counts)
+    got = exchange(sent.reshape(400, 1, 128), "z").reshape(400, 128)
     nodes = jnp.concatenate(
         [
             wavenumber,
@@ -429,21 +440,8 @@
             node_weights,
             jnp.zeros((65,), jnp.float32),
         ]
-    ).reshape(1, 128)
-    sent = pl.pallas_call(
-        sort_kernel,
-        out_shape=jax.ShapeDtypeStruct((320, 128), jnp.float32),
-        in_specs=[HBM, HBM],
-        out_specs=VMEM,
-        scratch_shapes=[
-            pltpu.VMEM((8, 128), jnp.int32),
-            pltpu.VMEM((1024, 128), jnp.int32),
-            pltpu.SemaphoreType.DMA((2,)),
-        ],
-        compiler_params=pltpu.CompilerParams(vmem_limit_bytes=62 * 1024 * 1024),
-    )(piece_ids.reshape(8, 128), point_counts)
-    got = exchange(sent.reshape(320, 1, 128), ("z", "x_high")).reshape(320, 128)
-    got = lax.all_gather(got, "core", axis=0, tiled=True)
+    ).reshape(1, 128) + mark[0:1]
+    nodes = lax.all_gather(nodes, "y", axis=0, tiled=True)
     grid = pl.pallas_call(
         place_kernel,
         out_shape=jax.ShapeDtypeStruct((1152, 128), jnp.float32),
@@ -451,21 +449,21 @@
         out_specs=VMEM,
         compiler_params=PARAMS,
     )(nodes, got)
-    grid = exchange(grid.reshape(1152, 1, 128), ("x_low", "y")).reshape(1152, 128)
+    grid = exchange(grid.reshape(1152, 1, 128), ("x", "core")).reshape(1152, 128)
     sent = pl.pallas_call(
         fill_kernel,
         out_shape=jax.ShapeDtypeStruct((1536, 128), jnp.float32),
         in_specs=[VMEM] * 5,
         out_specs=VMEM,
         scratch_shapes=[
-            pltpu.VMEM((40, 128), jnp.float32),
+            pltpu.VMEM((80, 128), jnp.float32),
             pltpu.VMEM((48, PLANES * ROWS * 128), jnp.float32),
             pltpu.VMEM((768, 256), jnp.float32),
         ],
         compiler_params=PARAMS,
     )(nodes, grid, first, turn_one, second)
     got = exchange(
-        sent.reshape(1536, 1, 128), ("z", "x_high", "x_low", "core", "y")
+        sent.reshape(1536, 1, 128), ("z", "x", "core", "y")
     ).reshape(1536, 128)
     shape = jax.ShapeDtypeStruct((PLANES, 8, LENGTH), jnp.float32)
     return pl.pallas_call(
@@ -484,9 +482,9 @@
 
 
 def solution(mesh):
-    every = ("z", "x_high", "x_low", "core", "y")
-    fine = Mesh(mesh.devices.reshape(16, 2, 2, 2, 4), every)
-    wide = every[:4]
+    every = ("z", "x", "core", "y")
+    fine = Mesh(mesh.devices.reshape(16, 4, 2, 4), every)
+    wide = every[:3]
     placed = (P(wide), P(wide, None), P("y"), P("y"), P(None, "y"), P(), P())
     return jax.shard_map(
         shards,

time: 120 us -> 118 us (0.983)
  waiting for transfers between devices: 11.8 us -> 0.01 us
  blocking collectives: 77.6 us -> 88.9 us
  starting transfers between devices: 18.5 us -> 15.8 us
    all_to_all x1, waiting for transfers between devices: 11.8 us -> 0.01 us  [exchange(): return lax.all_to_all(values, axes, split_axis=0, concat_axis=0, tiled=True)]
    all_to_all x2, blocking collectives: 72.3 us -> 80.4 us  [exchange(): return lax.all_to_all(values, axes, split_axis=0, concat_axis=0, tiled=True)]
    all_gather x1, blocking collectives: 5.29 us -> 8.48 us  [shards(): nodes = lax.all_gather(nodes, 'y', axis=0, tiled=True)]
    all_to_all x1, starting transfers between devices: 18.5 us -> 15.8 us  [exchange(): return lax.all_to_all(values, axes, split_axis=0, concat_axis=0, tiled=True)]
  transfers between devices with their start and end apart: 1 -> 1, of which waited for: 1 -> 0; matrix products, arithmetic and copies ran while one was open for 2% -> 2% of each run, Pallas kernels for 0% -> 0%
where the time goes in v4:
time: 118 us; the launch traced here: 117 us
  blocking collectives  88.9 us (75%)
  starting transfers between devices  15.8 us (13%)
  Pallas kernels  7.18 us (6%)
  local copies, waits for them, and re-layouts  2.64 us (2%)
  between operations  2.04 us (2%)
    all_to_all x2, blocking collectives, exchange(): return lax.all_to_all(values, axes, split_axis=0, concat_axis=0, tiled=True)  80.4 us
    all_to_all x1, starting transfers between devices, exchange(): return lax.all_to_all(values, axes, split_axis=0, concat_axis=0, tiled=True)  15.8 us
    all_gather x1, blocking collectives, shards(): nodes = lax.all_gather(nodes, 'y', axis=0, tiled=True)  8.48 us
    pallas_call x1, Pallas kernels, shards(): pl.pallas_call(sort_kernel, out_shape=(jax.ShapeDtypeStruct((400, 128), j...  2.4 us
  transfers between devices with their start and end apart: 1, of which 0 were waited for; matrix products, arithmetic and copies ran while one was open for 2% of the time, Pallas kernels for 0%

profile of v4, /device:TPU:1, one launch (start us, length us, event | category | flops | bytes accessed | tf_op | source)
XLA Modules:
  0.0 117.2 jit_solution(10537070508878486810)
XLA Ops:
  0.6 2.4 %shard_map.140 = (f32[400,128]{1,0:T(8,128)}, f32[8,128]{1,0:T(8,128)}) custom-call(s32[8,128]{1,0:T(8,128)} %bitcast.34, s32[1024,128]{1,0:T(8,128)} %counts_hbm.1), custom_call_target="tpu_custom_call" | custom-call | tf_op jit(solution)/shard_map/pallas_call | solution.py:413
  3.0 15.8 %all-to-all-start = ((f32[400,1,128]{2,1,0:T(1,128)}), f32[400,1,128]{2,1,0:T(1,128)S(1)}, u32[]{:S(2)}, u32[]{:S(2)}) async-start(f32[400,1,128]{2,1,0:T(1,128)} %bitcast.33), calls=%async_computation | async-start | bytes 409600 | tf_op jit(solution)/shard_map/all_to_all | solution.py:406
  19.4 0.0 copy-start.5
  20.1 0.0 copy-done.5
  20.1 0.0 copy-start.6
  20.1 0.6 fusion.1
  20.7 0.1 copy-done.6
  20.8 0.6 copy-done.7
  21.5 1.3 %concatenate.3 = f32[128]{0:T(128)S(1)} concatenate(f32[1]{0:T(128)S(6)} %copy.19, f32[1]{0:T(128)S(6)} %copy.20, f32[1]{0:T(128)} %bitcast, f32[1]{0:T(128)} %bitcast.1, f32[12]{0:T(128)S(1)} %broadcast.3, f32[15]{0:T(128)S(1)} %get-tuple-element.7, f32[1]{0:T(128)} %constant.5.clone.1, f32[15]{0:T(128)S(1)} %get-tuple-element.6, f32[1]{0:T(128)} %constant.5.clone.1, ...), dimensions={0} | concatenate | bytes 1024 | tf_op jit(solution)/shard_map/concatenate | solution.py:429
  22.7 0.7 fusion
  23.4 8.5 %all-gather = f32[4,1,128]{2,1,0:T(1,128)S(1)} all-gather(f32[1,1,128]{2,1,0:T(1,128)S(1)} %fusion), channel_id=1, replica_groups=mesh['z'=16,'x'=4,'core'=2,'y'=4] {'y'}, dimensions={0}, use_global_device_ids=true | all-gather | bytes 2560 | tf_op jit(solution)/shard_map/all_gather | solution.py:444
  31.9 0.0 all-to-all-done
  31.9 0.4 shard_map.141
  32.4 0.0 copy-start
  32.4 0.0 copy-start.3
  32.4 0.0 copy-start.4
  32.4 19.1 %all_to_all.15 = f32[1152,1,128]{2,1,0:T(1,128)S(1)} all-to-all(f32[1152,1,128]{2,1,0:T(1,128)S(1)} %bitcast.28), channel_id=1, replica_groups=mesh['z'=16,'x'=4,'core'=2,'y'=4] {'x','core'}, dimensions={0} | all-to-all | bytes 1179648 | tf_op jit(solution)/shard_map/all_to_all | solution.py:406
  51.5 0.0 copy-done
  51.5 2.3 %shard_map.142 = f32[1536,128]{1,0:T(8,128)S(1)} custom-call(f32[4,128]{1,0:T(4,128)S(1)} %bitcast.32, f32[1152,128]{1,0:T(8,128)S(1)} %bitcast.29, bf16[64,144]{1,0:T(8,128)(2,1)S(1)} %copy-done.4, f32[64,128]{1,0:T(8,128)S(1)} %copy-done.3, bf16[512,256]{1,0:T(8,128)(2,1)S(1)} %copy-done), custom_call_target="tpu_custom_call" | custom-call | tf_op jit(solution)/shard_map/pallas_call | solution.py:453
  53.8 0.0 copy-start.1
  53.8 0.0 copy-start.2
  53.8 61.3 %all_to_all.16 = f32[1536,1,128]{2,1,0:T(1,128)S(1)} all-to-all(f32[1536,1,128]{2,1,0:T(1,128)S(1)} %bitcast.27), channel_id=1, replica_groups=mesh['z'=16,'x'=4,'core'=2,'y'=4] {'z','x','core','y'}, dimensions={0} | all-to-all | bytes 1572864 | tf_op jit(solution)/shard_map/all_to_all | solution.py:406
  115.2 0.0 copy-done.2
  115.2 2.0 %shard_map.143 = (f32[4,8,4096]{2,1,0:T(8,128)}, f32[4,8,4096]{2,1,0:T(8,128)}) custom-call(f32[1536,128]{1,0:T(8,128)S(1)} %bitcast.26, bf16[256,256]{1,0:T(8,128)(2,1)S(1)} %copy-done.2, bf16[256,256]{1,0:T(8,128)(2,1)S(1)} %copy-done.1, f32[64,128]{1,0:T(8,128)S(1)} %copy-done.3), custom_call_target="tpu_custom_call" | custom-call | tf_op jit(solution)/shard_map/pallas_call | solution.py:469
  (7 shorter events, 0.0 us)
Async XLA Ops:
  3.0 28.9 %all-to-all-start = ((f32[400,1,128]{2,1,0:T(1,128)}), f32[400,1,128]{2,1,0:T(1,128)S(1)}, u32[]{:S(2)}, u32[]{:S(2)}) async-start(f32[400,1,128]{2,1,0:T(1,128)} %bitcast.33), calls=%async_computation | async-start | bytes 409600 | tf_op jit(solution)/shard_map/all_to_all | solution.py:406
  19.4 0.7 copy-start.5
  20.1 0.7 copy-start.6
  20.8 0.7 copy-start.7
  32.4 19.1 %copy-start = (bf16[512,256]{1,0:T(8,128)(2,1)S(1)}, bf16[512,256]{1,0:T(8,128)(2,1)}, u32[]{:S(2)}) copy-start(bf16[512,256]{1,0:T(8,128)(2,1)} %constant.17.clone.second_ref) | copy-start | bytes 786436
  32.4 19.1 %copy-start.3 = (f32[64,128]{1,0:T(8,128)S(1)}, f32[64,128]{1,0:T(8,128)}, u32[]{:S(2)}) copy-start(f32[64,128]{1,0:T(8,128)} %constant.16.clone.turn_ref) | copy-start | bytes 98308
  32.4 19.1 %copy-start.4 = (bf16[64,144]{1,0:T(8,128)(2,1)S(1)}, bf16[64,144]{1,0:T(8,128)(2,1)}, u32[]{:S(2)}) copy-start(bf16[64,144]{1,0:T(8,128)(2,1)} %constant.6.clone.first_ref) | copy-start | bytes 55300
  53.8 61.4 %copy-start.1 = (bf16[256,256]{1,0:T(8,128)(2,1)S(1)}, bf16[256,256]{1,0:T(8,128)(2,1)}, u32[]{:S(2)}) copy-start(bf16[256,256]{1,0:T(8,128)(2,1)} %constant.19.clone.low_ref) | copy-start | bytes 393220
  53.8 61.4 %copy-start.2 = (bf16[256,256]{1,0:T(8,128)(2,1)S(1)}, bf16[256,256]{1,0:T(8,128)(2,1)}, u32[]{:S(2)}) copy-start(bf16[256,256]{1,0:T(8,128)(2,1)} %constant.18.clone.high_ref) | copy-start | bytes 393220

commit v5 on v4

--- a/solution.py
+++ b/solution.py
@@ -147,6 +147,20 @@
             name = picked[rows, 128:129] * 32.0 + picked[rows, 129:130]
             names = jnp.where(lane[:16] == kind * RANKS + s, name, names)
     out_ref[pl.ds(24, 16, stride=25), :] = names
+
+
+def traits_kernel(
+    wave_ref, strength_ref, shift_ref, position_ref, weight_ref, mark_ref, out_ref
+):
+    lane = iota((1, 128), 1)
+    row = mark_ref[0:1, :]
+    for m, value in enumerate((wave_ref[0], strength_ref[0], shift_ref[0, 0], shift_ref[1, 0])):
+        row = jnp.where(lane == m, value, row)
+    for q in range(NODES):
+        row = jnp.where(lane == 16 + q, position_ref[0, q], row)
+        row = jnp.where(lane == 32 + q, position_ref[1, q], row)
+        row = jnp.where(lane == 48 + q, weight_ref[q], row)
+    out_ref[...] = row
 
 
 def place_kernel(nodes_ref, got_ref, out_ref):
@@ -426,21 +440,13 @@
         compiler_params=pltpu.CompilerParams(vmem_limit_bytes=62 * 1024 * 1024),
     )(piece_ids.reshape(8, 128), point_counts)
     got = exchange(sent.reshape(400, 1, 128), "z").reshape(400, 128)
-    nodes = jnp.concatenate(
-        [
-            wavenumber,
-            strength,
-            displacement[0],
-            displacement[1],
-            jnp.zeros((12,), jnp.float32),
-            node_position[0],
-            jnp.zeros((1,), jnp.float32),
-            node_position[1],
-            jnp.zeros((1,), jnp.float32),
-            node_weights,
-            jnp.zeros((65,), jnp.float32),
-        ]
-    ).reshape(1, 128) + mark[0:1]
+    nodes = pl.pallas_call(
+        traits_kernel,
+        out_shape=jax.ShapeDtypeStruct((1, 128), jnp.float32),
+        in_specs=[SMEM] * 5 + [VMEM],
+        out_specs=VMEM,
+        compiler_params=PARAMS,
+    )(wavenumber, strength, displacement, node_position, node_weights, mark)
     nodes = lax.all_gather(nodes, "y", axis=0, tiled=True)
     grid = pl.pallas_call(
         place_kernel,

time: 118 us -> 116 us (0.983)
  local copies, waits for them, and re-layouts: 2.64 us -> 0.82 us
  blocking collectives: 88.9 us -> 87.5 us
  waiting for transfers between devices: 0.01 us -> 1.36 us
    all_to_all x2, blocking collectives: 80.4 us -> 79 us  [exchange(): return lax.all_to_all(values, axes, split_axis=0, concat_axis=0, tiled=True)]
    all_to_all x1, waiting for transfers between devices: 0.01 us -> 1.36 us  [exchange(): return lax.all_to_all(values, axes, split_axis=0, concat_axis=0, tiled=True)]
    concatenate x1 -> x0, local copies, waits for them, and re-layouts: 1.27 us -> none  [shards(): jnp.concatenate([wavenumber, strength, displacement[0], displacement[1],...]
  transfers between devices with their start and end apart: 1 -> 1, of which waited for: 0 -> 1; matrix products, arithmetic and copies ran while one was open for 2% -> 0% of each run, Pallas kernels for 0% -> 1%
where the time goes in v5:
time: 116 us; the launch traced here: 115 us
  blocking collectives  87.5 us (75%)
  starting transfers between devices  15.8 us (14%)
  Pallas kernels  7.77 us (7%)
  between operations  2.05 us (2%)
  waiting for transfers between devices  1.36 us (1%)
    all_to_all x2, blocking collectives, exchange(): return lax.all_to_all(values, axes, split_axis=0, concat_axis=0, tiled=True)  79 us
    all_to_all x1, starting transfers between devices, exchange(): return lax.all_to_all(values, axes, split_axis=0, concat_axis=0, tiled=True)  15.8 us
    all_gather x1, blocking collectives, shards(): nodes = lax.all_gather(nodes, 'y', axis=0, tiled=True)  8.49 us
    pallas_call x1, Pallas kernels, shards(): pl.pallas_call(sort_kernel, out_shape=(jax.ShapeDtypeStruct((400, 128), j...  2.4 us
    pallas_call x1, Pallas kernels, shards(): pl.pallas_call(fill_kernel, out_shape=jax.ShapeDtypeStruct((1536, 128), j...  2.33 us
  transfers between devices with their start and end apart: 1, of which 1 were waited for; matrix products, arithmetic and copies ran while one was open for 0% of the time, Pallas kernels for 1%

profile of v5, /device:TPU:1, one launch (start us, length us, event | category | flops | bytes accessed | tf_op | source)
XLA Modules:
  0.0 115.3 jit_solution(14826177448700107223)
XLA Ops:
  0.6 2.4 %shard_map.140 = (f32[400,128]{1,0:T(8,128)}, f32[8,128]{1,0:T(8,128)}) custom-call(s32[8,128]{1,0:T(8,128)} %bitcast.24, s32[1024,128]{1,0:T(8,128)} %counts_hbm.1), custom_call_target="tpu_custom_call" | custom-call | tf_op jit(solution)/shard_map/pallas_call | solution.py:427
  3.0 0.0 copy-start.8
  3.0 15.8 %all-to-all-start = ((f32[400,1,128]{2,1,0:T(1,128)}), f32[400,1,128]{2,1,0:T(1,128)S(1)}, u32[]{:S(2)}, u32[]{:S(2)}) async-start(f32[400,1,128]{2,1,0:T(1,128)} %bitcast.23), calls=%async_computation | async-start | bytes 409600 | tf_op jit(solution)/shard_map/all_to_all | solution.py:420
  18.8 0.0 copy-start.5
  20.1 0.0 copy-done.8
  20.1 0.1 copy.17.shift_ref
  20.2 0.0 copy-done.5
  20.2 0.7 copy-done.6
  20.9 0.0 copy-done.7
  20.9 0.6 shard_map.141
  21.5 8.5 %all-gather = f32[4,1,128]{2,1,0:T(1,128)S(1)} all-gather(f32[1,1,128]{2,1,0:T(1,128)S(1)} %bitcast.22), channel_id=1, replica_groups=mesh['z'=16,'x'=4,'core'=2,'y'=4] {'y'}, dimensions={0}, use_global_device_ids=true | all-gather | bytes 2560 | tf_op jit(solution)/shard_map/all_gather | solution.py:450
  30.0 1.4 %all-to-all-done = f32[400,1,128]{2,1,0:T(1,128)S(1)} async-done(((f32[400,1,128]{2,1,0:T(1,128)}), f32[400,1,128]{2,1,0:T(1,128)S(1)}, u32[]{:S(2)}, u32[]{:S(2)}) %all-to-all-start) | async-done | bytes 204832 | tf_op jit(solution)/shard_map/all_to_all | solution.py:420
  31.4 0.4 shard_map.142
  31.8 0.0 copy-start
  31.8 0.0 copy-start.3
  31.8 0.0 copy-start.4
  31.8 19.6 %all_to_all.15 = f32[1152,1,128]{2,1,0:T(1,128)S(1)} all-to-all(f32[1152,1,128]{2,1,0:T(1,128)S(1)} %bitcast.17), channel_id=1, replica_groups=mesh['z'=16,'x'=4,'core'=2,'y'=4] {'x','core'}, dimensions={0} | all-to-all | bytes 1179648 | tf_op jit(solution)/shard_map/all_to_all | solution.py:420
  51.5 0.0 copy-done
  51.5 0.0 copy-done.3
  51.5 2.3 %shard_map.143 = f32[1536,128]{1,0:T(8,128)S(1)} custom-call(f32[4,128]{1,0:T(4,128)S(1)} %bitcast.21, f32[1152,128]{1,0:T(8,128)S(1)} %bitcast.18, bf16[64,144]{1,0:T(8,128)(2,1)S(1)} %copy-done.4, f32[64,128]{1,0:T(8,128)S(1)} %copy-done.3, bf16[512,256]{1,0:T(8,128)(2,1)S(1)} %copy-done), custom_call_target="tpu_custom_call" | custom-call | tf_op jit(solution)/shard_map/pallas_call | solution.py:459
  53.8 0.0 copy-start.1
  53.8 0.0 copy-start.2
  53.8 59.4 %all_to_all.16 = f32[1536,1,128]{2,1,0:T(1,128)S(1)} all-to-all(f32[1536,1,128]{2,1,0:T(1,128)S(1)} %bitcast.16), channel_id=1, replica_groups=mesh['z'=16,'x'=4,'core'=2,'y'=4] {'z','x','core','y'}, dimensions={0} | all-to-all | bytes 1572864 | tf_op jit(solution)/shard_map/all_to_all | solution.py:420
  113.3 2.0 %shard_map.144 = (f32[4,8,4096]{2,1,0:T(8,128)}, f32[4,8,4096]{2,1,0:T(8,128)}) custom-call(f32[1536,128]{1,0:T(8,128)S(1)} %bitcast.15, bf16[256,256]{1,0:T(8,128)(2,1)S(1)} %copy-done.2, bf16[256,256]{1,0:T(8,128)(2,1)S(1)} %copy-done.1, f32[64,128]{1,0:T(8,128)S(1)} %copy-done.3), custom_call_target="tpu_custom_call" | custom-call | tf_op jit(solution)/shard_map/pallas_call | solution.py:475
  (5 shorter events, 0.0 us)
Async XLA Ops:
  3.0 17.1 %copy-start.8 = (f32[2,1]{0,1:T(1,128)S(1)}, f32[2,1]{0,1:T(1,128)}, u32[]{:S(2)}) copy-start(f32[2,1]{0,1:T(1,128)} %param.17) | copy-start | bytes 28
  3.0 28.3 %all-to-all-start = ((f32[400,1,128]{2,1,0:T(1,128)}), f32[400,1,128]{2,1,0:T(1,128)S(1)}, u32[]{:S(2)}, u32[]{:S(2)}) async-start(f32[400,1,128]{2,1,0:T(1,128)} %bitcast.23), calls=%async_computation | async-start | bytes 409600 | tf_op jit(solution)/shard_map/all_to_all | solution.py:420
  18.8 1.4 %copy-start.5 = (f32[8,128]{1,0:T(8,128)S(1)}, f32[8,128]{1,0:T(8,128)}, u32[]{:S(2)}) copy-start(f32[8,128]{1,0:T(8,128)} %get-tuple-element.4.mark_ref) | copy-start | bytes 12292
  20.2 0.7 copy-start.6
  20.2 0.7 copy-start.7
  31.8 19.7 %copy-start = (bf16[512,256]{1,0:T(8,128)(2,1)S(1)}, bf16[512,256]{1,0:T(8,128)(2,1)}, u32[]{:S(2)}) copy-start(bf16[512,256]{1,0:T(8,128)(2,1)} %constant.12.clone.second_ref) | copy-start | bytes 786436
  31.8 19.7 %copy-start.3 = (f32[64,128]{1,0:T(8,128)S(1)}, f32[64,128]{1,0:T(8,128)}, u32[]{:S(2)}) copy-start(f32[64,128]{1,0:T(8,128)} %constant.11.clone.turn_ref) | copy-start | bytes 98308
  31.8 19.7 %copy-start.4 = (bf16[64,144]{1,0:T(8,128)(2,1)S(1)}, bf16[64,144]{1,0:T(8,128)(2,1)}, u32[]{:S(2)}) copy-start(bf16[64,144]{1,0:T(8,128)(2,1)} %constant.10.clone.first_ref) | copy-start | bytes 55300
  53.8 59.4 %copy-start.1 = (bf16[256,256]{1,0:T(8,128)(2,1)S(1)}, bf16[256,256]{1,0:T(8,128)(2,1)}, u32[]{:S(2)}) copy-start(bf16[256,256]{1,0:T(8,128)(2,1)} %constant.14.clone.low_ref) | copy-start | bytes 393220
  53.8 59.4 %copy-start.2 = (bf16[256,256]{1,0:T(8,128)(2,1)S(1)}, bf16[256,256]{1,0:T(8,128)(2,1)}, u32[]{:S(2)}) copy-start(bf16[256,256]{1,0:T(8,128)(2,1)} %constant.13.clone.high_ref) | copy-start | bytes 393220

commit v6 on v4

--- a/solution.py
+++ b/solution.py
@@ -18,6 +18,8 @@
 HALF = 1536
 ROWS = 6
 PLANES = 4
+FAR_ROWS = PLANES * ROWS * FAR * 48
+TERM_ROWS = FAR_ROWS + (NODES - FAR) * 32
 
 ROUNDER = 12582912.0
 
@@ -91,12 +93,43 @@
     return high, low
 
 
-def sort_kernel(ids_hbm, counts_hbm, out_ref, mark_ref, ids_ref, counts_ref, sem):
+def sort_kernel(
+    ids_hbm,
+    counts_hbm,
+    wave_hbm,
+    strength_hbm,
+    shift_hbm,
+    position_hbm,
+    weight_hbm,
+    out_ref,
+    nodes_ref,
+    ids_ref,
+    counts_ref,
+    wave_ref,
+    strength_ref,
+    shift_ref,
+    position_ref,
+    weight_ref,
+    sem,
+):
     ids_copy = pltpu.make_async_copy(ids_hbm, ids_ref, sem.at[0])
     ids_copy.start()
     counts_copy = pltpu.make_async_copy(counts_hbm, counts_ref, sem.at[1])
     counts_copy.start()
-    mark_ref[...] = jnp.zeros((8, 128), jnp.float32)
+    small = [
+        pltpu.make_async_copy(source, target, sem.at[2 + m])
+        for m, (source, target) in enumerate(
+            (
+                (wave_hbm, wave_ref),
+                (strength_hbm, strength_ref),
+                (shift_hbm, shift_ref),
+                (position_hbm, position_ref),
+                (weight_hbm, weight_ref),
+            )
+        )
+    ]
+    for one in small:
+        one.start()
     group = lax.axis_index("y")
     seat = iota((32, 128), 0)
     lane = iota((128, 128), 1)
@@ -126,6 +159,16 @@
         chosen.append(
             jnp.concatenate([as_mask(here[k] & (rank == float(s))) for s in range(RANKS)], 0)
         )
+    for one in small:
+        one.wait()
+    row = jnp.zeros((1, 128), jnp.float32)
+    for m, value in enumerate((wave_ref[0], strength_ref[0], shift_ref[0], shift_ref[1])):
+        row = jnp.where(lane[0:1] == m, value, row)
+    for q in range(NODES):
+        row = jnp.where(lane[0:1] == 16 + q, position_ref[0, q], row)
+        row = jnp.where(lane[0:1] == 32 + q, position_ref[1, q], row)
+        row = jnp.where(lane[0:1] == 48 + q, weight_ref[q], row)
+    nodes_ref[...] = row
     counts_copy.wait()
     picked = jnp.zeros((RANKS * 32, 256), jnp.float32)
     for k in range(0, 8, 2):
@@ -149,7 +192,7 @@
     out_ref[pl.ds(24, 16, stride=25), :] = names
 
 
-def place_kernel(nodes_ref, got_ref, out_ref):
+def place_kernel(terms_ref, got_ref, out_ref):
     names = got_ref[pl.ds(24, 16, stride=25), :]
     names = [names] + [pltpu.roll(names, 128 - s, 1) for s in range(1, 8)]
     names = jnp.concatenate(names, 0).T
@@ -185,12 +228,59 @@
     sine = SIN_TURN[-1] * arg + SIN_TURN[-2]
     for value in SIN_TURN[-3::-1]:
         sine = sine * arg + value
-    amplitude = weight * (1.0 + strength * inverse)
+    amplitude = weight + (weight * strength) * inverse
     return amplitude * cosine, amplitude * (turns * sine)
 
 
+def terms_kernel(nodes_ref, out_ref, near_ref):
+    z, group = lax.axis_index("z"), lax.axis_index("y")
+    seat = lax.axis_index("x") * 2 + lax.axis_index("core")
+    cluster = (z >> 1) * 4 + group
+    base = ((z & 1) * 32 + cluster) * 32 + seat * 4 - HALF
+    base_split = (64 + cluster) * 32 + (z & 1) * 16 + seat * 2 - HALF
+    column = (
+        iota((LIVE_BLOCKS, 128), 0) * 128 + iota((LIVE_BLOCKS, 128), 1) - HALF
+    ).astype(jnp.float32)
+    traits = [[nodes_ref[p : p + 1, e : e + 1] for e in range(4)] for p in range(PLANES)]
+    node_row = [nodes_ref[0:1, 16 + q : 17 + q] for q in range(NODES)]
+    node_col = [nodes_ref[0:1, 32 + q : 33 + q] for q in range(NODES)]
+    node_weight = [nodes_ref[0:1, 48 + q : 49 + q] for q in range(NODES)]
+    for p in range(PLANES):
+        for e in range(4):
+            at = e * 16 + p * 4
+            near_ref[at : at + 4, :] = jnp.broadcast_to(traits[p][e], (4, 128))
+    lane = iota((16, 128), 1)
+    near_wave = near_ref[0:16, :] * (0.5 / math.pi)
+    near_strength = near_ref[16:32, :]
+    near_row = (base + (iota((16, 128), 0) & 3)).astype(jnp.float32) + near_ref[32:48, :]
+    near_col = jnp.where(lane < 64, lane, lane - 128).astype(jnp.float32) + near_ref[48:64, :]
+    for q in range(FAR, NODES):
+        row_pos = near_row + node_row[q]
+        col_pos = near_col + node_col[q]
+        square = row_pos * row_pos + col_pos * col_pos + HEIGHT_SQ
+        real, imag = evaluate(square, near_wave, near_strength, node_weight[q])
+        at = FAR_ROWS + (q - FAR) * 32
+        out_ref[at : at + 16, :] = real
+        out_ref[at + 16 : at + 32, :] = imag
+    for p in range(PLANES):
+        wave, strength = traits[p][0] * (0.5 / math.pi), traits[p][1]
+        shift_row, shift_col = traits[p][2], traits[p][3]
+        col_base = column + shift_col
+        for q in range(FAR):
+            col_pos = col_base + node_col[q]
+            col_sq = col_pos * col_pos
+            for b in range(ROWS):
+                offset = (base + b if b < 4 else base_split + (b - 4)).astype(jnp.float32)
+                row_pos = (offset + shift_row) + node_row[q]
+                square = col_sq + (row_pos * row_pos + HEIGHT_SQ)
+                real, imag = evaluate(square, wave, strength, node_weight[q])
+                at = ((p * ROWS + b) * FAR + q) * 48
+                out_ref[at : at + 24, :] = real
+                out_ref[at + 24 : at + 48, :] = imag
+
+
 def fill_kernel(
-    nodes_ref,
+    terms_ref,
     got_ref,
     first_ref,
     turn_ref,
@@ -200,75 +290,40 @@
     fill_ref,
     turned_ref,
 ):
-    z, group = lax.axis_index("z"), lax.axis_index("y")
-    seat = lax.axis_index("x") * 2 + lax.axis_index("core")
-    cluster = (z >> 1) * 4 + group
-    base = ((z & 1) * 32 + cluster) * 32 + seat * 4 - HALF
-    base_split = (64 + cluster) * 32 + (z & 1) * 16 + seat * 2 - HALF
-    column = (
-        iota((LIVE_BLOCKS, 128), 0) * 128 + iota((LIVE_BLOCKS, 128), 1) - HALF
-    ).astype(jnp.float32)
-    traits = [[nodes_ref[p : p + 1, e : e + 1] for e in range(4)] for p in range(PLANES)]
     counts = []
     for b in range(ROWS):
         parts = [got_ref[m * 144 + b * 24 : m * 144 + b * 24 + 24, :] for m in range(8)]
         while len(parts) > 1:
             parts = [parts[m] + parts[m + 1] for m in range(0, len(parts), 2)]
         counts.append(parts[0])
-    lane = iota((16, 128), 1)
-    inner = lane < 64
+    inner = iota((2, 128), 1) < 64
     for m in range(4):
         pair = counts[m][11:13]
         merged = jnp.where(inner[0:1], pair[1:2], pair[0:1])
         for p in range(PLANES):
             near_ref[p * 4 + m : p * 4 + m + 1, :] = merged
-    for p in range(PLANES):
-        for e in range(4):
-            at = 16 + e * 16 + p * 4
-            near_ref[at : at + 4, :] = jnp.broadcast_to(traits[p][e], (4, 128))
-    near_counts = near_ref[0:16, :]
-    near_row = (base + (iota((16, 128), 0) & 3)).astype(jnp.float32) + near_ref[48:64, :]
-    near_col = jnp.where(inner, lane, lane - 128).astype(jnp.float32) + near_ref[64:80, :]
-    near_wave = near_ref[16:32, :] * (0.5 / math.pi)
-    near_strength = near_ref[32:48, :]
-    node_row = [nodes_ref[0:1, 16 + q : 17 + q] for q in range(NODES)]
-    node_col = [nodes_ref[0:1, 32 + q : 33 + q] for q in range(NODES)]
-    node_weight = [nodes_ref[0:1, 48 + q : 49 + q] for q in range(NODES)]
-    weights = [
-        [jnp.where(counts[b] > float(q), node_weight[q], 0.0) for q in range(FAR)]
-        for b in range(ROWS)
-    ]
+    near_counts = near_ref[...]
     extra_real = jnp.zeros((16, 128), jnp.float32)
     extra_imag = jnp.zeros((16, 128), jnp.float32)
     for q in range(FAR, NODES):
-        row_pos = near_row + node_row[q]
-        col_pos = near_col + node_col[q]
-        square = row_pos * row_pos + col_pos * col_pos + HEIGHT_SQ
-        weight = jnp.where(near_counts > float(q), node_weight[q], 0.0)
-        real, imag = evaluate(square, near_wave, near_strength, weight)
-        extra_real = extra_real + real
-        extra_imag = extra_imag + imag
-    inner_pair = (iota((2, 128), 0) == 1) == inner[0:2]
+        used = near_counts > float(q)
+        at = FAR_ROWS + (q - FAR) * 32
+        extra_real = extra_real + jnp.where(used, terms_ref[at : at + 16, :], 0.0)
+        extra_imag = extra_imag + jnp.where(used, terms_ref[at + 16 : at + 32, :], 0.0)
+    inner_pair = (iota((2, 128), 0) == 1) == inner
+    used = [[counts[b] > float(q) for q in range(FAR)] for b in range(ROWS)]
     turn_real = turn_ref[0:32, :]
     turn_imag = turn_ref[32:64, :]
     for p in range(PLANES):
-        wave, strength = traits[p][0] * (0.5 / math.pi), traits[p][1]
-        shift_row, shift_col = traits[p][2], traits[p][3]
-        col_base = column + shift_col
-        col_sq = []
-        for q in range(FAR):
-            col_pos = col_base + node_col[q]
-            col_sq.append(col_pos * col_pos)
         for b in range(ROWS):
-            row_offset = (base + b if b < 4 else base_split + (b - 4)).astype(jnp.float32)
             total_real = jnp.zeros((LIVE_BLOCKS, 128), jnp.float32)
             total_imag = jnp.zeros((LIVE_BLOCKS, 128), jnp.float32)
             for q in range(FAR):
-                row_pos = (row_offset + shift_row) + node_row[q]
-                square = col_sq[q] + (row_pos * row_pos + HEIGHT_SQ)
-                real, imag = evaluate(square, wave, strength, weights[b][q])
-                total_real = total_real + real
-                total_imag = total_imag + imag
+                at = ((p * ROWS + b) * FAR + q) * 48
+                total_real = total_real + jnp.where(used[b][q], terms_ref[at : at + 24, :], 0.0)
+                total_imag = total_imag + jnp.where(
+                    used[b][q], terms_ref[at + 24 : at + 48, :], 0.0
+                )
             lanes = slice((p * ROWS + b) * 128, (p * ROWS + b) * 128 + 128)
             fill_ref[0:24, lanes] = total_real
             fill_ref[24:48, lanes] = -total_imag
@@ -410,45 +465,51 @@
     piece_ids, point_counts, wavenumber, strength, displacement, node_position, node_weights
 ):
     first, turn_one, second, third, turn_two = tables()
-    sent, mark = pl.pallas_call(
+    sent, nodes = pl.pallas_call(
         sort_kernel,
         out_shape=(
             jax.ShapeDtypeStruct((400, 128), jnp.float32),
-            jax.ShapeDtypeStruct((8, 128), jnp.float32),
+            jax.ShapeDtypeStruct((1, 128), jnp.float32),
         ),
-        in_specs=[HBM, HBM],
+        in_specs=[HBM] * 7,
         out_specs=(VMEM, VMEM),
         scratch_shapes=[
             pltpu.VMEM((8, 128), jnp.int32),
             pltpu.VMEM((1024, 128), jnp.int32),
-            pltpu.SemaphoreType.DMA((2,)),
+            pltpu.SMEM((1,), jnp.float32),
+            pltpu.SMEM((1,), jnp.float32),
+            pltpu.SMEM((2,), jnp.float32),
+            pltpu.SMEM((2, NODES), jnp.float32),
+            pltpu.SMEM((NODES,), jnp.float32),
+            pltpu.SemaphoreType.DMA((7,)),
         ],
         compiler_params=pltpu.CompilerParams(vmem_limit_bytes=62 * 1024 * 1024),
-    )(piece_ids.reshape(8, 128), point_counts)
+    )(
+        piece_ids.reshape(8, 128),
+        point_counts,
+        wavenumber,
+        strength,
+        displacement.reshape(2),
+        node_position,
+        node_weights,
+    )
     got = exchange(sent.reshape(400, 1, 128), "z").reshape(400, 128)
-    nodes = jnp.concatenate(
-        [
-            wavenumber,
-            strength,
-            displacement[0],
-            displacement[1],
-            jnp.zeros((12,), jnp.float32),
-            node_position[0],
-            jnp.zeros((1,), jnp.float32),
-            node_position[1],
-            jnp.zeros((1,), jnp.float32),
-            node_weights,
-            jnp.zeros((65,), jnp.float32),
-        ]
-    ).reshape(1, 128) + mark[0:1]
     nodes = lax.all_gather(nodes, "y", axis=0, tiled=True)
+    terms = pl.pallas_call(
+        terms_kernel,
+        out_shape=jax.ShapeDtypeStruct((TERM_ROWS, 128), jnp.float32),
+        in_specs=[VMEM],
+        out_specs=VMEM,
+        scratch_shapes=[pltpu.VMEM((64, 128), jnp.float32)],
+        compiler_params=PARAMS,
+    )(nodes)
     grid = pl.pallas_call(
         place_kernel,
         out_shape=jax.ShapeDtypeStruct((1152, 128), jnp.float32),
-        in_specs=[VMEM, VMEM],
+        in_specs=[pl.BlockSpec(memory_space=pl.ANY), VMEM],
         out_specs=VMEM,
         compiler_params=PARAMS,
-    )(nodes, got)
+    )(terms, got)
     grid = exchange(grid.reshape(1152, 1, 128), ("x", "core")).reshape(1152, 128)
     sent = pl.pallas_call(
         fill_kernel,
@@ -456,12 +517,12 @@
         in_specs=[VMEM] * 5,
         out_specs=VMEM,
         scratch_shapes=[
-            pltpu.VMEM((80, 128), jnp.float32),
+            pltpu.VMEM((16, 128), jnp.float32),
             pltpu.VMEM((48, PLANES * ROWS * 128), jnp.float32),
             pltpu.VMEM((768, 256), jnp.float32),
         ],
         compiler_params=PARAMS,
-    )(nodes, grid, first, turn_one, second)
+    )(terms, grid, first, turn_one, second)
     got = exchange(
         sent.reshape(1536, 1, 128), ("z", "x", "core", "y")
     ).reshape(1536, 128)

time: 118 us -> 115 us (0.975)
  waiting for transfers between devices: 0.01 us -> 2.86 us
  local copies, waits for them, and re-layouts: 2.64 us -> 0.02 us
  blocking collectives: 88.9 us -> 86.7 us
    all_to_all x1, waiting for transfers between devices: 0.01 us -> 2.86 us  [exchange(): return lax.all_to_all(values, axes, split_axis=0, concat_axis=0, tiled=True)]
    all_to_all x2, blocking collectives: 80.4 us -> 78.3 us  [exchange(): return lax.all_to_all(values, axes, split_axis=0, concat_axis=0, tiled=True)]
    pallas_call x0 -> x1, Pallas kernels: none -> 1.33 us  [shards(): pl.pallas_call(terms_kernel, out_shape=jax.ShapeDtypeStruct((TERM_ROWS, 1...]
    pallas_call x1, Pallas kernels: 2.33 us -> 1.04 us  [shards(): pl.pallas_call(fill_kernel, out_shape=jax.ShapeDtypeStruct((1536, 128), j...]
    concatenate x1 -> x0, local copies, waits for them, and re-layouts: 1.27 us -> none  [shards(): jnp.concatenate([wavenumber, strength, displacement[0], displacement[1],...]
  transfers between devices with their start and end apart: 1 -> 1, of which waited for: 0 -> 1; matrix products, arithmetic and copies ran while one was open for 2% -> 0% of each run, Pallas kernels for 0% -> 1%
where the time goes in v6:
time: 115 us
  blocking collectives  86.7 us (75%)
  starting transfers between devices  15.8 us (14%)
  Pallas kernels  7.27 us (6%)
  waiting for transfers between devices  2.86 us (2%)
  between operations  1.99 us (2%)
    all_to_all x2, blocking collectives, exchange(): return lax.all_to_all(values, axes, split_axis=0, concat_axis=0, tiled=True)  78.3 us
    all_to_all x1, starting transfers between devices, exchange(): return lax.all_to_all(values, axes, split_axis=0, concat_axis=0, tiled=True)  15.8 us
    all_gather x1, blocking collectives, shards(): nodes = lax.all_gather(nodes, 'y', axis=0, tiled=True)  8.37 us
    all_to_all x1, waiting for transfers between devices, exchange(): return lax.all_to_all(values, axes, split_axis=0, concat_axis=0, tiled=True)  2.86 us
    pallas_call x1, Pallas kernels, shards(): pl.pallas_call(sort_kernel, out_shape=(jax.ShapeDtypeStruct((400, 128), j...  2.44 us
  transfers between devices with their start and end apart: 1, of which 1 were waited for; matrix products, arithmetic and copies ran while one was open for 0% of the time, Pallas kernels for 1%

profile of v6, /device:TPU:1, one launch (start us, length us, event | category | flops | bytes accessed | tf_op | source)
XLA Modules:
  0.0 114.5 jit_solution(13935787000978401291)
XLA Ops:
  1.9 2.4 %shard_map.140 = (f32[400,128]{1,0:T(8,128)}, f32[1,128]{1,0:T(1,128)}) custom-call(s32[8,128]{1,0:T(8,128)} %bitcast.23, s32[1024,128]{1,0:T(8,128)} %counts_hbm.1, f32[1]{0:T(128)S(6)} %copy.19.wave_hbm, f32[1]{0:T(128)S(6)} %copy.20.strength_hbm, f32[2]{0:T(128)} %bitcast.25, f32[2,15]{1,0:T(2,128)} %position_hbm.1, f32[15]{0:T(128)} %weight_hbm.1), custom_call_target="tpu_custom_call" | custom-call | tf_op jit(solution)/shard_map/pallas_call | solution.py:468
  4.4 15.8 %all-to-all-start = ((f32[400,1,128]{2,1,0:T(1,128)}), f32[400,1,128]{2,1,0:T(1,128)S(1)}, u32[]{:S(2)}, u32[]{:S(2)}) async-start(f32[400,1,128]{2,1,0:T(1,128)} %bitcast.22), calls=%async_computation | async-start | bytes 409600 | tf_op jit(solution)/shard_map/all_to_all | solution.py:461
  20.1 8.4 %all-gather = f32[4,1,128]{2,1,0:T(1,128)S(1)} all-gather(f32[1,1,128]{2,1,0:T(1,128)} %bitcast.24), channel_id=1, replica_groups=mesh['z'=16,'x'=4,'core'=2,'y'=4] {'y'}, dimensions={0}, use_global_device_ids=true | all-gather | bytes 2560 | tf_op jit(solution)/shard_map/all_gather | solution.py:497
  28.5 1.3 %shard_map.141.terms_ref = f32[3840,128]{1,0:T(8,128)S(1)} custom-call(f32[4,128]{1,0:T(4,128)S(1)} %bitcast.21), custom_call_target="tpu_custom_call" | custom-call | tf_op jit(solution)/shard_map/pallas_call | solution.py:498
  29.8 2.9 %all-to-all-done = f32[400,1,128]{2,1,0:T(1,128)S(1)} async-done(((f32[400,1,128]{2,1,0:T(1,128)}), f32[400,1,128]{2,1,0:T(1,128)S(1)}, u32[]{:S(2)}, u32[]{:S(2)}) %all-to-all-start) | async-done | bytes 204832 | tf_op jit(solution)/shard_map/all_to_all | solution.py:461
  32.7 0.0 copy-start
  32.7 0.0 copy-start.1
  32.7 0.0 copy-start.4
  32.7 0.4 shard_map.142
  33.1 19.5 %all_to_all.15 = f32[1152,1,128]{2,1,0:T(1,128)S(1)} all-to-all(f32[1152,1,128]{2,1,0:T(1,128)S(1)} %bitcast.19), channel_id=1, replica_groups=mesh['z'=16,'x'=4,'core'=2,'y'=4] {'x','core'}, dimensions={0} | all-to-all | bytes 1179648 | tf_op jit(solution)/shard_map/all_to_all | solution.py:461
  52.6 0.0 copy-done
  52.6 0.0 copy-done.1
  52.6 0.0 copy-done.4
  52.6 0.0 copy-start.2
  52.7 0.0 copy-start.3
  52.7 1.0 shard_map.143
  53.7 58.8 %all_to_all.16 = f32[1536,1,128]{2,1,0:T(1,128)S(1)} all-to-all(f32[1536,1,128]{2,1,0:T(1,128)S(1)} %bitcast.16), channel_id=1, replica_groups=mesh['z'=16,'x'=4,'core'=2,'y'=4] {'z','x','core','y'}, dimensions={0} | all-to-all | bytes 1572864 | tf_op jit(solution)/shard_map/all_to_all | solution.py:461
  112.5 0.0 copy-done.2
  112.5 0.0 copy-done.3
  112.5 2.0 %shard_map.144 = (f32[4,8,4096]{2,1,0:T(8,128)}, f32[4,8,4096]{2,1,0:T(8,128)}) custom-call(f32[1536,128]{1,0:T(8,128)S(1)} %bitcast.17, bf16[256,256]{1,0:T(8,128)(2,1)S(1)} %copy-done.3, bf16[256,256]{1,0:T(8,128)(2,1)S(1)} %copy-done.2, f32[64,128]{1,0:T(8,128)S(1)} %copy-done.1), custom_call_target="tpu_custom_call" | custom-call | tf_op jit(solution)/shard_map/pallas_call | solution.py:530
Async XLA Ops:
  4.4 28.3 %all-to-all-start = ((f32[400,1,128]{2,1,0:T(1,128)}), f32[400,1,128]{2,1,0:T(1,128)S(1)}, u32[]{:S(2)}, u32[]{:S(2)}) async-start(f32[400,1,128]{2,1,0:T(1,128)} %bitcast.22), calls=%async_computation | async-start | bytes 409600 | tf_op jit(solution)/shard_map/all_to_all | solution.py:461
  32.7 19.9 %copy-start = (bf16[512,256]{1,0:T(8,128)(2,1)S(1)}, bf16[512,256]{1,0:T(8,128)(2,1)}, u32[]{:S(2)}) copy-start(bf16[512,256]{1,0:T(8,128)(2,1)} %constant.12.clone.second_ref) | copy-start | bytes 786436
  32.7 19.9 %copy-start.1 = (f32[64,128]{1,0:T(8,128)S(1)}, f32[64,128]{1,0:T(8,128)}, u32[]{:S(2)}) copy-start(f32[64,128]{1,0:T(8,128)} %constant.11.clone.turn_ref) | copy-start | bytes 98308
  32.7 19.9 %copy-start.4 = (bf16[64,144]{1,0:T(8,128)(2,1)S(1)}, bf16[64,144]{1,0:T(8,128)(2,1)}, u32[]{:S(2)}) copy-start(bf16[64,144]{1,0:T(8,128)(2,1)} %constant.10.clone.first_ref) | copy-start | bytes 55300
  52.6 59.9 %copy-start.2 = (bf16[256,256]{1,0:T(8,128)(2,1)S(1)}, bf16[256,256]{1,0:T(8,128)(2,1)}, u32[]{:S(2)}) copy-start(bf16[256,256]{1,0:T(8,128)(2,1)} %constant.14.clone.low_ref) | copy-start | bytes 393220
  52.7 59.9 %copy-start.3 = (bf16[256,256]{1,0:T(8,128)(2,1)S(1)}, bf16[256,256]{1,0:T(8,128)(2,1)}, u32[]{:S(2)}) copy-start(bf16[256,256]{1,0:T(8,128)(2,1)} %constant.13.clone.high_ref) | copy-start | bytes 393220

commit v7 on v6

--- a/solution.py
+++ b/solution.py
@@ -56,7 +56,9 @@
     t = np.arange(128)
     angle = 2.0 * np.pi * (v1[:, None] * t[None, :]) / LENGTH
     turn_one = np.concatenate([np.cos(angle), -np.sin(angle)], 0).astype(np.float32)
-    angle = 2.0 * np.pi * ((t[:, None] * t[None, :]) % 128) / 128
+    core, z, x = np.arange(2)[:, None, None], np.arange(16)[:, None], np.arange(4)
+    wide = (z * 8 + x * 2 + core).reshape(128)
+    angle = 2.0 * np.pi * ((wide[:, None] * t[None, :]) % 128) / 128
     cos, sin = np.cos(angle), np.sin(angle)
     second = np.concatenate([np.concatenate([cos, sin], 1), np.concatenate([-sin, cos], 1)], 0)
     second = np.concatenate(split_np(second / 64.0), 0)
@@ -410,11 +412,11 @@
     for pair in range(16):
         parts = []
         for j in range(4):
-            at = ((pair >> 1) * 4 + j) * 3 + (pair & 1)
-            parts.append(got_ref[pl.ds(at, 16, stride=96), :])
+            at = ((pair >> 1 & 1) * 256 + (pair >> 2) * 4 + j) * 3 + (pair & 1)
+            parts.append(got_ref[pl.ds(at, 16, stride=48), :])
         for j in range(4):
-            at = ((pair >> 3) * 32 + (pair & 7) * 4 + j) * 3 + 2
-            parts.append(got_ref[pl.ds(at, 8, stride=192), :])
+            at = ((pair & 1) * 256 + (pair >> 3) * 16 + (pair >> 1 & 3) * 4 + j) * 3 + 2
+            parts.append(got_ref[pl.ds(at, 8, stride=96), :])
         flipped = jnp.concatenate(parts + [blank], 0).T
         for m in range(2):
             for ri in range(2):
@@ -524,7 +526,7 @@
         compiler_params=PARAMS,
     )(terms, grid, first, turn_one, second)
     got = exchange(
-        sent.reshape(1536, 1, 128), ("z", "x", "core", "y")
+        sent.reshape(1536, 1, 128), ("core", "z", "x", "y")
     ).reshape(1536, 128)
     shape = jax.ShapeDtypeStruct((PLANES, 8, LENGTH), jnp.float32)
     return pl.pallas_call(

time: 115 us -> 112 us (0.974)
  blocking collectives: 86.7 us -> 84 us
    all_to_all x2, blocking collectives: 78.3 us -> 75.7 us  [exchange(): return lax.all_to_all(values, axes, split_axis=0, concat_axis=0, tiled=True)]
where the time goes in v7:
time: 112 us
  blocking collectives  84 us (75%)
  starting transfers between devices  15.8 us (14%)
  Pallas kernels  7.14 us (6%)
  waiting for transfers between devices  2.86 us (3%)
  between operations  1.99 us (2%)
    all_to_all x2, blocking collectives, exchange(): return lax.all_to_all(values, axes, split_axis=0, concat_axis=0, tiled=True)  75.7 us
    all_to_all x1, starting transfers between devices, exchange(): return lax.all_to_all(values, axes, split_axis=0, concat_axis=0, tiled=True)  15.8 us
    all_gather x1, blocking collectives, shards(): nodes = lax.all_gather(nodes, 'y', axis=0, tiled=True)  8.37 us
    all_to_all x1, waiting for transfers between devices, exchange(): return lax.all_to_all(values, axes, split_axis=0, concat_axis=0, tiled=True)  2.86 us
    pallas_call x1, Pallas kernels, shards(): pl.pallas_call(sort_kernel, out_shape=(jax.ShapeDtypeStruct((400, 128), j...  2.44 us
  transfers between devices with their start and end apart: 1, of which 1 were waited for; matrix products, arithmetic and copies ran while one was open for 0% of the time, Pallas kernels for 1%

profile of v7, /device:TPU:1, one launch (start us, length us, event | category | flops | bytes accessed | tf_op | source)
XLA Modules:
  0.0 111.8 jit_solution(16696350728433548808)
XLA Ops:
  1.9 2.4 %shard_map.140 = (f32[400,128]{1,0:T(8,128)}, f32[1,128]{1,0:T(1,128)}) custom-call(s32[8,128]{1,0:T(8,128)} %bitcast.23, s32[1024,128]{1,0:T(8,128)} %counts_hbm.1, f32[1]{0:T(128)S(6)} %copy.19.wave_hbm, f32[1]{0:T(128)S(6)} %copy.20.strength_hbm, f32[2]{0:T(128)} %bitcast.25, f32[2,15]{1,0:T(2,128)} %position_hbm.1, f32[15]{0:T(128)} %weight_hbm.1), custom_call_target="tpu_custom_call" | custom-call | tf_op jit(solution)/shard_map/pallas_call | solution.py:470
  4.4 15.8 %all-to-all-start = ((f32[400,1,128]{2,1,0:T(1,128)}), f32[400,1,128]{2,1,0:T(1,128)S(1)}, u32[]{:S(2)}, u32[]{:S(2)}) async-start(f32[400,1,128]{2,1,0:T(1,128)} %bitcast.22), calls=%async_computation | async-start | bytes 409600 | tf_op jit(solution)/shard_map/all_to_all | solution.py:463
  20.1 8.4 %all-gather = f32[4,1,128]{2,1,0:T(1,128)S(1)} all-gather(f32[1,1,128]{2,1,0:T(1,128)} %bitcast.24), channel_id=1, replica_groups=mesh['z'=16,'x'=4,'core'=2,'y'=4] {'y'}, dimensions={0}, use_global_device_ids=true | all-gather | bytes 2560 | tf_op jit(solution)/shard_map/all_gather | solution.py:499
  28.5 1.3 %shard_map.141.terms_ref = f32[3840,128]{1,0:T(8,128)S(1)} custom-call(f32[4,128]{1,0:T(4,128)S(1)} %bitcast.21), custom_call_target="tpu_custom_call" | custom-call | tf_op jit(solution)/shard_map/pallas_call | solution.py:500
  29.8 2.9 %all-to-all-done = f32[400,1,128]{2,1,0:T(1,128)S(1)} async-done(((f32[400,1,128]{2,1,0:T(1,128)}), f32[400,1,128]{2,1,0:T(1,128)S(1)}, u32[]{:S(2)}, u32[]{:S(2)}) %all-to-all-start) | async-done | bytes 204832 | tf_op jit(solution)/shard_map/all_to_all | solution.py:463
  32.7 0.0 copy-start
  32.7 0.0 copy-start.1
  32.7 0.0 copy-start.4
  32.7 0.4 shard_map.142
  33.1 19.5 %all_to_all.15 = f32[1152,1,128]{2,1,0:T(1,128)S(1)} all-to-all(f32[1152,1,128]{2,1,0:T(1,128)S(1)} %bitcast.19), channel_id=1, replica_groups=mesh['z'=16,'x'=4,'core'=2,'y'=4] {'x','core'}, dimensions={0} | all-to-all | bytes 1179648 | tf_op jit(solution)/shard_map/all_to_all | solution.py:463
  52.6 0.0 copy-done
  52.6 0.0 copy-done.1
  52.6 0.0 copy-done.4
  52.6 0.0 copy-start.2
  52.7 0.0 copy-start.3
  52.7 1.0 shard_map.143
  53.7 56.2 %all_to_all.16 = f32[1536,1,128]{2,1,0:T(1,128)S(1)} all-to-all(f32[1536,1,128]{2,1,0:T(1,128)S(1)} %bitcast.16), channel_id=1, replica_groups=mesh['z'=16,'x'=4,'core'=2,'y'=4] {'core','z','x','y'}, dimensions={0} | all-to-all | bytes 1572864 | tf_op jit(solution)/shard_map/all_to_all | solution.py:463
  109.9 0.0 copy-done.2
  109.9 0.0 copy-done.3
  109.9 1.9 %shard_map.144 = (f32[4,8,4096]{2,1,0:T(8,128)}, f32[4,8,4096]{2,1,0:T(8,128)}) custom-call(f32[1536,128]{1,0:T(8,128)S(1)} %bitcast.17, bf16[256,256]{1,0:T(8,128)(2,1)S(1)} %copy-done.3, bf16[256,256]{1,0:T(8,128)(2,1)S(1)} %copy-done.2, f32[64,128]{1,0:T(8,128)S(1)} %copy-done.1), custom_call_target="tpu_custom_call" | custom-call | tf_op jit(solution)/shard_map/pallas_call | solution.py:532
Async XLA Ops:
  4.4 28.3 %all-to-all-start = ((f32[400,1,128]{2,1,0:T(1,128)}), f32[400,1,128]{2,1,0:T(1,128)S(1)}, u32[]{:S(2)}, u32[]{:S(2)}) async-start(f32[400,1,128]{2,1,0:T(1,128)} %bitcast.22), calls=%async_computation | async-start | bytes 409600 | tf_op jit(solution)/shard_map/all_to_all | solution.py:463
  32.7 19.9 %copy-start = (bf16[512,256]{1,0:T(8,128)(2,1)S(1)}, bf16[512,256]{1,0:T(8,128)(2,1)}, u32[]{:S(2)}) copy-start(bf16[512,256]{1,0:T(8,128)(2,1)} %constant.12.clone.second_ref) | copy-start | bytes 786436
  32.7 19.9 %copy-start.1 = (f32[64,128]{1,0:T(8,128)S(1)}, f32[64,128]{1,0:T(8,128)}, u32[]{:S(2)}) copy-start(f32[64,128]{1,0:T(8,128)} %constant.11.clone.turn_ref) | copy-start | bytes 98308
  32.7 19.9 %copy-start.4 = (bf16[64,144]{1,0:T(8,128)(2,1)S(1)}, bf16[64,144]{1,0:T(8,128)(2,1)}, u32[]{:S(2)}) copy-start(bf16[64,144]{1,0:T(8,128)(2,1)} %constant.10.clone.first_ref) | copy-start | bytes 55300
  52.6 57.3 %copy-start.2 = (bf16[256,256]{1,0:T(8,128)(2,1)S(1)}, bf16[256,256]{1,0:T(8,128)(2,1)}, u32[]{:S(2)}) copy-start(bf16[256,256]{1,0:T(8,128)(2,1)} %constant.14.clone.low_ref) | copy-start | bytes 393220
  52.7 57.2 %copy-start.3 = (bf16[256,256]{1,0:T(8,128)(2,1)S(1)}, bf16[256,256]{1,0:T(8,128)(2,1)}, u32[]{:S(2)}) copy-start(bf16[256,256]{1,0:T(8,128)(2,1)} %constant.13.clone.high_ref) | copy-start | bytes 393220

commit v8 on v7

--- a/solution.py
+++ b/solution.py
@@ -18,6 +18,7 @@
 HALF = 1536
 ROWS = 6
 PLANES = 4
+Z_ORDER = list(range(0, 16, 2)) + list(range(1, 16, 2))
 FAR_ROWS = PLANES * ROWS * FAR * 48
 TERM_ROWS = FAR_ROWS + (NODES - FAR) * 32
 
@@ -56,15 +57,16 @@
     t = np.arange(128)
     angle = 2.0 * np.pi * (v1[:, None] * t[None, :]) / LENGTH
     turn_one = np.concatenate([np.cos(angle), -np.sin(angle)], 0).astype(np.float32)
-    core, z, x = np.arange(2)[:, None, None], np.arange(16)[:, None], np.arange(4)
+    core, x = np.arange(2)[:, None, None], np.arange(4)
+    z = np.array(Z_ORDER)[:, None]
     wide = (z * 8 + x * 2 + core).reshape(128)
     angle = 2.0 * np.pi * ((wide[:, None] * t[None, :]) % 128) / 128
     cos, sin = np.cos(angle), np.sin(angle)
     second = np.concatenate([np.concatenate([cos, sin], 1), np.concatenate([-sin, cos], 1)], 0)
     second = np.concatenate(split_np(second / 64.0), 0)
-    j, z = np.arange(4)[:, None], np.arange(16)[None, :]
+    j, z = np.arange(4)[:, None], np.array(Z_ORDER)[None, :]
     whole = ((z & 1) * 32 + (z >> 1) * 4 + j).reshape(64)
-    c = np.concatenate([whole, (64 + z[:, :8] * 4 + j).reshape(32)])
+    c = np.concatenate([whole, (64 + np.arange(8)[None, :] * 4 + j).reshape(32)])
     angle = 2.0 * np.pi * (((c[:, None] - 48) * t[None, :]) % 128) / 128
     third = np.zeros((2, 128, 2, 128))
     third[0, :96, 0] = np.cos(angle)
@@ -415,8 +417,8 @@
             at = ((pair >> 1 & 1) * 256 + (pair >> 2) * 4 + j) * 3 + (pair & 1)
             parts.append(got_ref[pl.ds(at, 16, stride=48), :])
         for j in range(4):
-            at = ((pair & 1) * 256 + (pair >> 3) * 16 + (pair >> 1 & 3) * 4 + j) * 3 + 2
-            parts.append(got_ref[pl.ds(at, 8, stride=96), :])
+            at = ((pair & 1) * 256 + (pair >> 3) * 128 + (pair >> 1 & 3) * 4 + j) * 3 + 2
+            parts.append(got_ref[pl.ds(at, 8, stride=48), :])
         flipped = jnp.concatenate(parts + [blank], 0).T
         for m in range(2):
             for ri in range(2):
@@ -525,8 +527,20 @@
         ],
         compiler_params=PARAMS,
     )(terms, grid, first, turn_one, second)
-    got = exchange(
-        sent.reshape(1536, 1, 128), ("core", "z", "x", "y")
+    order = [
+        z * 32 + x * 8 + core * 4 + y
+        for core in range(2)
+        for z in Z_ORDER
+        for x in range(4)
+        for y in range(4)
+    ]
+    got = lax.all_to_all(
+        sent.reshape(1536, 1, 128),
+        ("z", "x", "core", "y"),
+        split_axis=0,
+        concat_axis=0,
+        axis_index_groups=[order],
+        tiled=True,
     ).reshape(1536, 128)
     shape = jax.ShapeDtypeStruct((PLANES, 8, LENGTH), jnp.float32)
     return pl.pallas_call(

time: 112 us -> 112 us (level)
    all_to_all x2 -> x1, blocking collectives: 75.7 us -> 19.5 us  [exchange(): return lax.all_to_all(values, axes, split_axis=0, concat_axis=0, tiled=True)]
    all_to_all x0 -> x1, blocking collectives: none -> 55.2 us  [shards(): lax.all_to_all(sent.reshape(1536, 1, 128), ('z', 'x', 'core', 'y'), split...]
where the time goes in v8:
time: 112 us; the launch traced here: 111 us
  blocking collectives  83 us (74%)
  starting transfers between devices  15.8 us (14%)
  Pallas kernels  7.08 us (6%)
  waiting for transfers between devices  2.86 us (3%)
  between operations  1.99 us (2%)
    all_to_all x1, blocking collectives, shards(): lax.all_to_all(sent.reshape(1536, 1, 128), ('z', 'x', 'core', 'y'), split...  55.2 us
    all_to_all x1, blocking collectives, exchange(): return lax.all_to_all(values, axes, split_axis=0, concat_axis=0, tiled=True)  19.5 us
    all_to_all x1, starting transfers between devices, exchange(): return lax.all_to_all(values, axes, split_axis=0, concat_axis=0, tiled=True)  15.8 us
    all_gather x1, blocking collectives, shards(): nodes = lax.all_gather(nodes, 'y', axis=0, tiled=True)  8.37 us
    all_to_all x1, waiting for transfers between devices, exchange(): return lax.all_to_all(values, axes, split_axis=0, concat_axis=0, tiled=True)  2.86 us
    pallas_call x1, Pallas kernels, shards(): pl.pallas_call(sort_kernel, out_shape=(jax.ShapeDtypeStruct((400, 128), j...  2.44 us
  transfers between devices with their start and end apart: 1, of which 1 were waited for; matrix products, arithmetic and copies ran while one was open for 0% of the time, Pallas kernels for 1%

profile of v8, /device:TPU:1, one launch (start us, length us, event | category | flops | bytes accessed | tf_op | source)
XLA Modules:
  0.0 110.7 jit_solution(17806637386471750982)
XLA Ops:
  1.9 2.4 %shard_map.140 = (f32[400,128]{1,0:T(8,128)}, f32[1,128]{1,0:T(1,128)}) custom-call(s32[8,128]{1,0:T(8,128)} %bitcast.23, s32[1024,128]{1,0:T(8,128)} %counts_hbm.1, f32[1]{0:T(128)S(6)} %copy.19.wave_hbm, f32[1]{0:T(128)S(6)} %copy.20.strength_hbm, f32[2]{0:T(128)} %bitcast.25, f32[2,15]{1,0:T(2,128)} %position_hbm.1, f32[15]{0:T(128)} %weight_hbm.1), custom_call_target="tpu_custom_call" | custom-call | tf_op jit(solution)/shard_map/pallas_call | solution.py:472
  4.4 15.8 %all-to-all-start = ((f32[400,1,128]{2,1,0:T(1,128)}), f32[400,1,128]{2,1,0:T(1,128)S(1)}, u32[]{:S(2)}, u32[]{:S(2)}) async-start(f32[400,1,128]{2,1,0:T(1,128)} %bitcast.22), calls=%async_computation | async-start | bytes 409600 | tf_op jit(solution)/shard_map/all_to_all | solution.py:465
  20.1 8.4 %all-gather = f32[4,1,128]{2,1,0:T(1,128)S(1)} all-gather(f32[1,1,128]{2,1,0:T(1,128)} %bitcast.24), channel_id=1, replica_groups=mesh['z'=16,'x'=4,'core'=2,'y'=4] {'y'}, dimensions={0}, use_global_device_ids=true | all-gather | bytes 2560 | tf_op jit(solution)/shard_map/all_gather | solution.py:501
  28.5 1.3 %shard_map.141.terms_ref = f32[3840,128]{1,0:T(8,128)S(1)} custom-call(f32[4,128]{1,0:T(4,128)S(1)} %bitcast.21), custom_call_target="tpu_custom_call" | custom-call | tf_op jit(solution)/shard_map/pallas_call | solution.py:502
  29.8 2.9 %all-to-all-done = f32[400,1,128]{2,1,0:T(1,128)S(1)} async-done(((f32[400,1,128]{2,1,0:T(1,128)}), f32[400,1,128]{2,1,0:T(1,128)S(1)}, u32[]{:S(2)}, u32[]{:S(2)}) %all-to-all-start) | async-done | bytes 204832 | tf_op jit(solution)/shard_map/all_to_all | solution.py:465
  32.7 0.0 copy-start
  32.7 0.0 copy-start.1
  32.7 0.0 copy-start.4
  32.7 0.4 shard_map.142
  33.1 19.5 %all_to_all.15 = f32[1152,1,128]{2,1,0:T(1,128)S(1)} all-to-all(f32[1152,1,128]{2,1,0:T(1,128)S(1)} %bitcast.19), channel_id=1, replica_groups=mesh['z'=16,'x'=4,'core'=2,'y'=4] {'x','core'}, dimensions={0} | all-to-all | bytes 1179648 | tf_op jit(solution)/shard_map/all_to_all | solution.py:465
  52.6 0.0 copy-done
  52.6 0.0 copy-done.1
  52.6 0.0 copy-done.4
  52.6 0.0 copy-start.2
  52.7 0.0 copy-start.3
  52.7 1.0 shard_map.143
  53.7 55.2 %all_to_all.16 = f32[1536,1,128]{2,1,0:T(1,128)S(1)} all-to-all(f32[1536,1,128]{2,1,0:T(1,128)S(1)} %bitcast.16), channel_id=1, replica_groups={{0,1,2,3,8,9,10,11,16,17,18,19,24,25,26,27,64,65,66,67,72,73,74,75,80,8..., dimensions={0} | all-to-all | bytes 1572864 | tf_op jit(solution)/shard_map/all_to_all | solution.py:537
  108.9 0.0 copy-done.2
  108.9 0.0 copy-done.3
  108.9 1.8 %shard_map.144 = (f32[4,8,4096]{2,1,0:T(8,128)}, f32[4,8,4096]{2,1,0:T(8,128)}) custom-call(f32[1536,128]{1,0:T(8,128)S(1)} %bitcast.17, bf16[256,256]{1,0:T(8,128)(2,1)S(1)} %copy-done.3, bf16[256,256]{1,0:T(8,128)(2,1)S(1)} %copy-done.2, f32[64,128]{1,0:T(8,128)S(1)} %copy-done.1), custom_call_target="tpu_custom_call" | custom-call | tf_op jit(solution)/shard_map/pallas_call | solution.py:546
Async XLA Ops:
  4.4 28.3 %all-to-all-start = ((f32[400,1,128]{2,1,0:T(1,128)}), f32[400,1,128]{2,1,0:T(1,128)S(1)}, u32[]{:S(2)}, u32[]{:S(2)}) async-start(f32[400,1,128]{2,1,0:T(1,128)} %bitcast.22), calls=%async_computation | async-start | bytes 409600 | tf_op jit(solution)/shard_map/all_to_all | solution.py:465
  32.7 19.9 %copy-start = (bf16[512,256]{1,0:T(8,128)(2,1)S(1)}, bf16[512,256]{1,0:T(8,128)(2,1)}, u32[]{:S(2)}) copy-start(bf16[512,256]{1,0:T(8,128)(2,1)} %constant.12.clone.second_ref) | copy-start | bytes 786436
  32.7 19.9 %copy-start.1 = (f32[64,128]{1,0:T(8,128)S(1)}, f32[64,128]{1,0:T(8,128)}, u32[]{:S(2)}) copy-start(f32[64,128]{1,0:T(8,128)} %constant.11.clone.turn_ref) | copy-start | bytes 98308
  32.7 19.9 %copy-start.4 = (bf16[64,144]{1,0:T(8,128)(2,1)S(1)}, bf16[64,144]{1,0:T(8,128)(2,1)}, u32[]{:S(2)}) copy-start(bf16[64,144]{1,0:T(8,128)(2,1)} %constant.10.clone.first_ref) | copy-start | bytes 55300
  52.6 56.2 %copy-start.2 = (bf16[256,256]{1,0:T(8,128)(2,1)S(1)}, bf16[256,256]{1,0:T(8,128)(2,1)}, u32[]{:S(2)}) copy-start(bf16[256,256]{1,0:T(8,128)(2,1)} %constant.14.clone.low_ref) | copy-start | bytes 393220
  52.7 56.2 %copy-start.3 = (bf16[256,256]{1,0:T(8,128)(2,1)S(1)}, bf16[256,256]{1,0:T(8,128)(2,1)}, u32[]{:S(2)}) copy-start(bf16[256,256]{1,0:T(8,128)(2,1)} %constant.13.clone.high_ref) | copy-start | bytes 393220

commit v9 on v8

--- a/solution.py
+++ b/solution.py
@@ -146,7 +146,7 @@
     block = ((ids >> 10) + 48) & 127
     role = block >> 5
     low_bit = jnp.where(role == 2, local >> 9, role)
-    target = ((block >> 2) & 7) * 2 + low_bit + jnp.where(role == 2, 16, 0)
+    target = ((block >> 2) & 7) + low_bit * 8 + jnp.where(role == 2, 16, 0)
     target = jnp.where(((block & 3) == group) & (role < 3), target, -1)
     here = [seat == target[k : k + 1, :] for k in range(8)]
     sums = dot(jnp.concatenate([as_mask(mask) for mask in here], 0), prefix)
@@ -497,7 +497,14 @@
         node_position,
         node_weights,
     )
-    got = exchange(sent.reshape(400, 1, 128), "z").reshape(400, 128)
+    got = lax.all_to_all(
+        sent.reshape(400, 1, 128),
+        "z",
+        split_axis=0,
+        concat_axis=0,
+        axis_index_groups=[Z_ORDER],
+        tiled=True,
+    ).reshape(400, 128)
     nodes = lax.all_gather(nodes, "y", axis=0, tiled=True)
     terms = pl.pallas_call(
         terms_kernel,

time: 112 us -> 112 us (level)
    all_to_all x1, blocking collectives: 19.5 us -> 17.7 us  [exchange(): return lax.all_to_all(values, axes, split_axis=0, concat_axis=0, tiled=True)]
where the time goes in v9:
time: 112 us; the launch traced here: 111 us
  blocking collectives  82 us (73%)
  starting transfers between devices  15.8 us (14%)
  Pallas kernels  7.09 us (6%)
  waiting for transfers between devices  3.91 us (3%)
  between operations  1.99 us (2%)
    all_to_all x1, blocking collectives, shards(): lax.all_to_all(sent.reshape(1536, 1, 128), ('z', 'x', 'core', 'y'), split...  55.9 us
    all_to_all x1, blocking collectives, exchange(): return lax.all_to_all(values, axes, split_axis=0, concat_axis=0, tiled=True)  17.7 us
    all_to_all x1, starting transfers between devices, shards(): lax.all_to_all(sent.reshape(400, 1, 128), 'z', split_axis=0, concat_axis=...  15.8 us
    all_gather x1, blocking collectives, shards(): nodes = lax.all_gather(nodes, 'y', axis=0, tiled=True)  8.37 us
    all_to_all x1, waiting for transfers between devices, shards(): lax.all_to_all(sent.reshape(400, 1, 128), 'z', split_axis=0, concat_axis=...  3.91 us
    pallas_call x1, Pallas kernels, shards(): pl.pallas_call(sort_kernel, out_shape=(jax.ShapeDtypeStruct((400, 128), j...  2.44 us
  transfers between devices with their start and end apart: 1, of which 1 were waited for; matrix products, arithmetic and copies ran while one was open for 0% of the time, Pallas kernels for 1%

profile of v9, /device:TPU:1, one launch (start us, length us, event | category | flops | bytes accessed | tf_op | source)
XLA Modules:
  0.0 110.7 jit_solution(12966599322882929804)
XLA Ops:
  1.9 2.4 %shard_map.140 = (f32[400,128]{1,0:T(8,128)}, f32[1,128]{1,0:T(1,128)}) custom-call(s32[8,128]{1,0:T(8,128)} %bitcast.23, s32[1024,128]{1,0:T(8,128)} %counts_hbm.1, f32[1]{0:T(128)S(6)} %copy.19.wave_hbm, f32[1]{0:T(128)S(6)} %copy.20.strength_hbm, f32[2]{0:T(128)} %bitcast.25, f32[2,15]{1,0:T(2,128)} %position_hbm.1, f32[15]{0:T(128)} %weight_hbm.1), custom_call_target="tpu_custom_call" | custom-call | tf_op jit(solution)/shard_map/pallas_call | solution.py:472
  4.4 15.8 %all-to-all-start = ((f32[400,1,128]{2,1,0:T(1,128)}), f32[400,1,128]{2,1,0:T(1,128)S(1)}, u32[]{:S(2)}, u32[]{:S(2)}) async-start(f32[400,1,128]{2,1,0:T(1,128)} %bitcast.22), calls=%async_computation | async-start | bytes 409600 | tf_op jit(solution)/shard_map/all_to_all | solution.py:500
  20.1 8.4 %all-gather = f32[4,1,128]{2,1,0:T(1,128)S(1)} all-gather(f32[1,1,128]{2,1,0:T(1,128)} %bitcast.24), channel_id=1, replica_groups=mesh['z'=16,'x'=4,'core'=2,'y'=4] {'y'}, dimensions={0}, use_global_device_ids=true | all-gather | bytes 2560 | tf_op jit(solution)/shard_map/all_gather | solution.py:508
  28.5 1.3 %shard_map.141.terms_ref = f32[3840,128]{1,0:T(8,128)S(1)} custom-call(f32[4,128]{1,0:T(4,128)S(1)} %bitcast.21), custom_call_target="tpu_custom_call" | custom-call | tf_op jit(solution)/shard_map/pallas_call | solution.py:509
  29.8 3.9 %all-to-all-done = f32[400,1,128]{2,1,0:T(1,128)S(1)} async-done(((f32[400,1,128]{2,1,0:T(1,128)}), f32[400,1,128]{2,1,0:T(1,128)S(1)}, u32[]{:S(2)}, u32[]{:S(2)}) %all-to-all-start) | async-done | bytes 204832 | tf_op jit(solution)/shard_map/all_to_all | solution.py:500
  33.8 0.0 copy-start
  33.8 0.0 copy-start.1
  33.8 0.0 copy-start.4
  33.8 0.4 shard_map.142
  34.2 17.7 %all_to_all.15 = f32[1152,1,128]{2,1,0:T(1,128)S(1)} all-to-all(f32[1152,1,128]{2,1,0:T(1,128)S(1)} %bitcast.19), channel_id=1, replica_groups=mesh['z'=16,'x'=4,'core'=2,'y'=4] {'x','core'}, dimensions={0} | all-to-all | bytes 1179648 | tf_op jit(solution)/shard_map/all_to_all | solution.py:465
  51.9 0.0 copy-done
  51.9 0.0 copy-done.1
  51.9 0.0 copy-done.4
  51.9 0.0 copy-start.2
  51.9 0.0 copy-start.3
  51.9 1.0 shard_map.143
  52.9 55.9 %all_to_all.16 = f32[1536,1,128]{2,1,0:T(1,128)S(1)} all-to-all(f32[1536,1,128]{2,1,0:T(1,128)S(1)} %bitcast.16), channel_id=1, replica_groups={{0,1,2,3,8,9,10,11,16,17,18,19,24,25,26,27,64,65,66,67,72,73,74,75,80,8..., dimensions={0} | all-to-all | bytes 1572864 | tf_op jit(solution)/shard_map/all_to_all | solution.py:544
  108.9 0.0 copy-done.2
  108.9 0.0 copy-done.3
  108.9 1.8 %shard_map.144 = (f32[4,8,4096]{2,1,0:T(8,128)}, f32[4,8,4096]{2,1,0:T(8,128)}) custom-call(f32[1536,128]{1,0:T(8,128)S(1)} %bitcast.17, bf16[256,256]{1,0:T(8,128)(2,1)S(1)} %copy-done.3, bf16[256,256]{1,0:T(8,128)(2,1)S(1)} %copy-done.2, f32[64,128]{1,0:T(8,128)S(1)} %copy-done.1), custom_call_target="tpu_custom_call" | custom-call | tf_op jit(solution)/shard_map/pallas_call | solution.py:553
Async XLA Ops:
  4.4 29.4 %all-to-all-start = ((f32[400,1,128]{2,1,0:T(1,128)}), f32[400,1,128]{2,1,0:T(1,128)S(1)}, u32[]{:S(2)}, u32[]{:S(2)}) async-start(f32[400,1,128]{2,1,0:T(1,128)} %bitcast.22), calls=%async_computation | async-start | bytes 409600 | tf_op jit(solution)/shard_map/all_to_all | solution.py:500
  33.8 18.1 %copy-start = (bf16[512,256]{1,0:T(8,128)(2,1)S(1)}, bf16[512,256]{1,0:T(8,128)(2,1)}, u32[]{:S(2)}) copy-start(bf16[512,256]{1,0:T(8,128)(2,1)} %constant.12.clone.second_ref) | copy-start | bytes 786436
  33.8 18.1 %copy-start.1 = (f32[64,128]{1,0:T(8,128)S(1)}, f32[64,128]{1,0:T(8,128)}, u32[]{:S(2)}) copy-start(f32[64,128]{1,0:T(8,128)} %constant.11.clone.turn_ref) | copy-start | bytes 98308
  33.8 18.1 %copy-start.4 = (bf16[64,144]{1,0:T(8,128)(2,1)S(1)}, bf16[64,144]{1,0:T(8,128)(2,1)}, u32[]{:S(2)}) copy-start(bf16[64,144]{1,0:T(8,128)(2,1)} %constant.10.clone.first_ref) | copy-start | bytes 55300
  51.9 57.0 %copy-start.2 = (bf16[256,256]{1,0:T(8,128)(2,1)S(1)}, bf16[256,256]{1,0:T(8,128)(2,1)}, u32[]{:S(2)}) copy-start(bf16[256,256]{1,0:T(8,128)(2,1)} %constant.14.clone.low_ref) | copy-start | bytes 393220
  51.9 57.0 %copy-start.3 = (bf16[256,256]{1,0:T(8,128)(2,1)S(1)}, bf16[256,256]{1,0:T(8,128)(2,1)}, u32[]{:S(2)}) copy-start(bf16[256,256]{1,0:T(8,128)(2,1)} %constant.13.clone.high_ref) | copy-start | bytes 393220
